TPU v7x, 32 devices: a whole 2x2x4 slice. The times are simulated.
32 devices in a mesh: dp: 2 (over y), mp: 16 (over z, x, core).
Axes of the slice: x: 2, y: 2, z: 4, core: 2. Of those that a mesh axis runs over, the one named last changes fastest.
Arguments:
- inputs: bfloat16 [16384, 2048], P(('dp', 'mp')), may hold values from -6 to 6
- item_counts: int32 [2, 4], P('dp'), may hold values from 1 to 8, 16 in all within a row
- first_gain: bfloat16 [2048], replicated, may hold values from 0.5 to 1.5
- first_shift: bfloat16 [2048], replicated, may hold values from -0.59765625 to 0.59765625
- query_weight: bfloat16 [2048, 2048], P(None, 'mp'), may hold values from -0.125 to 0.125
- query_bias: bfloat16 [2048], P('mp'), may hold values from -3 to 3
- key_weight: bfloat16 [2048, 2048], P(None, 'mp'), may hold values from -0.125 to 0.125
- value_weight: bfloat16 [2048, 2048], P(None, 'mp'), may hold values from -0.125 to 0.125
- value_bias: bfloat16 [2048], P('mp'), may hold values from -0.59765625 to 0.59765625
- output_weight: bfloat16 [2048, 2048], P('mp'), may hold values from -0.5 to 0.5
- output_bias: bfloat16 [2048], replicated, may hold values from -3 to 3
- second_gain: bfloat16 [2048], replicated, may hold values from 0.5 to 1.5
- second_shift: bfloat16 [2048], replicated, may hold values from -3 to 3
- expand_weight: bfloat16 [2048, 8192], P(None, 'mp'), may hold values from -0.125 to 0.125
- expand_bias: bfloat16 [8192], P('mp'), may hold values from -3 to 3
- contract_weight: bfloat16 [8192, 2048], P('mp'), may hold values from -0.0625 to 0.0625
- contract_bias: bfloat16 [2048], replicated, may hold values from -3 to 3
- cotangent: bfloat16 [16384, 2048], P(('dp', 'mp')), may hold values from -6 to 6
Outputs:
- layer_out: bfloat16 [16384, 2048], P(('dp', 'mp'))
- input_grad: bfloat16 [16384, 2048], P(('dp', 'mp'))
- first_gain_grad: float32 [2048], replicated
- first_shift_grad: float32 [2048], replicated
- query_weight_grad: float32 [2048, 2048], P(None, 'mp')
- query_bias_grad: float32 [2048], P('mp')
- key_weight_grad: float32 [2048, 2048], P(None, 'mp')
- value_weight_grad: float32 [2048, 2048], P(None, 'mp')
- value_bias_grad: float32 [2048], P('mp')
- output_weight_grad: float32 [2048, 2048], P('mp')
- output_bias_grad: float32 [2048], replicated
- second_gain_grad: float32 [2048], replicated
- second_shift_grad: float32 [2048], replicated
- expand_weight_grad: float32 [2048, 8192], P(None, 'mp')
- expand_bias_grad: float32 [8192], P('mp')
- contract_weight_grad: float32 [8192, 2048], P('mp')
- contract_bias_grad: float32 [2048], replicated
Inputs may be any that keep to these rules, and one draw needn't show every extreme that they name: Each row of item_counts sums to 16, and some item of each row has exactly 8 segments.
All inputs are finite; a program needn't handle non-finite values.
Results may differ from a plain program's by a relative error of at most 0.02.
Values may be sent and summed in bfloat16 or wider, within the bound.
No kernel may reach another device: no remote copies, remote signals or barrier semaphores. Data moves between devices by JAX's collectives and lax.ppermute only.
A program may use at most 576 MiB of HBM per device.

v0:
```python
import jax
import jax.numpy as jnp
from jax import lax
from jax.sharding import PartitionSpec as P

HD = 64
SEG = 512
NSUM = 50


EPSILON = 1e-05
MASKED = -1e30


def smooth_gate(values):
    return (
        0.5
        * values
        * (1.0 + jnp.tanh(0.7978845608 * (values + 0.044715 * values * values * values)))
    )


def normalize(values, scaling, offset):
    centre = jnp.mean(values, axis=-1, keepdims=True)
    centred = values - centre
    spread = jnp.mean(centred * centred, axis=-1, keepdims=True)
    return centred * lax.rsqrt(spread + EPSILON) * scaling + offset


def slot_items(counts, slot_count):
    item_ends = jnp.cumsum(counts)
    places = jnp.arange(slot_count, dtype=jnp.int32)
    return jnp.sum((places[:, None] >= item_ends[None, :]).astype(jnp.int32), axis=1)


def summary_allowed(slot_item):
    slot_count = slot_item.shape[0]
    key_items = jnp.repeat(slot_item, NSUM)
    key_slots = jnp.repeat(jnp.arange(slot_count, dtype=jnp.int32), NSUM)
    own_slots = jnp.arange(slot_count, dtype=jnp.int32)
    return (key_items[None, :] == slot_item[:, None]) & (key_slots[None, :] < own_slots[:, None])


def product(former, latter):
    return jnp.dot(former, latter, preferred_element_type=jnp.float32)


def to_blocks(rows_in, slot_count):
    return rows_in.reshape(slot_count, SEG, rows_in.shape[1] // HD, HD)


def summary_rows(blocks):
    return blocks[:, SEG - NSUM :].reshape(-1, blocks.shape[2], HD)


def block_scores(query_block, key_block, summary_keys, allow_row):
    row_pos = lax.broadcasted_iota(jnp.int32, (SEG, SEG), 0)
    col_pos = lax.broadcasted_iota(jnp.int32, (SEG, SEG), 1)
    visible = jnp.concatenate(
        [row_pos >= col_pos, jnp.broadcast_to(allow_row[None, :], (SEG, allow_row.shape[0]))],
        axis=1,
    )
    key_rows = jnp.concatenate([key_block, summary_keys], axis=0)
    scores = jnp.einsum("qhd,khd->hqk", query_block, key_rows, preferred_element_type=jnp.float32)
    return (jnp.where(visible[None], scores, MASKED), key_rows)


def attend_forward(queries, key_all, value_all, allowed):
    slot_count = allowed.shape[0]
    query_blocks = to_blocks(queries, slot_count)
    key_blocks = to_blocks(key_all, slot_count)
    value_blocks = to_blocks(value_all, slot_count)
    summary_keys = summary_rows(key_blocks)
    summary_values = summary_rows(value_blocks)

    def one_block(pieces):
        query_block, key_block, value_block, allow_row = pieces
        scores, key_rows = block_scores(query_block, key_block, summary_keys, allow_row)
        highest = jnp.max(scores, axis=-1, keepdims=True)
        weights = jnp.exp(scores - highest)
        totals = jnp.sum(weights, axis=-1, keepdims=True)
        shares = (weights / totals).astype(jnp.bfloat16)
        value_rows = jnp.concatenate([value_block, summary_values], axis=0)
        mixture = jnp.einsum("hqk,khd->qhd", shares, value_rows, preferred_element_type=jnp.float32)
        return (mixture.astype(jnp.bfloat16).reshape(SEG, -1), (highest + jnp.log(totals))[:, :, 0])

    mixture, log_totals = lax.map(one_block, (query_blocks, key_blocks, value_blocks, allowed))
    return (mixture.reshape(-1, mixture.shape[-1]), log_totals)


def attend_backward(queries, key_all, value_all, allowed, log_totals, mixture_grad):
    slot_count = allowed.shape[0]
    query_blocks = to_blocks(queries, slot_count)
    key_blocks = to_blocks(key_all, slot_count)
    value_blocks = to_blocks(value_all, slot_count)
    grad_blocks = to_blocks(mixture_grad, slot_count)
    summary_keys = summary_rows(key_blocks)
    summary_values = summary_rows(value_blocks)
    head_count = query_blocks.shape[2]

    def one_step(running, pieces):
        key_extra, value_extra = running
        query_block, key_block, value_block, grad_block, allow_row, log_block = pieces
        scores, key_rows = block_scores(query_block, key_block, summary_keys, allow_row)
        shares = jnp.exp(scores - log_block[:, :, None])
        value_rows = jnp.concatenate([value_block, summary_values], axis=0)
        share_grad = jnp.einsum(
            "qhd,khd->hqk", grad_block, value_rows, preferred_element_type=jnp.float32
        )
        centre = jnp.sum(shares * share_grad, axis=-1, keepdims=True)
        score_grad = (shares * (share_grad - centre)).astype(jnp.bfloat16)
        query_part = jnp.einsum(
            "hqk,khd->qhd", score_grad, key_rows, preferred_element_type=jnp.float32
        )
        key_part = jnp.einsum(
            "hqk,qhd->khd", score_grad, query_block, preferred_element_type=jnp.float32
        )
        value_part = jnp.einsum(
            "hqk,qhd->khd",
            shares.astype(jnp.bfloat16),
            grad_block,
            preferred_element_type=jnp.float32,
        )
        running = (key_extra + key_part[SEG:], value_extra + value_part[SEG:])
        return (running, (query_part, key_part[:SEG], value_part[:SEG]))

    zero_block = jnp.zeros((slot_count * NSUM, head_count, HD), jnp.float32)
    (key_extra, value_extra), (query_grad, key_grad, value_grad) = lax.scan(
        one_step,
        (zero_block, zero_block),
        (query_blocks, key_blocks, value_blocks, grad_blocks, allowed, log_totals),
    )
    key_grad = key_grad.at[:, SEG - NSUM :].add(key_extra.reshape(slot_count, NSUM, head_count, HD))
    value_grad = value_grad.at[:, SEG - NSUM :].add(
        value_extra.reshape(slot_count, NSUM, head_count, HD)
    )
    col_width = head_count * HD
    return (
        query_grad.reshape(-1, col_width).astype(jnp.bfloat16),
        key_grad.reshape(-1, col_width).astype(jnp.bfloat16),
        value_grad.reshape(-1, col_width).astype(jnp.bfloat16),
    )


def body(
    inputs,
    item_counts,
    first_gain,
    first_shift,
    query_weight,
    query_bias,
    key_weight,
    value_weight,
    value_bias,
    output_weight,
    output_bias,
    second_gain,
    second_shift,
    expand_weight,
    expand_bias,
    contract_weight,
    contract_bias,
    cotangent,
):
    local_rows = inputs.shape[0]
    slot_count = local_rows * lax.axis_size("mp") // SEG
    allowed = summary_allowed(slot_items(item_counts[0], slot_count))
    query_scale = HD ** (-0.5)
    hidden_in = inputs.astype(jnp.float32)
    gain_first = first_gain.astype(jnp.float32)
    shift_first = first_shift.astype(jnp.float32)
    gain_second = second_gain.astype(jnp.float32)
    shift_second = second_shift.astype(jnp.float32)

    def attention_part():
        normed = normalize(hidden_in, gain_first, shift_first).astype(jnp.bfloat16)
        gathered = lax.all_gather(normed, "mp", axis=0, tiled=True)
        queries = (
            (product(gathered, query_weight) + query_bias.astype(jnp.float32)) * query_scale
        ).astype(jnp.bfloat16)
        key_all = product(gathered, key_weight).astype(jnp.bfloat16)
        value_all = (product(gathered, value_weight) + value_bias.astype(jnp.float32)).astype(
            jnp.bfloat16
        )
        mixture, log_totals = attend_forward(queries, key_all, value_all, allowed)
        branch = lax.psum_scatter(
            product(mixture, output_weight).astype(jnp.bfloat16),
            "mp",
            scatter_dimension=0,
            tiled=True,
        ).astype(jnp.float32)
        middle = hidden_in + branch + output_bias.astype(jnp.float32)
        return (gathered, queries, key_all, value_all, mixture, log_totals, middle)

    def feed_front(middle):
        normed_two = normalize(middle, gain_second, shift_second).astype(jnp.bfloat16)
        gathered_two = lax.all_gather(normed_two, "mp", axis=0, tiled=True)
        before = product(gathered_two, expand_weight) + expand_bias.astype(jnp.float32)
        active = smooth_gate(before).astype(jnp.bfloat16)
        return (gathered_two, before, active)

    attention_state = attention_part()
    feed_state = feed_front(attention_state[6])
    forward_active = feed_state[2]
    branch_two = lax.psum_scatter(
        product(forward_active, contract_weight).astype(jnp.bfloat16),
        "mp",
        scatter_dimension=0,
        tiled=True,
    ).astype(jnp.float32)
    layer_out = (attention_state[6] + branch_two + contract_bias.astype(jnp.float32)).astype(
        jnp.bfloat16
    )
    (
        hidden_in,
        query_weight,
        key_weight,
        value_weight,
        output_weight,
        expand_weight,
        expand_bias,
        layer_out,
    ) = lax.optimization_barrier(
        (
            hidden_in,
            query_weight,
            key_weight,
            value_weight,
            output_weight,
            expand_weight,
            expand_bias,
            layer_out,
        )
    )
    attention_state = attention_part()
    feed_state = feed_front(attention_state[6])
    gathered, queries, key_all, value_all, mixture, log_totals, middle = attention_state
    gathered_two, before, active = feed_state
    cot_local = cotangent.astype(jnp.float32)
    full_cotangent = lax.all_gather(cotangent, "mp", axis=0, tiled=True)
    contract_weight_grad = jnp.einsum(
        "rf,rd->fd", active, full_cotangent, preferred_element_type=jnp.float32
    )
    active_grad = jnp.einsum(
        "rd,fd->rf", full_cotangent, contract_weight, preferred_element_type=jnp.float32
    )
    ignored, pull_gate = jax.vjp(smooth_gate, before)
    before_grad = pull_gate(active_grad)[0].astype(jnp.bfloat16)
    expand_bias_grad = jnp.sum(before_grad.astype(jnp.float32), axis=0)
    expand_weight_grad = jnp.einsum(
        "rd,rf->df", gathered_two, before_grad, preferred_element_type=jnp.float32
    )
    normed_two_grad = lax.psum_scatter(
        jnp.einsum(
            "rf,df->rd", before_grad, expand_weight, preferred_element_type=jnp.float32
        ).astype(jnp.bfloat16),
        "mp",
        scatter_dimension=0,
        tiled=True,
    ).astype(jnp.float32)
    ignored, pull_second = jax.vjp(normalize, middle, gain_second, shift_second)
    middle_part, second_gain_grad, second_shift_grad = pull_second(normed_two_grad)
    middle_grad = cot_local + middle_part
    full_middle = lax.all_gather(middle_grad.astype(jnp.bfloat16), "mp", axis=0, tiled=True)
    output_weight_grad = jnp.einsum(
        "rc,rd->cd", mixture, full_middle, preferred_element_type=jnp.float32
    )
    mixture_grad = jnp.einsum(
        "rd,cd->rc", full_middle, output_weight, preferred_element_type=jnp.float32
    ).astype(jnp.bfloat16)
    query_grad, key_grad, value_grad = attend_backward(
        queries, key_all, value_all, allowed, log_totals, mixture_grad
    )
    query_step = query_grad * query_scale
    query_weight_grad = jnp.einsum(
        "rd,rc->dc", gathered, query_step, preferred_element_type=jnp.float32
    )
    query_bias_grad = jnp.sum(query_step.astype(jnp.float32), axis=0)
    key_weight_grad = jnp.einsum(
        "rd,rc->dc", gathered, key_grad, preferred_element_type=jnp.float32
    )
    value_weight_grad = jnp.einsum(
        "rd,rc->dc", gathered, value_grad, preferred_element_type=jnp.float32
    )
    value_bias_grad = jnp.sum(value_grad.astype(jnp.float32), axis=0)
    total = jnp.einsum("rc,dc->rd", query_step, query_weight, preferred_element_type=jnp.float32)
    total = total + jnp.einsum(
        "rc,dc->rd", key_grad, key_weight, preferred_element_type=jnp.float32
    )
    normed_grad = lax.psum_scatter(
        (
            total
            + jnp.einsum("rc,dc->rd", value_grad, value_weight, preferred_element_type=jnp.float32)
        ).astype(jnp.bfloat16),
        "mp",
        scatter_dimension=0,
        tiled=True,
    ).astype(jnp.float32)
    ignored, pull_first = jax.vjp(normalize, hidden_in, gain_first, shift_first)
    input_part, first_gain_grad, first_shift_grad = pull_first(normed_grad)
    input_grad = (middle_grad + input_part).astype(jnp.bfloat16)
    output_bias_grad = jnp.sum(middle_grad, axis=0)
    contract_bias_grad = jnp.sum(cot_local, axis=0)
    small_totals = lax.psum(
        (
            first_gain_grad,
            first_shift_grad,
            output_bias_grad,
            second_gain_grad,
            second_shift_grad,
            contract_bias_grad,
        ),
        ("dp", "mp"),
    )
    weight_totals = (
        lax.psum(query_weight_grad.astype(jnp.bfloat16), "dp").astype(jnp.float32),
        lax.psum(query_bias_grad.astype(jnp.bfloat16), "dp").astype(jnp.float32),
        lax.psum(key_weight_grad.astype(jnp.bfloat16), "dp").astype(jnp.float32),
        lax.psum(value_weight_grad.astype(jnp.bfloat16), "dp").astype(jnp.float32),
        lax.psum(value_bias_grad.astype(jnp.bfloat16), "dp").astype(jnp.float32),
        lax.psum(output_weight_grad.astype(jnp.bfloat16), "dp").astype(jnp.float32),
        lax.psum(expand_weight_grad.astype(jnp.bfloat16), "dp").astype(jnp.float32),
        lax.psum(expand_bias_grad.astype(jnp.bfloat16), "dp").astype(jnp.float32),
        lax.psum(contract_weight_grad.astype(jnp.bfloat16), "dp").astype(jnp.float32),
    )
    return (
        layer_out,
        input_grad,
        small_totals[0],
        small_totals[1],
        weight_totals[0],
        weight_totals[1],
        weight_totals[2],
        weight_totals[3],
        weight_totals[4],
        weight_totals[5],
        small_totals[2],
        small_totals[3],
        small_totals[4],
        weight_totals[6],
        weight_totals[7],
        weight_totals[8],
        small_totals[5],
    )


def solution(mesh):
    placed = (
        P(("dp", "mp"), None),
        P("dp", None),
        P(),
        P(),
        P(None, "mp"),
        P("mp"),
        P(None, "mp"),
        P(None, "mp"),
        P("mp"),
        P("mp", None),
        P(),
        P(),
        P(),
        P(None, "mp"),
        P("mp"),
        P("mp", None),
        P(),
        P(("dp", "mp"), None),
    )
    return jax.shard_map(
        body,
        mesh=mesh,
        in_specs=placed,
        out_specs=(
            P(("dp", "mp"), None),
            P(("dp", "mp"), None),
            P(),
            P(),
            P(None, "mp"),
            P("mp"),
            P(None, "mp"),
            P(None, "mp"),
            P("mp"),
            P("mp", None),
            P(),
            P(),
            P(),
            P(None, "mp"),
            P("mp"),
            P("mp", None),
            P(),
        ),
        check_vma=False,
    )
```

profile of v0, /device:TPU:0, one launch (start us, length us, event | category | flops | bytes accessed | tf_op | source)
XLA Modules:
  0.0 3981.3 jit_solution(9307161281005600023)
XLA Ops:
  15.9 170.2 %all-gather.7.cloned.1.call-done = bf16[8192,2048]{1,0:T(8,128)(2,1)} async-done(((bf16[512,2048]{1,0:T(8,128)(2,1)}), bf16[8192,2048]{1,0:T(8,128)(2,1)}) %all-gather.7.cloned.1.call-update) | async-done | bytes 33554448 | tf_op jit(solution)/shard_map/all_gather | solution.py:177
  276.8 140.5 %while.43 = (s32[]{:T(128)}, bf16[16,512,128]{2,1,0:T(8,128)(2,1)}, bf16[16,512,2,64]{1,3,2,0:T(8,128)(2,1)}, bf16[800,2,64]{0,2,1:T(8,128)(2,1)}, pred[16,800]{...) while((s32[]{:T(128)}, bf16[16,512,128]{2,1,0:T(8,128)(2,1)}, ...), condition=%wide.region_7.8_spmd, body=%wide.region_4.7_spmd.sunk | while | flops 528322112 | bytes 5026850 | solution.py:87
  433.9 332.1 %reduce-scatter.6.cloned.1.call-done = bf16[512,2048]{1,0:T(8,128)(2,1)} async-done(((bf16[8192,2048]{1,0:T(8,128)(2,1)}), bf16[512,2048]{1,0:T(8,128)(2,1)}) %reduce-scatter.6.cloned.1.call-update) | async-done | bytes 2097168 | tf_op jit(solution)/shard_map/reduce_scatter | solution.py:186
  773.3 167.2 %all-gather.9.cloned.1.call-done = bf16[8192,2048]{1,0:T(8,128)(2,1)} async-done(((bf16[512,2048]{1,0:T(8,128)(2,1)}), bf16[8192,2048]{1,0:T(8,128)(2,1)}) %all-gather.9.cloned.1.call-update) | async-done | bytes 33554448 | tf_op jit(solution)/shard_map/all_gather | solution.py:197
  940.5 46.4 %convolution_convert_fusion.1 = bf16[8192,2048]{1,0:T(8,128)(2,1)} fusion(bf16[512,2048]{1,0:T(8,128)(2,1)} %param.43, bf16[8192,2048]{1,0:T(8,128)(2,1)} %all-gather.9.cloned.1.call-done, bf16[2048,512]{1,0:T(8,128)(2,1)S(1)} %copy-done, f32[512]{0:T(512)S(1)} %convert_element_type.232), kind=kOutput, calls=%fused_computation.105 | convolution fusion | flops 34418458624 | bytes 71305216 | tf_op jit(solution)/shard_map/dot_general | solution.py:45
  991.4 328.3 %reduce-scatter.8.cloned.1.call-done = bf16[512,2048]{1,0:T(8,128)(2,1)} async-done(((bf16[8192,2048]{1,0:T(8,128)(2,1)}), bf16[512,2048]{1,0:T(8,128)(2,1)}) %reduce-scatter.8.cloned.1.call-update) | async-done | bytes 2097168 | tf_op jit(solution)/shard_map/reduce_scatter | solution.py:205
  1333.5 167.2 %all-gather.11.cloned.1.call-done = bf16[8192,2048]{1,0:T(8,128)(2,1)} async-done(((bf16[512,2048]{1,0:T(8,128)(2,1)}), bf16[8192,2048]{1,0:T(8,128)(2,1)}) %all-gather.11.cloned.1.call-update) | async-done | bytes 33554448 | tf_op jit(solution)/shard_map/all_gather | solution.py:177
  1591.7 133.7 %while.44 = (s32[]{:T(128)}, bf16[16,512,128]{2,1,0:T(8,128)(2,1)}, f32[16,2,512]{2,1,0:T(2,128)}, bf16[16,512,2,64]{1,3,2,0:T(8,128)(2,1)}, bf16[800,2,64]{0,2,...) while((s32[]{:T(128)}, bf16[16,512,128]{2,1,0:T(8,128)(2,1)}, ...), condition=%wide.region_17.18_spmd, body=%wide.region_14.17_spmd.sunk | while | flops 358366208 | bytes 21353512 | solution.py:87
  1741.2 332.7 %reduce-scatter.10.cloned.1.call-done = bf16[512,2048]{1,0:T(8,128)(2,1)} async-done(((bf16[8192,2048]{1,0:T(8,128)(2,1)}), bf16[512,2048]{1,0:T(8,128)(2,1)}) %reduce-scatter.10.cloned.1.call-update) | async-done | bytes 2097168 | tf_op jit(solution)/shard_map/reduce_scatter | solution.py:186
  2082.4 166.4 %all-gather.13.cloned.1.call-done = bf16[8192,2048]{1,0:T(8,128)(2,1)} async-done(((bf16[512,2048]{1,0:T(8,128)(2,1)}), bf16[8192,2048]{1,0:T(8,128)(2,1)}) %all-gather.13.cloned.1.call-update) | async-done | bytes 33554448 | tf_op jit(solution)/shard_map/all_gather | solution.py:197
  2248.8 24.7 fusion.143
  2273.5 145.0 %all-gather.15.cloned.1.call-done = bf16[8192,2048]{1,0:T(8,128)(2,1)} async-done(((bf16[512,2048]{1,0:T(8,128)(2,1)}), bf16[8192,2048]{1,0:T(8,128)(2,1)}) %all-gather.15.cloned.1.call-update) | async-done | bytes 33554448 | tf_op jit(solution)/shard_map/all_gather | solution.py:240
  2418.5 40.5 %fusion.134 = (bf16[512]{0:T(512)(128)(2,1)}, bf16[8192,512]{1,0:T(8,128)(2,1)}) fusion(f32[8192,512]{1,0:T(8,128)} %fusion.143, f32[512]{0:T(512)S(1)} %convert_element_type.246, bf16[8192,2048]{1,0:T(8,128)(2,1)} %all-gather.15.cloned.1.call-done, bf16[512,2048]{1,0:T(8,128)(2,1)} %param.43), kind=kOutput, calls=%fused_computation.214 | convolution fusion | flops 17288921088 | bytes 60820480 | tf_op jit(solution)/shard_map/rd,fd->rf/dot_general | solution.py:244
  2459.0 25.1 convolution_convert_fusion
  2484.2 332.8 %reduce-scatter.12.cloned.1.call-done = bf16[512,2048]{1,0:T(8,128)(2,1)} async-done(((bf16[8192,2048]{1,0:T(8,128)(2,1)}), bf16[512,2048]{1,0:T(8,128)(2,1)}) %reduce-scatter.12.cloned.1.call-update) | async-done | bytes 2097168 | tf_op jit(solution)/shard_map/reduce_scatter | solution.py:253
  2827.3 25.2 convolution_convert_fusion.7
  2852.5 28.9 fusion.118
  2881.4 113.0 %all-gather.17.cloned.1.call-done = bf16[8192,2048]{1,0:T(8,128)(2,1)} async-done(((bf16[512,2048]{1,0:T(8,128)(2,1)}), bf16[8192,2048]{1,0:T(8,128)(2,1)}) %all-gather.17.cloned.1.call-update) | async-done | bytes 33554448 | tf_op jit(solution)/shard_map/all_gather | solution.py:264
  3024.1 252.2 %while.45 = (s32[]{:T(128)}, f32[800,2,64]{0,2,1:T(8,128)S(1)}, f32[800,2,64]{0,2,1:T(8,128)S(1)}, bf16[16,512,2,64]{1,3,2,0:T(8,128)(2,1)}, f32[16,512,2,64]{1,...) while((s32[]{:T(128)}, f32[800,2,64]{0,2,1:T(8,128)S(1)}, ...), condition=%wide.region_26.27_spmd.clone, body=%wide.region_24.26_spmd.clone.sunk | while | flops 873937920 | bytes 49366132 | solution.py:128
  3344.2 24.3 fusion.144
  3432.0 55.9 %add_convert_fusion = bf16[8192,2048]{1,0:T(8,128)(2,1)} fusion(f32[8192,2048]{1,0:T(8,128)} %fusion.144, f32[8192,2048]{1,0:T(8,128)} %fusion.145, bf16[8192,128]{0,1:T(8,128)(2,1)S(1)} %bitcast.224, bf16[2048,128]{1,0:T(8,128)(2,1)S(1)} %copy-done.34), kind=kOutput, calls=%fused_computation.103 | convolution fusion | flops 4345298944 | bytes 170393600 | tf_op jit(solution)/shard_map/rc,dc->rd/dot_general | solution.py:293
  3495.4 90.9 %all-reduce.5.cloned.1.call-done = (bf16[2048,128]{1,0:T(8,128)(2,1)}, bf16[2048,128]{1,0:T(8,128)(2,1)}, bf16[2048,128]{1,0:T(8,128)(2,1)}, bf16[128,2048]{1,0:...) async-done(((bf16[2048,128]{1,0:T(8,128)(2,1)}, bf16[2048,128]{1,0:T(8,128)(2,1)}, bf16[2048,128]{1,0:T(8,128)(2,1)}, bf16[128,2048]{1,0:T(8,128)(2,1)}, ...) | async-done | bytes 6291472 | tf_op jit(solution)/shard_map/psum | solution.py:316
  3598.9 324.8 %reduce-scatter.14.cloned.1.call-done = bf16[512,2048]{1,0:T(8,128)(2,1)} async-done(((bf16[8192,2048]{1,0:T(8,128)(2,1)}), bf16[512,2048]{1,0:T(8,128)(2,1)}) %reduce-scatter.14.cloned.1.call-update) | async-done | bytes 2097168 | tf_op jit(solution)/shard_map/reduce_scatter | solution.py:290
  3934.1 40.1 %all-reduce = (f32[2048]{0:T(1024)}, f32[2048]{0:T(1024)}, f32[2048]{0:T(1024)}, f32[2048]{0:T(1024)}, f32[2048]{0:T(1024)}, /*index=5*/f32[2048]{0:T(1024)}) all-reduce(f32[2048]{0:T(1024)S(1)} %get-tuple-element.369, f32[2048]{0:T(1024)S(1)} %get-tuple-element.376, ...), channel_id=1, replica_groups=mesh['dp'=2,'mp'=16] {'dp','mp'}, use_global_device_ids=true, to_apply=%region_31.32 | all-reduce | flops 12288 | bytes 98304 | tf_op jit(solution)/shard_map/psum | solution.py:304
  (859 shorter events, 982.0 us)
Async XLA Ops:
  7.2 933.3 %copy-start = (bf16[2048,512]{1,0:T(8,128)(2,1)S(1)}, bf16[2048,512]{1,0:T(8,128)(2,1)}, u32[]{:S(2)}) copy-start(bf16[2048,512]{1,0:T(8,128)(2,1)} %param.41) | copy-start | bytes 6291460
  7.2 178.9 %all-gather.7.cloned.1.call-start = ((), (), s32[]{:S(2)}) async-start(), calls=%async_computation.5 | async-start | bytes 35651584 | tf_op jit(solution)/shard_map/all_gather | solution.py:177
  9.4 176.7 %copy-start.29 = (bf16[2048,128]{1,0:T(8,128)(2,1)S(1)}, bf16[2048,128]{1,0:T(8,128)(2,1)}, u32[]{:S(2)}) copy-start(bf16[2048,128]{1,0:T(8,128)(2,1)} %param.34) | copy-start | bytes 1572868
  15.2 750.9 %reduce-scatter.6.cloned.1.call-start = ((), (), s32[]{:S(2)}) async-start(), calls=%async_computation.6 | async-start | bytes 35651584 | tf_op jit(solution)/shard_map/reduce_scatter | solution.py:186
  15.3 224.4 %copy-start.70 = (f32[128]{0:T(128)}, f32[128]{0:T(128)S(1)}, u32[]{:S(2)}) copy-start(f32[128]{0:T(128)S(1)} %convert_element_type.223) | copy-start | bytes 1540
  15.3 196.7 %copy-start.72 = (f32[128]{0:T(128)}, f32[128]{0:T(128)S(1)}, u32[]{:S(2)}) copy-start(f32[128]{0:T(128)S(1)} %convert_element_type.220) | copy-start | bytes 1540
  433.2 507.3 %all-gather.9.cloned.1.call-start = ((), (), s32[]{:S(2)}) async-start(), calls=%async_computation.7 | async-start | bytes 35651584 | tf_op jit(solution)/shard_map/all_gather | solution.py:197
  433.9 336.7 %copy-start.40 = (f32[2048]{0:T(1024)}, f32[2048]{0:T(1024)S(1)}, u32[]{:S(2)}) copy-start(f32[2048]{0:T(1024)S(1)} %convert_element_type.229) | copy-start | bytes 24580
  433.9 336.7 %copy-start.42 = (f32[2048]{0:T(1024)}, f32[2048]{0:T(1024)S(1)}, u32[]{:S(2)}) copy-start(f32[2048]{0:T(1024)S(1)} %convert_element_type.230) | copy-start | bytes 24580
  773.2 546.4 %reduce-scatter.8.cloned.1.call-start = ((), (), s32[]{:S(2)}) async-start(), calls=%async_computation.8 | async-start | bytes 35651584 | tf_op jit(solution)/shard_map/reduce_scatter | solution.py:205
  987.0 513.8 %all-gather.11.cloned.1.call-start = ((), (), s32[]{:S(2)}) async-start(), calls=%async_computation.9 | async-start | bytes 35651584 | tf_op jit(solution)/shard_map/all_gather | solution.py:177
  1331.4 169.4 %copy-start.33 = (bf16[2048,128]{1,0:T(8,128)(2,1)S(1)}, bf16[2048,128]{1,0:T(8,128)(2,1)}, u32[]{:S(2)}) copy-start(bf16[2048,128]{1,0:T(8,128)(2,1)} %param.35) | copy-start | bytes 1572868
  1331.4 169.4 %copy-start.73 = (f32[128]{0:T(128)S(1)}, f32[128]{0:T(128)}, u32[]{:S(2)}) copy-start(f32[128]{0:T(128)} %copy-done.72) | copy-start | bytes 1540
  1333.5 740.4 %reduce-scatter.10.cloned.1.call-start = ((), (), s32[]{:S(2)}) async-start(), calls=%async_computation.10 | async-start | bytes 35651584 | tf_op jit(solution)/shard_map/reduce_scatter | solution.py:186
  1741.1 507.7 %all-gather.13.cloned.1.call-start = ((), (), s32[]{:S(2)}) async-start(), calls=%async_computation.11 | async-start | bytes 35651584 | tf_op jit(solution)/shard_map/all_gather | solution.py:197
  2081.6 337.0 %all-gather.15.cloned.1.call-start = ((), (), s32[]{:S(2)}) async-start(), calls=%async_computation.12 | async-start | bytes 35651584 | tf_op jit(solution)/shard_map/all_gather | solution.py:240
  2082.3 734.7 %reduce-scatter.12.cloned.1.call-start = ((), (), s32[]{:S(2)}) async-start(), calls=%async_computation.13 | async-start | bytes 35651584 | tf_op jit(solution)/shard_map/reduce_scatter | solution.py:253
  2484.2 510.3 %all-gather.17.cloned.1.call-start = ((), (), s32[]{:S(2)}) async-start(), calls=%async_computation.14 | async-start | bytes 35651584 | tf_op jit(solution)/shard_map/all_gather | solution.py:264
  2827.2 759.1 %all-reduce.5.cloned.1.call-start = ((), (), s32[]{:S(2)}) async-start(), calls=%async_computation.16 | async-start | bytes 12582912 | tf_op jit(solution)/shard_map/psum | solution.py:316
  3431.0 492.7 %reduce-scatter.14.cloned.1.call-start = ((), (), s32[]{:S(2)}) async-start(), calls=%async_computation.15 | async-start | bytes 35651584 | tf_op jit(solution)/shard_map/reduce_scatter | solution.py:290
  3596.4 327.3 %copy-start.39 = (f32[2048]{0:T(1024)S(1)}, f32[2048]{0:T(1024)}, u32[]{:S(2)}) copy-start(f32[2048]{0:T(1024)} %copy-done.37) | copy-start | bytes 24580
  3596.4 327.3 %copy-start.47 = (f32[512]{0:T(512)S(1)}, f32[512]{0:T(512)}, u32[]{:S(2)}) copy-start(f32[512]{0:T(512)} %copy-done.46) | copy-start | bytes 6148
  3598.9 328.8 %copy-start.53 = (f32[512]{0:T(512)S(1)}, f32[512]{0:T(512)}, u32[]{:S(2)}) copy-start(f32[512]{0:T(512)} %copy-done.52) | copy-start | bytes 6148
  3598.9 328.8 %copy-start.51 = (f32[512]{0:T(512)S(1)}, f32[512]{0:T(512)}, u32[]{:S(2)}) copy-start(f32[512]{0:T(512)} %copy-done.50) | copy-start | bytes 6148
  (62 other events, 632.4 us)
Sparse Core Ops, SparseCore 0:
  15.3 170.7 all-gather.6
  433.4 332.6 reduce-scatter.5
  773.4 167.1 all-gather.8
  987.1 332.5 reduce-scatter.7
  1333.6 167.1 all-gather.10
  1741.3 332.5 reduce-scatter.9
  2081.7 167.1 all-gather.12
  2250.4 168.0 all-gather.14
  2484.3 332.6 reduce-scatter.11
  2827.3 167.0 all-gather.16
  3431.2 155.1 all-reduce.4
  3591.0 332.6 reduce-scatter.13
where the time goes:
time: 4000 us; the launch traced here: 3980 us
  waiting for transfers between devices  2670 us (67%)
  matrix products  819 us (20%)
  local copies, waits for them, and re-layouts  277 us (7%)
  other arithmetic  150 us (4%)
  blocking collectives  45.1 us (1%)
    reduce_scatter x2, waiting for transfers between devices, attention_part(): lax.psum_scatter(product(mixture, output_weight).astype(jnp.bfloat16), 'm...  665 us
    all_gather x2, waiting for transfers between devices, attention_part(): gathered = lax.all_gather(normed, 'mp', axis=0, tiled=True)  337 us
    all_gather x2, waiting for transfers between devices, feed_front(): gathered_two = lax.all_gather(normed_two, 'mp', axis=0, tiled=True)  334 us
    reduce_scatter x1, waiting for transfers between devices, body(): lax.psum_scatter(jnp.einsum('rf,df->rd', before_grad, expand_weight, pref...  333 us
    reduce_scatter x1, waiting for transfers between devices, body(): lax.psum_scatter(product(forward_active, contract_weight).astype(jnp.bflo...  328 us
    reduce_scatter x1, waiting for transfers between devices, body(): lax.psum_scatter((total + jnp.einsum('rc,dc->rd', value_grad, value_weigh...  325 us
    dot_general x10, matrix products, product(): return jnp.dot(former, latter, preferred_element_type=jnp.float32)  203 us
    all_gather x1, waiting for transfers between devices, body(): full_cotangent = lax.all_gather(cotangent, 'mp', axis=0, tiled=True)  145 us
  transfers between devices with their start and end apart: 12, of which 12 were waited for; matrix products, arithmetic and copies ran while one was open for 4% of the time, Pallas kernels for 0%

commit v1 on v0

v1 whole, which is shorter than its diff:
```python
import functools

import jax
import jax.numpy as jnp
from jax import lax
from jax.experimental import pallas as pl
from jax.experimental.pallas import tpu as pltpu
from jax.sharding import PartitionSpec as P

HD = 64
SEG = 512
NSUM = 50
TAIL = 64
TEAM = 4
PAIR = 2 * HD
QB = 256
EPSILON = 1e-05
MASKED = -1e30
LIGHT = pl.CostEstimate(flops=1024, bytes_accessed=1024, transcendentals=0)
F32 = jnp.float32
BF16 = jnp.bfloat16


def gelu_and_slope(v):
    inner = 0.7978845608 * (v + 0.044715 * v * v * v)
    t = jnp.tanh(inner)
    value = 0.5 * v * (1.0 + t)
    slope = 0.5 * (1.0 + t) + 0.5 * v * (1.0 - t * t) * (
        0.7978845608 * (1.0 + 3.0 * 0.044715 * v * v)
    )
    return value, slope


def normalize(values, scaling, offset):
    centre = jnp.mean(values, axis=-1, keepdims=True)
    centred = values - centre
    spread = jnp.mean(centred * centred, axis=-1, keepdims=True)
    return centred * lax.rsqrt(spread + EPSILON) * scaling + offset


def slot_items(counts, slot_count):
    item_ends = jnp.cumsum(counts)
    places = jnp.arange(slot_count, dtype=jnp.int32)
    return jnp.sum((places[:, None] >= item_ends[None, :]).astype(jnp.int32), axis=1)


def dot(a, b):
    return jnp.dot(a, b, preferred_element_type=F32)


def dot_nt(a, b):
    return lax.dot_general(a, b, (((1,), (1,)), ((), ())), preferred_element_type=F32)


def dot_tn(a, b):
    return lax.dot_general(a, b, (((0,), (0,)), ((), ())), preferred_element_type=F32)


def head_only(block, h):
    lane = lax.broadcasted_iota(jnp.int32, block.shape, 1)
    return jnp.where((lane // HD) == h, block, jnp.zeros_like(block))


def causal(block):
    key = lax.broadcasted_iota(jnp.int32, block.shape, 0)
    query = lax.broadcasted_iota(jnp.int32, block.shape, 1)
    return jnp.where(query >= key, block, MASKED)


def hide_rows(block, count):
    key = lax.broadcasted_iota(jnp.int32, block.shape, 0)
    return jnp.where(key >= count, block, MASKED)


def key_blocks(info_ref, e):
    slots = info_ref.shape[0] - 2
    team, mine = info_ref[slots], info_ref[slots + 1]
    i = mine ^ e
    item = info_ref[team * TEAM + i]

    def hidden(other):
        same = info_ref[jnp.maximum(other, 0)] == item
        return jnp.where(jnp.logical_and(other >= 0, same), TAIL - NSUM, TAIL)

    rows = TEAM * SEG
    out = [(rows + 2 * f * TAIL, hidden((team - 1) * TEAM + (mine ^ f))) for f in range(TEAM)]
    for d in range(1, TEAM):
        j = i ^ d
        inside = j < i
        start = jnp.where(
            inside, (e ^ d) * SEG + SEG - TAIL, rows + (2 * (e ^ d) + 1) * TAIL
        )
        out.append((start, hidden(jnp.where(inside, team, team - 2) * TEAM + j)))
    return out


def attend_kernel(first, count, info_ref, qkv_ref, mix_ref, log_ref):
    def segment(e, carry):
        base = pl.multiple_of(e * SEG, SEG)
        place = pl.multiple_of((e - first) * SEG, SEG)
        extra = key_blocks(info_ref, e)
        keys = qkv_ref[pl.ds(base, SEG), PAIR : 2 * PAIR]
        value_t = qkv_ref[pl.ds(base, SEG), 2 * PAIR : 3 * PAIR].T
        extra_keys = [
            qkv_ref[pl.ds(pl.multiple_of(s, TAIL), TAIL), PAIR : 2 * PAIR] for s, _ in extra
        ]
        extra_values = [
            qkv_ref[pl.ds(pl.multiple_of(s, TAIL), TAIL), 2 * PAIR : 3 * PAIR] for s, _ in extra
        ]
        extra_keys = jnp.concatenate(extra_keys, axis=0)
        extra_value_t = jnp.concatenate(extra_values, axis=0).T
        for qb in range(SEG // QB):
            query = qkv_ref[pl.ds(base + qb * QB, QB), 0:PAIR]
            seen = (qb + 1) * QB
            outs = []
            for h in range(2):
                qh = head_only(query, h)
                own = dot_nt(keys[:seen], qh)
                parts = [own[: qb * QB]] if qb else []
                parts.append(causal(own[qb * QB :]))
                far = dot_nt(extra_keys, qh)
                for n, (_, hidden) in enumerate(extra):
                    parts.append(hide_rows(far[n * TAIL : (n + 1) * TAIL], hidden))
                high = functools.reduce(
                    jnp.maximum, [jnp.max(p, axis=0, keepdims=True) for p in parts]
                )
                parts = [jnp.exp(p - high) for p in parts]
                total = functools.reduce(
                    jnp.add, [jnp.sum(p, axis=0, keepdims=True) for p in parts]
                )
                cut = 2 if qb else 1
                p_own = jnp.concatenate([p.astype(BF16) for p in parts[:cut]], axis=0)
                p_far = jnp.concatenate([p.astype(BF16) for p in parts[cut:]], axis=0)
                rows = slice(h * HD, (h + 1) * HD)
                mixed = dot(value_t[rows, :seen], p_own) + dot(extra_value_t[rows], p_far)
                outs.append(mixed / total)
                log_ref[0, e - first, h : h + 1, qb * QB : (qb + 1) * QB] = high + jnp.log(total)
            mix_ref[pl.ds(place + qb * QB, QB), :] = jnp.concatenate(outs, axis=0).T.astype(BF16)
        return carry

    lax.fori_loop(first, first + count, segment, 0)


def attend(info, qkv, first, count):
    pieces = qkv.shape[1] // (3 * PAIR)
    rows = count * SEG
    return pl.pallas_call(
        functools.partial(attend_kernel, first, count),
        grid_spec=pltpu.PrefetchScalarGridSpec(
            num_scalar_prefetch=1,
            grid=(pieces,),
            in_specs=[pl.BlockSpec((qkv.shape[0], 3 * PAIR), lambda r, t: (0, r))],
            out_specs=[
                pl.BlockSpec((rows, PAIR), lambda r, t: (0, r)),
                pl.BlockSpec((1, count, 2, SEG), lambda r, t: (r, 0, 0, 0)),
            ],
        ),
        out_shape=[
            jax.ShapeDtypeStruct((rows, pieces * PAIR), BF16),
            jax.ShapeDtypeStruct((pieces, count, 2, SEG), F32),
        ],
        compiler_params=pltpu.CompilerParams(vmem_limit_bytes=56 * 1024 * 1024),
        cost_estimate=LIGHT,
        name="attend",
    )(info, qkv)


def attend_back_kernel(first, count, info_ref, qkv_ref, mix_ref, grad_ref, log_ref, *rest):
    out_ref, key_acc, value_acc = rest[-3:]
    if len(rest) == 4:
        before_ref = rest[0]
        key_acc[...] = before_ref[:, PAIR : 2 * PAIR].astype(F32)
        value_acc[...] = before_ref[:, 2 * PAIR : 3 * PAIR].astype(F32)
        out_ref[:, 0:PAIR] = before_ref[:, 0:PAIR]
    else:
        key_acc[...] = jnp.zeros_like(key_acc)
        value_acc[...] = jnp.zeros_like(value_acc)
        out_ref[:, 0:PAIR] = jnp.zeros((out_ref.shape[0], PAIR), BF16)

    def segment(e, carry):
        base = pl.multiple_of(e * SEG, SEG)
        place = pl.multiple_of((e - first) * SEG, SEG)
        extra = key_blocks(info_ref, e)
        keys = qkv_ref[pl.ds(base, SEG), PAIR : 2 * PAIR]
        values = qkv_ref[pl.ds(base, SEG), 2 * PAIR : 3 * PAIR]
        key_t = keys.T
        extra_keys = jnp.concatenate(
            [qkv_ref[pl.ds(pl.multiple_of(s, TAIL), TAIL), PAIR : 2 * PAIR] for s, _ in extra],
            axis=0,
        )
        extra_values = jnp.concatenate(
            [qkv_ref[pl.ds(pl.multiple_of(s, TAIL), TAIL), 2 * PAIR : 3 * PAIR] for s, _ in extra],
            axis=0,
        )
        extra_key_t = extra_keys.T
        for qb in range(SEG // QB):
            here = pl.ds(base + qb * QB, QB)
            query = qkv_ref[here, 0:PAIR]
            grad = grad_ref[pl.ds(place + qb * QB, QB), :]
            both = (grad.astype(F32) * mix_ref[pl.ds(place + qb * QB, QB), :].astype(F32)).T
            seen = (qb + 1) * QB
            key_own, value_own, key_far, value_far = 0.0, 0.0, 0.0, 0.0
            query_grads = []
            for h in range(2):
                rows = slice(h * HD, (h + 1) * HD)
                qh, gh = head_only(query, h), head_only(grad, h)
                centre = jnp.sum(both[rows], axis=0, keepdims=True)
                log = log_ref[0, e - first, h : h + 1, qb * QB : (qb + 1) * QB]
                own = dot_nt(keys[:seen], qh)
                parts = [own[: qb * QB]] if qb else []
                parts.append(causal(own[qb * QB :]))
                own = jnp.exp((jnp.concatenate(parts, axis=0) if qb else parts[0]) - log)
                far = dot_nt(extra_keys, qh)
                far = jnp.concatenate(
                    [
                        hide_rows(far[n * TAIL : (n + 1) * TAIL], hidden)
                        for n, (_, hidden) in enumerate(extra)
                    ],
                    axis=0,
                )
                far = jnp.exp(far - log)
                own_step = (own * (dot_nt(values[:seen], gh) - centre)).astype(BF16)
                far_step = (far * (dot_nt(extra_values, gh) - centre)).astype(BF16)
                value_own += dot(own.astype(BF16), gh)
                value_far += dot(far.astype(BF16), gh)
                key_own += dot(own_step, qh)
                key_far += dot(far_step, qh)
                query_grads.append(dot(key_t[rows, :seen], own_step) + dot(extra_key_t[rows], far_step))
            query_grad = jnp.concatenate(query_grads, axis=0).T * (HD**-0.5)
            out_ref[here, 0:PAIR] = query_grad.astype(BF16)
            key_acc[pl.ds(base, seen), :] += key_own
            value_acc[pl.ds(base, seen), :] += value_own
            for n, (s, _) in enumerate(extra):
                there = pl.ds(pl.multiple_of(s, TAIL), TAIL)
                key_acc[there, :] += key_far[n * TAIL : (n + 1) * TAIL]
                value_acc[there, :] += value_far[n * TAIL : (n + 1) * TAIL]
        return carry

    lax.fori_loop(first, first + count, segment, 0)
    out_ref[:, PAIR : 2 * PAIR] = key_acc[...].astype(BF16)
    out_ref[:, 2 * PAIR : 3 * PAIR] = value_acc[...].astype(BF16)


def attend_back(info, qkv, mixture, grad, logs, first, count, before=None):
    pieces = qkv.shape[1] // (3 * PAIR)
    rows = count * SEG
    wide = pl.BlockSpec((qkv.shape[0], 3 * PAIR), lambda r, t: (0, r))
    narrow = pl.BlockSpec((rows, PAIR), lambda r, t: (0, r))
    more = () if before is None else (before,)
    return pl.pallas_call(
        functools.partial(attend_back_kernel, first, count),
        grid_spec=pltpu.PrefetchScalarGridSpec(
            num_scalar_prefetch=1,
            grid=(pieces,),
            in_specs=[
                wide,
                narrow,
                narrow,
                pl.BlockSpec((1, count, 2, SEG), lambda r, t: (r, 0, 0, 0)),
            ]
            + [wide] * len(more),
            out_specs=wide,
            scratch_shapes=[
                pltpu.VMEM((qkv.shape[0], PAIR), F32),
                pltpu.VMEM((qkv.shape[0], PAIR), F32),
            ],
        ),
        out_shape=jax.ShapeDtypeStruct(qkv.shape, BF16),
        compiler_params=pltpu.CompilerParams(vmem_limit_bytes=56 * 1024 * 1024),
        cost_estimate=LIGHT,
        name="attend_back",
    )(info, qkv, mixture, grad, logs, *more)


def weight_grad_kernel(order_ref, *refs):
    out_ref = refs[-1]
    total = None
    for left, right in zip(refs[:-1:2], refs[1:-1:2]):
        term = dot_tn(left[...], right[...])
        total = term if total is None else total + term
    out_ref[...] = total.astype(out_ref.dtype)


def weight_grad(pairs, column=0, columns=None, step=256, order=None):
    height = pairs[0][0].shape[1]
    columns = columns or pairs[0][1].shape[1]
    if order is None:
        order = jnp.arange(height // step, dtype=jnp.int32)
    specs = []
    for left, right, n in pairs:
        specs.append(pl.BlockSpec((left.shape[0], step), lambda i, o: (0, i)))
        specs.append(pl.BlockSpec((left.shape[0], columns), lambda i, o, n=n: (n, column)))
    return pl.pallas_call(
        weight_grad_kernel,
        grid_spec=pltpu.PrefetchScalarGridSpec(
            num_scalar_prefetch=1,
            grid=(height // step,),
            in_specs=specs,
            out_specs=pl.BlockSpec((step, columns), lambda i, o: (o[i], 0)),
        ),
        out_shape=jax.ShapeDtypeStruct((height, columns), BF16),
        compiler_params=pltpu.CompilerParams(vmem_limit_bytes=56 * 1024 * 1024),
        cost_estimate=LIGHT,
        name="weight_grad",
    )(order, *[v for pair in pairs for v in pair[:2]])


def project_kernel(pieces, which_ref, *refs):
    weights, rows, out_ref, first, last = (
        refs[: 2 * pieces],
        refs[2 * pieces : -3],
        refs[-3],
        refs[-2],
        refs[-1],
    )
    depth, block = first.shape[0], first.shape[1] // pieces
    for n in range(pieces):
        first[:, n * block : (n + 1) * block] = weights[2 * n][:depth, :]
        last[:, n * block : (n + 1) * block] = weights[2 * n + 1][:depth, :]
    bias = jnp.concatenate(
        [weights[2 * n][depth : depth + 1, :].astype(F32) for n in range(pieces)], axis=1
    )
    lane = lax.broadcasted_iota(jnp.int32, bias.shape, 1)
    scale = jnp.where(lane % block < PAIR, HD**-0.5, 1.0)
    held = pl.ds(pl.multiple_of(which_ref[0] * depth, depth), depth)
    other = pl.ds(pl.multiple_of((1 - which_ref[0]) * depth, depth), depth)
    at = 0
    for ref in rows:
        chunk = min(256, ref.shape[0])
        for start in range(0, ref.shape[0], chunk):
            here = slice(start, start + chunk)
            value = dot(ref[here, held], first[...]) + dot(ref[here, other], last[...])
            out_ref[at + start : at + start + chunk, :] = ((value + bias) * scale).astype(BF16)
        at += ref.shape[0]


def project(which, weights, rows):
    pieces = len(weights)
    depth, block = rows[0].shape[1] // 2, weights[0][0].shape[1]
    height = sum(v.shape[0] for v in rows)
    return pl.pallas_call(
        functools.partial(project_kernel, pieces),
        grid_spec=pltpu.PrefetchScalarGridSpec(
            num_scalar_prefetch=1,
            grid=(),
            in_specs=[pl.BlockSpec(memory_space=pltpu.VMEM)] * (2 * pieces + len(rows)),
            out_specs=pl.BlockSpec(memory_space=pltpu.VMEM),
            scratch_shapes=[pltpu.VMEM((depth, pieces * block), BF16)] * 2,
        ),
        out_shape=jax.ShapeDtypeStruct((height, pieces * block), BF16),
        compiler_params=pltpu.CompilerParams(vmem_limit_bytes=56 * 1024 * 1024),
        cost_estimate=LIGHT,
        name="project",
    )(which, *[v for pair in weights for v in pair], *rows)


def matmul_kernel(transposed, left_ref, right_ref, *rest):
    out_ref = rest[-1]
    chunk = min(256, left_ref.shape[0])
    for start in range(0, left_ref.shape[0], chunk):
        rows = slice(start, start + chunk)
        value = (dot_nt if transposed else dot)(left_ref[rows, :], right_ref[...])
        if len(rest) == 2:
            value = value * rest[0][rows, :].astype(F32)
        out_ref[rows, :] = value.astype(BF16)


def matmul(left, right, transposed, scale=None, place=0, rows=None, step=512):
    rows = rows or left.shape[0]
    depth = left.shape[1]
    columns = right.shape[0] if transposed else right.shape[1]
    right_spec = (
        pl.BlockSpec((step, depth), lambda i: (i, 0))
        if transposed
        else pl.BlockSpec((depth, step), lambda i: (0, i))
    )
    out_spec = pl.BlockSpec((rows, step), lambda i: (0, i))
    more = () if scale is None else (scale,)
    return pl.pallas_call(
        functools.partial(matmul_kernel, transposed),
        grid=(columns // step,),
        in_specs=[pl.BlockSpec((rows, depth), lambda i: (place, 0)), right_spec]
        + [out_spec] * len(more),
        out_specs=out_spec,
        out_shape=jax.ShapeDtypeStruct((rows, columns), BF16),
        compiler_params=pltpu.CompilerParams(vmem_limit_bytes=56 * 1024 * 1024),
        cost_estimate=LIGHT,
        name="matmul",
    )(left, right, *more)


def body(
    inputs,
    item_counts,
    first_gain,
    first_shift,
    query_weight,
    query_bias,
    key_weight,
    value_weight,
    value_bias,
    output_weight,
    output_bias,
    second_gain,
    second_shift,
    expand_weight,
    expand_bias,
    contract_weight,
    contract_bias,
    cotangent,
):
    n_mp, n_dp = lax.axis_size("mp"), lax.axis_size("dp")
    teams = n_mp // TEAM
    me = lax.axis_index("mp")
    team, mine = me // TEAM, me % TEAM
    second = lax.axis_index("dp") % 2

    def core_swap(v):
        return lax.ppermute(v, "mp", [(i, i ^ 1) for i in range(n_mp)])

    def chip_swap(v):
        return lax.ppermute(v, "mp", [(i, i ^ 2) for i in range(n_mp)])

    def ring_up(v, by=1):
        return lax.ppermute(v, "mp", [(i, (i + by * TEAM) % n_mp) for i in range(n_mp)])

    def ring_down(v):
        return lax.ppermute(v, "mp", [(i, (i - TEAM) % n_mp) for i in range(n_mp)])

    def line_up(v, by=1):
        return lax.ppermute(v, "mp", [(i, i + by * TEAM) for i in range(n_mp - by * TEAM)])

    def line_down(v, by=1):
        return lax.ppermute(v, "mp", [(i + by * TEAM, i) for i in range(n_mp - by * TEAM)])

    def group_swap(v, bit=1):
        return lax.ppermute(v, "dp", [(i, i ^ bit) for i in range(n_dp)])

    def half(v, axis, which):
        size = v.shape[axis] // 2
        return lax.dynamic_slice_in_dim(v, which * size, size, axis)

    def ordered(held, other, axis):
        return jnp.where(
            second == 0,
            jnp.concatenate([held, other], axis=axis),
            jnp.concatenate([other, held], axis=axis),
        )

    def add(*terms):
        return functools.reduce(jnp.add, [t.astype(F32) for t in terms]).astype(BF16)

    def other_groups(v):
        bit = 2
        while bit < n_dp:
            v = add(v, group_swap(v, bit))
            bit *= 2
        return v

    def sync(*values):
        return lax.optimization_barrier(values)

    slot_count = teams * TEAM
    items = slot_items(item_counts[0], slot_count)
    info = jnp.pad(items, (0, 2))
    at = lax.iota(jnp.int32, slot_count + 2)
    info = jnp.where(at == slot_count, team, jnp.where(at == slot_count + 1, mine, info))

    gain_first, shift_first = first_gain.astype(F32), first_shift.astype(F32)
    gain_second, shift_second = second_gain.astype(F32), second_shift.astype(F32)
    width = inputs.shape[1]
    cols = query_bias.shape[0]
    hid = expand_bias.shape[0]
    wide = hid // 2
    team_rows, near_rows = TEAM * SEG, 2 * SEG
    span = TEAM * TAIL
    block = 3 * PAIR
    pad = 16

    def with_bias(weight, bias):
        return jnp.concatenate(
            [weight, jnp.broadcast_to(bias[None], (pad, bias.shape[0]))], axis=0
        )

    def send_in(terms):
        size = terms.shape[0] // 2
        return add(terms[:size], core_swap(terms[size:]))

    def shard_halves(v):
        return [
            [v[:, (2 * r + k) * wide : (2 * r + k + 1) * wide] for k in range(2)]
            for r in range(teams)
        ]

    part = SEG // 2
    pairs_along = [
        [(first + d) * n_mp + t * TEAM + i for t in range(teams) for d in range(2)]
        for first in range(0, n_dp, 2)
        for i in range(TEAM)
    ]

    def scatter_sum(v):
        return lax.psum_scatter(
            v, ("dp", "mp"), scatter_dimension=0, axis_index_groups=pairs_along, tiled=True
        )

    def cat(*parts, axis=0):
        return jnp.concatenate(parts, axis=axis)

    qkv_local = cat(query_weight, key_weight, value_weight, axis=1)
    qkv_bias_local = cat(query_bias, jnp.zeros_like(query_bias), value_bias)
    packed = with_bias(half(qkv_local, 0, second), qkv_bias_local)
    q0_o = half(qkv_local, 0, 1 - second)
    hidden_in = inputs.astype(F32)
    normed = normalize(hidden_in, gain_first, shift_first).astype(BF16)
    packed, normed = sync(packed, normed)
    q1 = ring_up(packed)
    normed_xa = chip_swap(normed[:part])
    normed_c = core_swap(normed)
    early = line_up(normed[SEG - TAIL :])
    earlier = line_up(normed[SEG - TAIL :], 2)
    q1, normed_xa, normed_c, early, earlier, normed = sync(
        q1, normed_xa, normed_c, early, earlier, normed
    )
    q2 = ring_up(q1)
    q1_o = group_swap(q1)
    normed_xb = chip_swap(normed[part:])
    rest = cat(early, earlier)
    rest_x = chip_swap(rest)
    rest_c = core_swap(rest)
    q2, q1_o, normed_xb, rest_x, rest_c, cot = sync(q2, q1_o, normed_xb, rest_x, rest_c, cotangent)
    q3 = ring_up(q2)
    q2_o = group_swap(q2)
    normed_x = cat(normed_xa, normed_xb)
    normed_xc = core_swap(normed_x)
    rest_xc = core_swap(rest_x)
    cot_xa = chip_swap(cot[:part])
    tops = width // 2
    out_half = half(output_weight, 0, second)
    q3, q2_o, normed_xc, rest_xc, cot_xa, cot_late, out_half, expand_weight, expand_bias = sync(
        q3, q2_o, normed_xc, rest_xc, cot_xa, cot, out_half, expand_weight, expand_bias
    )
    q3_o = group_swap(q3)
    out_h = [ring_up(out_half, r) for r in range(1, teams)]
    cot_xb = chip_swap(cot_late[part:])
    row_blocks = [normed, normed_c, normed_x, normed_xc, rest, rest_c, rest_x, rest_xc]
    which = jnp.reshape(second, (1,)).astype(jnp.int32)
    qkv_a = project(which, [(packed, q0_o), (q1, q1_o), (q2, q2_o)], row_blocks)
    expand_own, expand_rest = half(expand_weight, 1, second), half(expand_weight, 1, 1 - second)
    expand_bias_own = half(expand_bias, 0, second)
    expand_bias_rest = half(expand_bias, 0, 1 - second)
    q3_o, cot_xb, qkv_a, e0, cot_late, *out_h = sync(
        q3_o, cot_xb, qkv_a, with_bias(expand_own, expand_bias_own), cot_late, *out_h
    )
    e1 = ring_up(e0)
    out_o = group_swap(cat(*out_h))
    cot_c = core_swap(cot_late)
    mix_far_a, log_far_a = attend(info, qkv_a, 2, 2)
    e1, out_o, cot_c, mix_far_a, cot_x = sync(e1, out_o, cot_c, mix_far_a, cat(cot_xa, cot_xb))
    e2 = ring_up(e1)
    e1_o = group_swap(e1)
    cot_xc = core_swap(cot_x)
    qkv_b = project(which, [(q3, q3_o)], row_blocks)
    mix_far_b, log_far_b = attend(info, qkv_b, 2, 2)
    quarter = cols // 2
    out_all = cat(
        output_weight,
        *[ordered(v, out_o[r * quarter : (r + 1) * quarter], 0) for r, v in enumerate(out_h)],
    )
    mix_far = cat(mix_far_a, mix_far_b, axis=1)
    far = matmul(mix_far, out_all, False)
    e2, e1_o, cot_xc, qkv_b, far, out_all, contract_weight = sync(
        e2, e1_o, cot_xc, qkv_b, far, out_all, contract_weight
    )
    far_c = core_swap(far[SEG:])
    far, far_c, qkv_a = sync(far, far_c, qkv_a)
    branch_in = add(far[:SEG], far_c)
    branch_xa = chip_swap(branch_in[:part])
    e3 = ring_up(e2)
    e2_o = group_swap(e2)
    mix_near_a, log_near_a = attend(info, qkv_a, 0, 2)
    contract_own = half(contract_weight, 0, second)
    contract_rest = half(contract_weight, 0, 1 - second)
    branch_xa, e3, e2_o, mix_near_a, branch_in, contract_own, qkv_b = sync(
        branch_xa, e3, e2_o, mix_near_a, branch_in, contract_own, qkv_b
    )
    branch_xb = chip_swap(branch_in[part:])
    k1 = ring_up(contract_own)
    e3_o = group_swap(e3)
    mix_near_b, log_near_b = attend(info, qkv_b, 0, 2)
    mix_near = cat(mix_near_a, mix_near_b, axis=1)
    near = matmul(mix_near, out_all, False)
    branch_xb, k1, e3_o, near, mix_near = sync(branch_xb, k1, e3_o, near, mix_near)
    near_c = core_swap(near[SEG:])
    near, near_c, k1 = sync(near, near_c, k1)
    branch_x = cat(branch_xa, branch_xb)
    branch = near[:SEG].astype(F32) + near_c.astype(F32) + branch_x.astype(F32)
    middle = hidden_in + branch + output_bias.astype(F32)
    normed_two = normalize(middle, gain_second, shift_second).astype(BF16)
    normed_two, k1, e3_o = sync(normed_two, k1, e3_o)
    two_xa = chip_swap(normed_two[:part])
    two_c = core_swap(normed_two)
    k2 = ring_up(k1)
    k1_o = group_swap(k1)
    expand_pairs = (e1, e1_o, e2, e2_o, e3, e3_o)
    expand_all = cat(expand_own, expand_rest, *[v[:width] for v in expand_pairs], axis=1)
    expand_bias_all = cat(
        expand_bias_own, expand_bias_rest, *[v[width] for v in expand_pairs]
    ).astype(F32)
    two_xa, two_c, k2, k1_o, expand_all, expand_bias_all, normed_two = sync(
        two_xa, two_c, k2, k1_o, expand_all, expand_bias_all, normed_two
    )
    two_xb = chip_swap(normed_two[part:])
    k3 = ring_up(k2)
    k2_o = group_swap(k2)

    def front(rows):
        value, slope = gelu_and_slope(dot(rows, expand_all) + expand_bias_all)
        return value.astype(BF16), slope.astype(BF16)

    two_near = cat(normed_two, two_c)
    active_near, slope_near = front(two_near)
    two_xb, k3, k2_o, active_near, slope_near, two_near = sync(
        two_xb, k3, k2_o, active_near, slope_near, two_near
    )
    two_x = cat(two_xa, two_xb)
    two_xc = core_swap(two_x)
    two_xc, k3, qkv_a, qkv_b, cot_c = sync(two_xc, k3, qkv_a, qkv_b, cot_c)
    k3_o = group_swap(k3)
    two_far = cat(two_x, two_xc)
    active_far, slope_far = front(two_far)
    qkv = cat(qkv_a, qkv_b, axis=1)
    k3_o, active_far, slope_far, two_far, cot_x, q0_o = sync(
        k3_o, active_far, slope_far, two_far, cot_x, q0_o
    )
    contract_all = cat(contract_own, contract_rest, k1, k1_o, k2, k2_o, k3, k3_o)
    cot_far = cat(cot_x, cot_xc)
    before_far = matmul(cot_far, contract_all, True, slope_far)
    far = matmul(before_far, expand_all, True)
    far, before_far, contract_all = sync(far, before_far, contract_all)
    far_c = core_swap(far[SEG:])
    cot_near = cat(cot, cot_c)
    far, far_c, cot_near, slope_near = sync(far, far_c, cot_near, slope_near)
    two_grad_in = add(far[:SEG], far_c)
    two_grad_xa = chip_swap(two_grad_in[:part])
    before_near = matmul(cot_near, contract_all, True, slope_near)
    near = matmul(before_near, expand_all, True)
    two_grad_xa, two_grad_in, before_near, near, active_near = sync(
        two_grad_xa, two_grad_in, before_near, near, active_near
    )
    two_grad_xb = chip_swap(two_grad_in[part:])
    hidden_order = []
    for r in range(teams):
        owner = (team + teams - r) % teams
        hidden_order += [owner * 2 + second, owner * 2 + 1 - second]
    hidden_order = jnp.stack(hidden_order).astype(jnp.int32)
    contract_grad = weight_grad(
        [(active_near, cot_near, 0), (active_far, cot_far, 0)], step=wide, order=hidden_order
    )
    two_grad_xb, contract_grad, near = sync(two_grad_xb, contract_grad, near)
    contract_mine = scatter_sum(contract_grad)
    near_c = core_swap(near[SEG:])
    near, near_c, two_grad_xb = sync(near, near_c, two_grad_xb)
    normed_two_grad = (
        near[:SEG].astype(F32)
        + near_c.astype(F32)
        + cat(two_grad_xa, two_grad_xb).astype(F32)
    )
    cot_local = cotangent.astype(F32)
    _, pull_second = jax.vjp(normalize, middle, gain_second, shift_second)
    middle_part, second_gain_grad, second_shift_grad = pull_second(normed_two_grad)
    middle_grad = cot_local + middle_part
    middle_low, before_near, active_far = sync(middle_grad.astype(BF16), before_near, active_far)
    middle_xa = chip_swap(middle_low[:part])
    middle_c = core_swap(middle_low)
    expand_grad = weight_grad([(two_near, before_near, 0), (two_far, before_far, 0)])
    middle_xa, middle_c, expand_grad, middle_low = sync(
        middle_xa, middle_c, expand_grad, middle_low
    )
    middle_xb = chip_swap(middle_low[part:])
    halves = shard_halves(expand_grad)
    s3_o = group_swap(halves[3][1])
    s2_o = group_swap(halves[2][1])
    middle_near = cat(middle_low, middle_c)
    mix_grad_near = matmul(middle_near, out_all, True)
    log_near = cat(log_near_a, log_near_b)
    part_grad = attend_back(info, qkv, mix_near, mix_grad_near, log_near, 0, 2)
    two_far_branch = matmul(active_far, contract_all, False)
    middle_xb, s3_o, s2_o, part_grad, expand_grad, middle_near, two_far_branch, q0_late = sync(
        middle_xb, s3_o, s2_o, part_grad, expand_grad, middle_near, two_far_branch, q0_o
    )
    middle_x = cat(middle_xa, middle_xb)
    middle_xc = core_swap(middle_x)
    out_c = core_swap(two_far_branch[SEG:])
    middle_xc, out_c, expand_grad = sync(middle_xc, out_c, expand_grad)
    halves = shard_halves(expand_grad)
    two_branch_x = chip_swap(add(two_far_branch[:SEG], out_c))
    s1_o = group_swap(halves[1][1])
    s0_o = group_swap(halves[0][1])
    a3 = ring_down(add(halves[3][0], s3_o))
    middle_far = cat(middle_x, middle_xc)
    mix_grad_far = matmul(middle_far, out_all, True)
    log_far = cat(log_far_a, log_far_b)
    qkv_grad = attend_back(info, qkv, mix_far, mix_grad_far, log_far, 2, 2, part_grad)
    qkv_all = cat(
        *[
            ordered(v[:tops], o, 0)
            for v, o in ((packed, q0_late), (q1, q1_o[:tops]), (q2, q2_o[:tops]), (q3, q3_o[:tops]))
        ],
        axis=1,
    )
    far = matmul(qkv_grad, qkv_all, True, place=1, rows=near_rows)
    s1_o, s0_o, a3, far, qkv_grad, expand_grad, middle_far, contract_mine, two_branch_x = sync(
        s1_o, s0_o, a3, far, qkv_grad, expand_grad, middle_far, contract_mine, two_branch_x
    )
    far_c = core_swap(far[SEG:])
    far, far_c, qkv_grad = sync(far, far_c, qkv_grad)

    def turn(v, by):
        shift = (by % teams) * block
        return cat(v[:, shift:], v[:, :shift], axis=1) if shift else v

    normed_in = add(far[:SEG], far_c)
    normed_ga = chip_swap(normed_in[:part])
    far_rows = qkv_grad[team_rows:].reshape(TEAM, 2, TAIL, -1)
    one = line_down(far_rows[:, 0].reshape(span, -1))
    two = line_down(far_rows[:, 1].reshape(span, -1), 2)
    contract_sum = other_groups(contract_mine)
    contract_other = group_swap(contract_sum)
    grad_pairs = [
        (v, qkv_grad, n)
        for n, v in enumerate([normed, normed_c, normed_x, normed_xc, cat(rest, rest_c, rest_x, rest_xc)])
    ]
    last_grad = weight_grad(grad_pairs, 1, 2 * block)
    near = matmul(qkv_grad, qkv_all, True, place=0, rows=near_rows)
    place_order = jnp.stack([(team + teams - r) % teams for r in range(teams)]).astype(jnp.int32)
    out_grad = weight_grad(
        [(mix_near, middle_near, 0), (mix_far, middle_far, 0)], step=cols, order=place_order
    )
    normed_ga, normed_in, one, two, last_grad, near, qkv_grad, contract_other, out_grad = sync(
        normed_ga, normed_in, one, two, last_grad, near, qkv_grad, contract_other, out_grad
    )

    def qkv_halves(v, k):
        piece = v[:, k * block : (k + 1) * block]
        return half(piece, 0, second), half(piece, 0, 1 - second)

    out_mine = scatter_sum(out_grad)
    normed_gb = chip_swap(normed_in[part:])
    kept3, sent3 = qkv_halves(last_grad, 1)
    kept2, sent2 = qkv_halves(last_grad, 0)
    q3_in = group_swap(sent3)
    q2_in = group_swap(sent2)
    near_c = core_swap(near[SEG:])
    late = add(turn(one, 1), turn(two, 2))
    late_terms = matmul(late, qkv_all, True)
    grad_pairs = [(v, qkv_grad, n) for v, _, n in grad_pairs]
    first_grad = weight_grad(grad_pairs, 0, 2 * block)
    normed_gb, q3_in, q2_in, near_c, late_terms, first_grad, expand_grad = sync(
        normed_gb, q3_in, q2_in, near_c, late_terms, first_grad, expand_grad
    )
    late_c, late_cn = core_swap(late_terms[3 * TAIL :]), core_swap(late_terms[TAIL : 2 * TAIL])
    late_c, late_cn, late_terms, first_grad, expand_grad = sync(
        late_c, late_cn, late_terms, first_grad, expand_grad
    )
    late_x = chip_swap(add(late_terms[2 * TAIL : 3 * TAIL], late_c))
    kept1, sent1 = qkv_halves(first_grad, 1)
    kept0, sent0 = qkv_halves(first_grad, 0)
    q1_in = group_swap(sent1)
    qa3 = ring_down(add(kept3, q3_in))
    halves = shard_halves(expand_grad)
    late_x, q1_in, qa3, sent0, expand_grad, active_near = sync(
        late_x, q1_in, qa3, sent0, expand_grad, active_near
    )
    q0_in = group_swap(sent0)
    qa2 = ring_down(add(qa3, add(kept2, q2_in)))
    halves = shard_halves(expand_grad)
    a2 = ring_down(add(a3, add(halves[2][0], s2_o)))
    normed_grad = near[:SEG].astype(F32) + near_c.astype(F32) + cat(normed_ga, normed_gb).astype(F32)
    tail = add(late_terms[:TAIL], late_cn).astype(F32) + late_x.astype(F32)
    normed_grad = normed_grad + cat(jnp.zeros((SEG - TAIL, width), F32), tail)
    _, pull_first = jax.vjp(normalize, hidden_in, gain_first, shift_first)
    input_part, first_gain_grad, first_shift_grad = pull_first(normed_grad)
    input_grad = (middle_grad + input_part).astype(BF16)
    qkv_bias_sums = jnp.sum(qkv_grad.astype(F32), axis=0)
    expand_bias_sums = jnp.sum(before_near.astype(F32), axis=0) + jnp.sum(
        before_far.astype(F32), axis=0
    )
    q0_in, qa2, a2, first_gain_grad, first_shift_grad, expand_grad, active_near = sync(
        q0_in, qa2, a2, first_gain_grad, first_shift_grad, expand_grad, active_near
    )
    halves = shard_halves(expand_grad)
    qa1 = ring_down(add(qa2, add(kept1, q1_in)))
    a1 = ring_down(add(a2, add(halves[1][0], s1_o)))
    two_near_branch = matmul(active_near, contract_all, False)
    expand_mine = other_groups(add(a1, add(halves[0][0], s0_o)))
    expand_other = group_swap(expand_mine)
    qkv_mine = other_groups(add(qa1, add(kept0, q0_in)))
    qkv_other = group_swap(qkv_mine)
    out_sum = other_groups(out_mine)
    out_other = group_swap(out_sum)
    small = jnp.concatenate(
        [
            first_gain_grad,
            first_shift_grad,
            jnp.sum(middle_grad, axis=0),
            second_gain_grad,
            second_shift_grad,
            jnp.sum(cot_local, axis=0),
        ]
    )
    place = block + hid
    owners = jnp.zeros((n_mp * place,), F32)
    for r in range(teams):
        owner = (team + teams - r) % teams
        mine_hid = ordered(
            expand_bias_sums[2 * r * wide : (2 * r + 1) * wide],
            expand_bias_sums[(2 * r + 1) * wide : (2 * r + 2) * wide],
            0,
        )
        piece = jnp.concatenate(
            [qkv_bias_sums[r * block : (r + 1) * block], mine_hid]
        )
        owners = lax.dynamic_update_slice(owners, piece, ((owner * TEAM + mine) * place,))

    def total(v, axes):
        for axis, size in axes:
            bit = 1
            while bit < size:
                v = v + lax.ppermute(v, axis, [(i, i ^ bit) for i in range(size)])
                bit *= 2
        return v

    vector = total(jnp.concatenate([small, owners]), (("mp", n_mp), ("dp", n_dp)))
    mine_spot = lax.dynamic_slice(vector, (6 * width + me * place,), (place,))
    six = [vector[k * width : (k + 1) * width] for k in range(6)]

    branch_two = (
        two_near_branch[:SEG].astype(F32)
        + core_swap(two_near_branch[SEG:]).astype(F32)
        + two_branch_x.astype(F32)
    )
    layer_out = (middle + branch_two + contract_bias.astype(F32)).astype(BF16)
    qkv_final = ordered(qkv_mine, qkv_other, 0).astype(F32)
    return (
        layer_out,
        input_grad,
        six[0],
        six[1],
        qkv_final[:, :cols],
        mine_spot[:cols],
        qkv_final[:, cols : 2 * cols],
        qkv_final[:, 2 * cols :],
        mine_spot[2 * cols : 3 * cols],
        ordered(out_sum, out_other, 0).astype(F32),
        six[2],
        six[3],
        six[4],
        ordered(expand_mine, expand_other, 1).astype(F32),
        mine_spot[block:],
        ordered(contract_sum, contract_other, 0).astype(F32),
        six[5],
    )


def solution(mesh):
    rows = P(("dp", "mp"), None)
    in_cols, in_rows = P(None, "mp"), P("mp", None)
    placed = (
        rows,
        P("dp", None),
        P(),
        P(),
        in_cols,
        P("mp"),
        in_cols,
        in_cols,
        P("mp"),
        in_rows,
        P(),
        P(),
        P(),
        in_cols,
        P("mp"),
        in_rows,
        P(),
        rows,
    )
    return jax.shard_map(
        body,
        mesh=mesh,
        in_specs=placed,
        out_specs=(
            rows,
            rows,
            P(),
            P(),
            in_cols,
            P("mp"),
            in_cols,
            in_cols,
            P("mp"),
            in_rows,
            P(),
            P(),
            P(),
            in_cols,
            P("mp"),
            in_rows,
            P(),
        ),
        check_vma=False,
    )
```

time: 4000 us -> 1030 us (0.26)
  waiting for transfers between devices: 2670 us -> 293 us
  matrix products: 819 us -> 38.8 us
  Pallas kernels: 0 us -> 361 us
  local copies, waits for them, and re-layouts: 277 us -> 126 us
  starting transfers between devices: 0.75 us -> 95.4 us
  other arithmetic: 150 us -> 94.3 us
  blocking collectives: 45.1 us -> 0 us
    reduce_scatter x5 -> x2, waiting for transfers between devices: 1650 us -> 0.04 us  [scatter_sum(): lax.psum_scatter(v, ('dp', 'mp'), scatter_dimension=0, axis_index_groups=...]
    all_gather x6 -> x0, waiting for transfers between devices: 929 us -> none  [the longest x2 337 us: attention_part(): gathered = lax.all_gather(normed, 'mp', axis=0, tiled=True)]
    dot_general x150 -> x2, matrix products: 772 us -> 38.8 us  [dot(): return jnp.dot(a, b, preferred_element_type=F32)]
    pallas_call x0 -> x26, Pallas kernels: none -> 361 us  [the longest x13 135 us: matmul(): pl.pallas_call(functools.partial(matmul_kernel, transposed), grid=(column...]
    ppermute x0 -> x86, waiting for transfers between devices: none -> 293 us  [the longest x22 103 us: group_swap(): return lax.ppermute(v, 'dp', [(i, i ^ bit) for i in range(n_dp)])]
    ppermute x0 -> x86, starting transfers between devices: none -> 95.3 us  [the longest x12 27.2 us: ring_up(): lax.ppermute(v, 'mp', [(i, (i + by * TEAM) % n_mp) for i in range(n_mp)])]
    psum x1 -> x0, waiting for transfers between devices: 90.9 us -> none  [body(): lax.psum(query_weight_grad.astype(jnp.bfloat16), 'dp').astype(jnp.float32)]
    squeeze x64 -> x0, local copies, waits for them, and re-layouts: 61.1 us -> none  [attend_forward(): lax.map(one_block, (query_blocks, key_blocks, value_blocks, allowed))]
  transfers between devices with their start and end apart: 12 -> 88, of which waited for: 12 -> 37; matrix products, arithmetic and copies ran while one was open for 4% -> 20% of each run, Pallas kernels for 0% -> 33%
where the time goes in v1:
time: 1030 us; the launch traced here: 1020 us
  Pallas kernels  361 us (35%)
  waiting for transfers between devices  293 us (28%)
  local copies, waits for them, and re-layouts  126 us (12%)
  starting transfers between devices  95.4 us (9%)
  other arithmetic  94.3 us (9%)
  matrix products  38.8 us (4%)
  between operations  16.4 us (2%)
    pallas_call x13, Pallas kernels, matmul(): pl.pallas_call(functools.partial(matmul_kernel, transposed), grid=(column...  135 us
    ppermute x22, waiting for transfers between devices, group_swap(): return lax.ppermute(v, 'dp', [(i, i ^ bit) for i in range(n_dp)])  103 us
    pallas_call x5, Pallas kernels, weight_grad(): pl.pallas_call(weight_grad_kernel, grid_spec=pltpu.PrefetchScalarGridSpec...  90.8 us
    ppermute x17, waiting for transfers between devices, chip_swap(): return lax.ppermute(v, 'mp', [(i, i ^ 2) for i in range(n_mp)])  58.7 us
    unnamed x230, local copies, waits for them, and re-layouts  53.1 us
    pallas_call x2, Pallas kernels, attend_back(): pl.pallas_call(functools.partial(attend_back_kernel, first, count), grid_...  52.8 us
    pallas_call x4, Pallas kernels, attend(): pl.pallas_call(functools.partial(attend_kernel, first, count), grid_spec=...  48 us
    ppermute x6, waiting for transfers between devices, ring_down(): return lax.ppermute(v, 'mp', [(i, (i - TEAM) % n_mp) for i in range(n_mp)])  42 us
  transfers between devices with their start and end apart: 88, of which 37 were waited for; matrix products, arithmetic and copies ran while one was open for 20% of the time, Pallas kernels for 33%

profile of v1, /device:TPU:0, one launch (start us, length us, event | category | flops | bytes accessed | tf_op | source)
XLA Modules:
  0.0 1024.0 jit_solution(16797541195336775436)
XLA Ops:
  30.7 17.1 %collective-permute-done.4 = bf16[64,2048]{1,0:T(8,128)(2,1)S(1)} collective-permute-done((bf16[64,2048]{1,0:T(8,128)(2,1)S(1)}, bf16[64,2048]{1,0:T(8,128)(2,1)S(1)}, u32[]{:S(2)}, u32[]{:S(2)}) %collective-permute-start.4) | collective-permute-done | bytes 262176 | tf_op jit(solution)/shard_map/ppermute | solution.py:431
  66.3 22.4 %collective-permute-done.8.refs_12_.refs_8_ = bf16[128,2048]{1,0:T(8,128)(2,1)S(1)} collective-permute-done((bf16[128,2048]{1,0:T(8,128)(2,1)S(1)}, bf16[128,2048]{1,0:T(8,128)(2,1)S(1)}, u32[]{:S(2)}, u32[]{:S(2)}) %collective-permute-start.8) | collective-permute-done | bytes 524320 | tf_op jit(solution)/shard_map/ppermute | solution.py:422
  133.8 22.2 %project.2.qkv_ref = bf16[2560,1152]{1,0:T(8,128)(2,1)} custom-call(s32[1]{0:T(128)} %bitcast.which_ref, bf16[1040,384]{1,0:T(8,128)(2,1)} %copy-done.30, bf16[1024,384]{1,0:T(8,128)(2,1)} %get-tuple-element.322.refs_1_, bf16[1040,384]{1,0:T(8,128)(2,1)} %copy-done.44, bf16[1040,384]{1,0:T(8,128)(2,1)} %copy-done.46, ...), custom_call_target="tpu_custom_call" | custom-call | flops 1024 | bytes 1024 | tf_op jit(solution)/shard_map/project/pallas_call | solution.py:341
  160.4 16.5 %attend.4 = (bf16[1024,384]{1,0:T(8,128)(2,1)}, f32[3,2,2,512]{3,2,1,0:T(2,128)}) custom-call(s32[18]{0:T(128)} %compare_select_fusion.1.info_ref, bf16[2560,1152]{1,0:T(8,128)(2,1)} %project.2.qkv_ref), custom_call_target="tpu_custom_call" | custom-call | flops 1024 | bytes 1024 | tf_op jit(solution)/shard_map/attend/pallas_call | solution.py:147
  241.9 16.5 %attend.6 = (bf16[1024,384]{1,0:T(8,128)(2,1)}, f32[3,2,2,512]{3,2,1,0:T(2,128)}) custom-call(s32[18]{0:T(128)} %compare_select_fusion.1.info_ref, bf16[2560,1152]{1,0:T(8,128)(2,1)} %project.2.qkv_ref), custom_call_target="tpu_custom_call" | custom-call | flops 1024 | bytes 1024 | tf_op jit(solution)/shard_map/attend/pallas_call | solution.py:147
  327.4 19.5 %collective-permute-done.34 = bf16[256,2048]{1,0:T(8,128)(2,1)} collective-permute-done((bf16[256,2048]{1,0:T(8,128)(2,1)}, bf16[256,2048]{1,0:T(8,128)(2,1)}, u32[]{:S(2)}, u32[]{:S(2)}) %collective-permute-start.34) | collective-permute-done | bytes 1048608 | tf_op jit(solution)/shard_map/ppermute | solution.py:422
  352.9 19.4 %fusion.6 = (bf16[1024,2048]{1,0:T(8,128)(2,1)}, bf16[1024,2048]{1,0:T(8,128)(2,1)}) fusion(f32[2048]{0:T(1024)S(1)} %convert_element_type.325, bf16[1024,2048]{1,0:T(8,128)(2,1)S(1)} %constant_dynamic-update-slice_fusion.12.refs_0_, bf16[2048,2048]{1,0:T(8,128)(2,1)} %slice_dynamic-update-slice_fusion.right_ref), kind=kOutput, calls=%fused_computation.11 | convolution fusion | flops 8633974784 | bytes 20979712 | tf_op jit(solution)/shard_map/dot_general | solution.py:48
  390.1 19.5 %fusion.13 = (bf16[1024,2048]{1,0:T(8,128)(2,1)}, bf16[1024,2048]{1,0:T(8,128)(2,1)}) fusion(f32[2048]{0:T(1024)S(1)} %convert_element_type.325, bf16[1024,2048]{1,0:T(8,128)(2,1)S(1)} %constant_dynamic-update-slice_fusion.14.refs_2_, bf16[2048,2048]{1,0:T(8,128)(2,1)} %slice_dynamic-update-slice_fusion.right_ref), kind=kOutput, calls=%fused_computation.18 | convolution fusion | flops 8633974784 | bytes 20979712 | tf_op jit(solution)/shard_map/dot_general | solution.py:48
  421.7 14.4 %matmul.15.left_ref.refs_3_ = bf16[1024,2048]{1,0:T(8,128)(2,1)} custom-call(bf16[1024,2048]{1,0:T(8,128)(2,1)} %copy-done.12, bf16[2048,2048]{1,0:T(8,128)(2,1)} %constant_dynamic-update-slice_fusion.19.right_ref, bf16[1024,2048]{1,0:T(8,128)(2,1)} %get-tuple-element.276.rest_0_), custom_call_target="tpu_custom_call" | custom-call | flops 1024 | bytes 1024 | tf_op jit(solution)/shard_map/matmul/pallas_call | solution.py:379
  457.8 14.3 %matmul.17.left_ref.refs_1_ = bf16[1024,2048]{1,0:T(8,128)(2,1)} custom-call(bf16[1024,2048]{1,0:T(8,128)(2,1)} %pad_maximum_fusion.1.left_ref.refs_1_, bf16[2048,2048]{1,0:T(8,128)(2,1)} %constant_dynamic-update-slice_fusion.19.right_ref, bf16[1024,2048]{1,0:T(8,128)(2,1)} %get-tuple-element.284.rest_0_), custom_call_target="tpu_custom_call" | custom-call | flops 1024 | bytes 1024 | tf_op jit(solution)/shard_map/matmul/pallas_call | solution.py:379
  487.7 24.6 %weight_grad.5 = bf16[2048,2048]{1,0:T(8,128)(2,1)} custom-call(s32[8]{0:T(128)} %stack.50.order_ref, bf16[1024,2048]{1,0:T(8,128)(2,1)} %get-tuple-element.360.refs_0_.left_ref, bf16[1024,2048]{1,0:T(8,128)(2,1)} %pad_maximum_fusion.1.left_ref.refs_1_, bf16[1024,2048]{1,0:T(8,128)(2,1)} %get-tuple-element.311.refs_2_.left_ref, bf16[1024,2048]{1,0:T(8,128)(2,1)} %copy-done.12), custom_call_target="tpu_custom_call" | custom-call | flops 1024 | bytes 1024 | tf_op jit(solution)/shard_map/weight_grad/pallas_call | solution.py:293
  532.6 25.2 %weight_grad.6 = bf16[2048,2048]{1,0:T(8,128)(2,1)} custom-call(s32[8]{0:T(128)} %iota.20.order_ref, bf16[1024,2048]{1,0:T(8,128)(2,1)} %copy-done.27, bf16[1024,2048]{1,0:T(8,128)(2,1)} %matmul.17.left_ref.refs_1_, bf16[1024,2048]{1,0:T(8,128)(2,1)} %copy-done.33, bf16[1024,2048]{1,0:T(8,128)(2,1)} %matmul.15.left_ref.refs_3_), custom_call_target="tpu_custom_call" | custom-call | flops 1024 | bytes 1024 | tf_op jit(solution)/shard_map/weight_grad/pallas_call | solution.py:293
  572.1 14.8 %matmul.20 = bf16[1024,2048]{1,0:T(8,128)(2,1)} custom-call(bf16[1024,2048]{1,0:T(8,128)(2,1)} %get-tuple-element.311.refs_2_.left_ref, bf16[2048,2048]{1,0:T(8,128)(2,1)} %constant_dynamic-update-slice_fusion.19.right_ref), custom_call_target="tpu_custom_call" | custom-call | flops 1024 | bytes 1024 | tf_op jit(solution)/shard_map/matmul/pallas_call | solution.py:379
  593.1 26.3 %attend_back.2.rest_0_ = bf16[2560,1536]{1,0:T(8,128)(2,1)} custom-call(s32[18]{0:T(128)} %compare_select_fusion.1.info_ref, bf16[2560,1536]{1,0:T(8,128)(2,1)} %constant_dynamic-update-slice_fusion.26.qkv_ref, bf16[1024,512]{1,0:T(8,128)(2,1)} %copy-done.24, bf16[1024,512]{1,0:T(8,128)(2,1)} %matmul.19.grad_ref, f32[4,2,2,512]{3,2,1,0:T(2,128)} %pad_maximum_fusion.9.log_ref), custom_call_target="tpu_custom_call" | custom-call | flops 1024 | bytes 1024 | tf_op jit(solution)/shard_map/attend_back/pallas_call | solution.py:250
  671.8 26.5 %attend_back.3.left_ref.refs_1_.refs_3_.refs_5_.refs_7_.refs_9_ = bf16[2560,1536]{1,0:T(8,128)(2,1)} custom-call(s32[18]{0:T(128)} %compare_select_fusion.1.info_ref, bf16[2560,1536]{1,0:T(8,128)(2,1)} %constant_dynamic-update-slice_fusion.26.qkv_ref, bf16[1024,512]{1,0:T(8,128)(2,1)} %copy-done.23, bf16[1024,512]{1,0:T(8,128)(2,1)} %matmul.21.grad_ref, ...), custom_call_target="tpu_custom_call" | custom-call | flops 1024 | bytes 1024 | tf_op jit(solution)/shard_map/attend_back/pallas_call | solution.py:250
  748.1 15.2 %weight_grad.7 = bf16[2048,768]{1,0:T(8,128)(2,1)} custom-call(s32[8]{0:T(128)} %iota.21.order_ref, bf16[512,2048]{1,0:T(8,128)(2,1)} %copy-done.5, bf16[2560,1536]{1,0:T(8,128)(2,1)} %attend_back.3.left_ref.refs_1_.refs_3_.refs_5_.refs_7_.refs_9_, bf16[512,2048]{1,0:T(8,128)(2,1)} %copy-done.10, ...), custom_call_target="tpu_custom_call" | custom-call | flops 1024 | bytes 1024 | tf_op jit(solution)/shard_map/weight_grad/pallas_call | solution.py:293
  763.3 14.5 %collective-permute-done.61 = bf16[256,1536]{1,0:T(8,128)(2,1)S(1)} collective-permute-done((bf16[256,1536]{1,0:T(8,128)(2,1)S(1)}, bf16[256,1536]{1,0:T(8,128)(2,1)S(1)}, u32[]{:S(2)}, u32[]{:S(2)}) %collective-permute-start.61) | collective-permute-done | bytes 786464 | tf_op jit(solution)/shard_map/ppermute | solution.py:434
  795.3 15.2 %weight_grad.9 = bf16[2048,768]{1,0:T(8,128)(2,1)} custom-call(s32[8]{0:T(128)} %iota.22.order_ref, bf16[512,2048]{1,0:T(8,128)(2,1)} %copy-done.5, bf16[2560,1536]{1,0:T(8,128)(2,1)} %attend_back.3.left_ref.refs_1_.refs_3_.refs_5_.refs_7_.refs_9_, bf16[512,2048]{1,0:T(8,128)(2,1)} %copy-done.10, ...), custom_call_target="tpu_custom_call" | custom-call | flops 1024 | bytes 1024 | tf_op jit(solution)/shard_map/weight_grad/pallas_call | solution.py:293
  816.6 20.4 %collective-permute-done.65 = bf16[1024,384]{1,0:T(8,128)(2,1)} collective-permute-done((bf16[1024,384]{1,0:T(8,128)(2,1)}, bf16[1024,384]{1,0:T(8,128)(2,1)}, u32[]{:S(2)}, u32[]{:S(2)}) %collective-permute-start.65) | collective-permute-done | bytes 786464 | tf_op jit(solution)/shard_map/ppermute | solution.py:437
  849.3 16.7 %collective-permute-done.71 = bf16[1024,384]{1,0:T(8,128)(2,1)S(1)} collective-permute-done((bf16[1024,384]{1,0:T(8,128)(2,1)S(1)}, bf16[1024,384]{1,0:T(8,128)(2,1)S(1)}, u32[]{:S(2)}, u32[]{:S(2)}) %collective-permute-start.71) | collective-permute-done | bytes 786464 | tf_op jit(solution)/shard_map/ppermute | solution.py:428
  889.4 21.1 %collective-permute-done.74 = bf16[2048,256]{1,0:T(8,128)(2,1)} collective-permute-done((bf16[2048,256]{1,0:T(8,128)(2,1)S(1)}, bf16[2048,256]{1,0:T(8,128)(2,1)}, u32[]{:S(2)}, u32[]{:S(2)}) %collective-permute-start.74) | collective-permute-done | bytes 1048608 | tf_op jit(solution)/shard_map/ppermute | solution.py:428
  924.7 16.1 %collective-permute-done.78 = f32[26624]{0:T(1024)S(1)} collective-permute-done((f32[26624]{0:T(1024)S(1)}, f32[26624]{0:T(1024)S(1)}, u32[]{:S(2)}, u32[]{:S(2)}) %collective-permute-start.78) | collective-permute-done | bytes 106528 | tf_op jit(solution)/shard_map/ppermute | solution.py:830
  975.5 14.6 %collective-permute-done.82 = bf16[1024,384]{1,0:T(8,128)(2,1)S(1)} collective-permute-done((bf16[1024,384]{1,0:T(8,128)(2,1)S(1)}, bf16[1024,384]{1,0:T(8,128)(2,1)S(1)}, u32[]{:S(2)}, u32[]{:S(2)}) %collective-permute-start.82) | collective-permute-done | bytes 786464 | tf_op jit(solution)/shard_map/ppermute | solution.py:437
  992.2 17.2 %collective-permute-done.85 = bf16[2048,256]{1,0:T(8,128)(2,1)S(1)} collective-permute-done((bf16[2048,256]{1,0:T(8,128)(2,1)S(1)}, bf16[2048,256]{1,0:T(8,128)(2,1)S(1)}, u32[]{:S(2)}, u32[]{:S(2)}) %collective-permute-start.85) | collective-permute-done | bytes 1048608 | tf_op jit(solution)/shard_map/ppermute | solution.py:437
  (584 shorter events, 557.2 us)
Async XLA Ops:
  7.3 701.8 %reduce-scatter.3.cloned.1.call-start = ((), (), s32[]{:S(2)}) async-start(), calls=%async_computation.2 | async-start | bytes 9437184 | tf_op jit(solution)/shard_map/reduce_scatter | solution.py:503
  121.2 36.2 %collective-permute-start.16 = (bf16[256,2048]{1,0:T(8,128)(2,1)}, bf16[256,2048]{1,0:T(8,128)(2,1)}, u32[]{:S(2)}, u32[]{:S(2)}) collective-permute-start(bf16[256,2048]{1,0:T(8,128)(2,1)} %slice.309), channel_id=1, source_target_pairs={{0,2},{1,3},{2,0},{3,1},{4,6},{5,7},{6,4},{7,5},{8,10},{9,11},{10,... | collective-permute-start | bytes 3145736 | tf_op jit(solution)/shard_map/ppermute | solution.py:422
  185.2 47.2 %collective-permute-start.25 = (bf16[512,2048]{1,0:T(8,128)(2,1)}, bf16[512,2048]{1,0:T(8,128)(2,1)}, u32[]{:S(2)}, u32[]{:S(2)}) collective-permute-start(bf16[512,2048]{1,0:T(8,128)(2,1)} %pad_maximum_fusion.2), channel_id=1, source_target_pairs={{0,1},{1,0},{2,3},{3,2},{4,5},{5,4},{6,7},{7,6},{8,9},{9,8},{10,11... | collective-permute-start | bytes 6291464 | tf_op jit(solution)/shard_map/ppermute | solution.py:419
  512.3 398.4 %reduce-scatter.5.cloned.1.call-start = ((), (), s32[]{:S(2)}) async-start(), calls=%async_computation.3 | async-start | bytes 2359296 | tf_op jit(solution)/shard_map/reduce_scatter | solution.py:503
  558.9 60.5 %collective-permute-start.49 = (bf16[256,2048]{1,0:T(8,128)(2,1)}, bf16[256,2048]{1,0:T(8,128)(2,1)}, u32[]{:S(2)}, u32[]{:S(2)}) collective-permute-start(bf16[256,2048]{1,0:T(8,128)(2,1)} %slice.340), channel_id=1, source_target_pairs={{0,2},{1,3},{2,0},{3,1},{4,6},{5,7},{6,4},{7,5},{8,10},{9,11},{10,... | collective-permute-start | bytes 3145736 | tf_op jit(solution)/shard_map/ppermute | solution.py:422
  563.4 56.1 %collective-permute-start.51 = (bf16[2048,256]{1,0:T(8,128)(2,1)}, bf16[2048,256]{1,0:T(8,128)(2,1)}, u32[]{:S(2)}, u32[]{:S(2)}) collective-permute-start(bf16[2048,256]{1,0:T(8,128)(2,1)} %get-tuple-element.395), channel_id=1, source_target_pairs={{0,16},{16,0},{1,17},{17,1},{2,18},{18,2},{3,19},{19,3},{4,20},{20... | collective-permute-start | bytes 3145736 | tf_op jit(solution)/shard_map/ppermute | solution.py:437
  563.9 69.6 %collective-permute-start.50 = (bf16[2048,256]{1,0:T(8,128)(2,1)}, bf16[2048,256]{1,0:T(8,128)(2,1)}, u32[]{:S(2)}, u32[]{:S(2)}) collective-permute-start(bf16[2048,256]{1,0:T(8,128)(2,1)} %get-tuple-element.396), channel_id=1, source_target_pairs={{0,16},{16,0},{1,17},{17,1},{2,18},{18,2},{3,19},{19,3},{4,20},{20... | collective-permute-start | bytes 3145736 | tf_op jit(solution)/shard_map/ppermute | solution.py:437
  649.6 59.4 %collective-permute-start.57 = (bf16[512,2048]{1,0:T(8,128)(2,1)S(1)}, bf16[512,2048]{1,0:T(8,128)(2,1)}, u32[]{:S(2)}, u32[]{:S(2)}) collective-permute-start(bf16[512,2048]{1,0:T(8,128)(2,1)S(1)} %add_convert_fusion.3), channel_id=1, source_target_pairs={{0,2},{1,3},{2,0},{3,1},{4,6},{5,7},{6,4},{7,5},{8,10},{9,11},{10,... | collective-permute-start | bytes 6291464 | tf_op jit(solution)/shard_map/ppermute | solution.py:422
  653.1 55.9 %collective-permute-start.56 = (bf16[2048,256]{1,0:T(8,128)(2,1)}, bf16[2048,256]{1,0:T(8,128)(2,1)}, u32[]{:S(2)}, u32[]{:S(2)}) collective-permute-start(bf16[2048,256]{1,0:T(8,128)(2,1)} %add_convert_fusion.13), channel_id=1, source_target_pairs={{0,12},{1,13},{2,14},{3,15},{4,0},{5,1},{6,2},{7,3},{8,4},{9,5},{1... | collective-permute-start | bytes 3145736 | tf_op jit(solution)/shard_map/ppermute | solution.py:428
  658.0 50.9 %collective-permute-start.55 = (bf16[2048,256]{1,0:T(8,128)(2,1)}, bf16[2048,256]{1,0:T(8,128)(2,1)}, u32[]{:S(2)}, u32[]{:S(2)}) collective-permute-start(bf16[2048,256]{1,0:T(8,128)(2,1)} %get-tuple-element.393), channel_id=1, source_target_pairs={{0,16},{16,0},{1,17},{17,1},{2,18},{18,2},{3,19},{19,3},{4,20},{20... | collective-permute-start | bytes 3145736 | tf_op jit(solution)/shard_map/ppermute | solution.py:437
  658.0 50.9 %collective-permute-start.54 = (bf16[2048,256]{1,0:T(8,128)(2,1)}, bf16[2048,256]{1,0:T(8,128)(2,1)}, u32[]{:S(2)}, u32[]{:S(2)}) collective-permute-start(bf16[2048,256]{1,0:T(8,128)(2,1)} %get-tuple-element.394), channel_id=1, source_target_pairs={{0,16},{16,0},{1,17},{17,1},{2,18},{18,2},{3,19},{19,3},{4,20},{20... | collective-permute-start | bytes 3145736 | tf_op jit(solution)/shard_map/ppermute | solution.py:437
  716.5 46.8 %collective-permute-start.62 = (bf16[256,2048]{1,0:T(8,128)(2,1)}, bf16[256,2048]{1,0:T(8,128)(2,1)}, u32[]{:S(2)}, u32[]{:S(2)}) collective-permute-start(bf16[256,2048]{1,0:T(8,128)(2,1)} %reduce-scatter.3.cloned.1.call-done), channel_id=1, source_target_pairs={{0,16},{16,0},{1,17},{17,1},{2,18},{18,2},{3,19},{19,3},{4,20},{20... | collective-permute-start | bytes 3145736 | tf_op jit(solution)/shard_map/ppermute | solution.py:437
  719.2 58.7 %collective-permute-start.59 = (bf16[256,2048]{1,0:T(8,128)(2,1)S(1)}, bf16[256,2048]{1,0:T(8,128)(2,1)}, u32[]{:S(2)}, u32[]{:S(2)}) collective-permute-start(bf16[256,2048]{1,0:T(8,128)(2,1)S(1)} %slice.407), channel_id=1, source_target_pairs={{0,2},{1,3},{2,0},{3,1},{4,6},{5,7},{6,4},{7,5},{8,10},{9,11},{10,... | collective-permute-start | bytes 3145736 | tf_op jit(solution)/shard_map/ppermute | solution.py:422
  722.2 41.1 %collective-permute-start.60 = (bf16[256,1536]{1,0:T(8,128)(2,1)}, bf16[256,1536]{1,0:T(8,128)(2,1)S(1)}, u32[]{:S(2)}, u32[]{:S(2)}) collective-permute-start(bf16[256,1536]{1,0:T(8,128)(2,1)} %bitcast.12), channel_id=1, source_target_pairs={{4,0},{5,1},{6,2},{7,3},{8,4},{9,5},{10,6},{11,7},{12,8},{13,9},{1... | collective-permute-start | bytes 2359304 | tf_op jit(solution)/shard_map/ppermute | solution.py:434
  723.7 54.2 %collective-permute-start.61 = (bf16[256,1536]{1,0:T(8,128)(2,1)S(1)}, bf16[256,1536]{1,0:T(8,128)(2,1)S(1)}, u32[]{:S(2)}, u32[]{:S(2)}) collective-permute-start(bf16[256,1536]{1,0:T(8,128)(2,1)S(1)} %bitcast.31), channel_id=1, source_target_pairs={{8,0},{9,1},{10,2},{11,3},{12,4},{13,5},{14,6},{15,7},{24,16},{25,... | collective-permute-start | bytes 2359304 | tf_op jit(solution)/shard_map/ppermute | solution.py:434
  779.5 57.6 %collective-permute-start.66 = (bf16[512,2048]{1,0:T(8,128)(2,1)}, bf16[512,2048]{1,0:T(8,128)(2,1)}, u32[]{:S(2)}, u32[]{:S(2)}) collective-permute-start(bf16[512,2048]{1,0:T(8,128)(2,1)} %slice.364), channel_id=1, source_target_pairs={{0,1},{1,0},{2,3},{3,2},{4,5},{5,4},{6,7},{7,6},{8,9},{9,8},{10,11... | collective-permute-start | bytes 6291464 | tf_op jit(solution)/shard_map/ppermute | solution.py:419
  788.1 49.0 %collective-permute-start.63 = (bf16[256,2048]{1,0:T(8,128)(2,1)}, bf16[256,2048]{1,0:T(8,128)(2,1)}, u32[]{:S(2)}, u32[]{:S(2)}) collective-permute-start(bf16[256,2048]{1,0:T(8,128)(2,1)} %slice.361), channel_id=1, source_target_pairs={{0,2},{1,3},{2,0},{3,1},{4,6},{5,7},{6,4},{7,5},{8,10},{9,11},{10,... | collective-permute-start | bytes 3145736 | tf_op jit(solution)/shard_map/ppermute | solution.py:422
  794.3 42.8 %collective-permute-start.65 = (bf16[1024,384]{1,0:T(8,128)(2,1)}, bf16[1024,384]{1,0:T(8,128)(2,1)}, u32[]{:S(2)}, u32[]{:S(2)}) collective-permute-start(bf16[1024,384]{1,0:T(8,128)(2,1)} %constant_dynamic-slice_fusion.2), channel_id=1, source_target_pairs={{0,16},{16,0},{1,17},{17,1},{2,18},{18,2},{3,19},{19,3},{4,20},{20... | collective-permute-start | bytes 2359304 | tf_op jit(solution)/shard_map/ppermute | solution.py:437
  873.5 37.0 %collective-permute-start.74 = (bf16[2048,256]{1,0:T(8,128)(2,1)S(1)}, bf16[2048,256]{1,0:T(8,128)(2,1)}, u32[]{:S(2)}, u32[]{:S(2)}) collective-permute-start(bf16[2048,256]{1,0:T(8,128)(2,1)S(1)} %add_convert_fusion.11), channel_id=1, source_target_pairs={{0,12},{1,13},{2,14},{3,15},{4,0},{5,1},{6,2},{7,3},{8,4},{9,5},{1... | collective-permute-start | bytes 3145736 | tf_op jit(solution)/shard_map/ppermute | solution.py:428
  910.7 54.6 %collective-permute-start.83 = (bf16[64,2048]{1,0:T(8,128)(2,1)}, bf16[64,2048]{1,0:T(8,128)(2,1)S(1)}, u32[]{:S(2)}, u32[]{:S(2)}) collective-permute-start(bf16[64,2048]{1,0:T(8,128)(2,1)} %reduce-scatter.5.cloned.1.call-done), channel_id=1, source_target_pairs={{0,16},{16,0},{1,17},{17,1},{2,18},{18,2},{3,19},{19,3},{4,20},{20... | collective-permute-start | bytes 786440 | tf_op jit(solution)/shard_map/ppermute | solution.py:437
  916.2 53.1 %collective-permute-start.81 = (bf16[1024,384]{1,0:T(8,128)(2,1)S(1)}, bf16[1024,384]{1,0:T(8,128)(2,1)S(1)}, u32[]{:S(2)}, u32[]{:S(2)}) collective-permute-start(bf16[1024,384]{1,0:T(8,128)(2,1)S(1)} %add_convert_fusion.16), channel_id=1, source_target_pairs={{0,12},{1,13},{2,14},{3,15},{4,0},{5,1},{6,2},{7,3},{8,4},{9,5},{1... | collective-permute-start | bytes 2359304 | tf_op jit(solution)/shard_map/ppermute | solution.py:428
  922.9 48.8 %collective-permute-start.84 = (bf16[2048,256]{1,0:T(8,128)(2,1)S(1)}, bf16[2048,256]{1,0:T(8,128)(2,1)S(1)}, u32[]{:S(2)}, u32[]{:S(2)}) collective-permute-start(bf16[2048,256]{1,0:T(8,128)(2,1)S(1)} %add_convert_fusion.9), channel_id=1, source_target_pairs={{0,12},{1,13},{2,14},{3,15},{4,0},{5,1},{6,2},{7,3},{8,4},{9,5},{1... | collective-permute-start | bytes 3145736 | tf_op jit(solution)/shard_map/ppermute | solution.py:428
  961.3 50.9 %collective-permute-start.75 = (bf16[512,2048]{1,0:T(8,128)(2,1)S(1)}, bf16[512,2048]{1,0:T(8,128)(2,1)S(1)}, u32[]{:S(2)}, u32[]{:S(2)}) collective-permute-start(bf16[512,2048]{1,0:T(8,128)(2,1)S(1)} %slice.411), channel_id=1, source_target_pairs={{0,1},{1,0},{2,3},{3,2},{4,5},{5,4},{6,7},{7,6},{8,9},{9,8},{10,11... | collective-permute-start | bytes 6291464 | tf_op jit(solution)/shard_map/ppermute | solution.py:419
  973.6 35.8 %collective-permute-start.85 = (bf16[2048,256]{1,0:T(8,128)(2,1)S(1)}, bf16[2048,256]{1,0:T(8,128)(2,1)S(1)}, u32[]{:S(2)}, u32[]{:S(2)}) collective-permute-start(bf16[2048,256]{1,0:T(8,128)(2,1)S(1)} %add_convert_fusion.7), channel_id=1, source_target_pairs={{0,16},{16,0},{1,17},{17,1},{2,18},{18,2},{3,19},{19,3},{4,20},{20... | collective-permute-start | bytes 3145736 | tf_op jit(solution)/shard_map/ppermute | solution.py:437
  (159 other events, 2769.2 us)
Sparse Core Ops, SparseCore 0:
  512.4 184.4 reduce-scatter.2
  780.8 76.5 reduce-scatter.4

commit v2 on v1

--- a/solution.py
+++ b/solution.py
@@ -272,37 +272,64 @@
     )(info, qkv, mixture, grad, logs, *more)
 
 
-def weight_grad_kernel(order_ref, *refs):
-    out_ref = refs[-1]
+def weight_grad_kernel(splits, halves, pairs, source_ref, target_ref, *refs):
+    outs = refs[2 * pairs :]
     total = None
-    for left, right in zip(refs[:-1:2], refs[1:-1:2]):
+    for left, right in zip(refs[: 2 * pairs : 2], refs[1 : 2 * pairs : 2]):
         term = dot_tn(left[...], right[...])
         total = term if total is None else total + term
-    out_ref[...] = total.astype(out_ref.dtype)
-
-
-def weight_grad(pairs, column=0, columns=None, step=256, order=None):
+    total = total.astype(BF16)
+    width = total.shape[1] // splits
+    columns = [total[:, k * width : (k + 1) * width] for k in range(splits)]
+    if not halves:
+        for k in range(splits):
+            outs[k][...] = columns[k]
+        return
+    step, steps = pl.program_id(0), pl.num_programs(0)
+
+    @pl.when(step < steps // 2)
+    def _():
+        for k in range(splits):
+            outs[2 * k][...] = columns[k]
+
+    @pl.when(step >= steps // 2)
+    def _():
+        for k in range(splits):
+            outs[2 * k + 1][...] = columns[k]
+
+
+def weight_grad(pairs, column=0, columns=None, step=256, splits=1, source=None, target=None, halves=False):
     height = pairs[0][0].shape[1]
     columns = columns or pairs[0][1].shape[1]
-    if order is None:
-        order = jnp.arange(height // step, dtype=jnp.int32)
+    steps, width = height // step, columns // splits
+    plain = jnp.arange(steps, dtype=jnp.int32)
     specs = []
     for left, right, n in pairs:
-        specs.append(pl.BlockSpec((left.shape[0], step), lambda i, o: (0, i)))
-        specs.append(pl.BlockSpec((left.shape[0], columns), lambda i, o, n=n: (n, column)))
+        specs.append(pl.BlockSpec((left.shape[0], step), lambda i, s, t: (0, s[i])))
+        specs.append(pl.BlockSpec((left.shape[0], columns), lambda i, s, t, n=n: (n, column)))
+    if halves:
+        outs = [
+            pl.BlockSpec((step, width), lambda i, s, t: (jnp.minimum(i, steps // 2 - 1), 0)),
+            pl.BlockSpec((step, width), lambda i, s, t: (jnp.maximum(i - steps // 2, 0), 0)),
+        ] * splits
+        shapes = [jax.ShapeDtypeStruct((height // 2, width), BF16)] * (2 * splits)
+    else:
+        outs = [pl.BlockSpec((step, width), lambda i, s, t: (t[i], 0))] * splits
+        shapes = [jax.ShapeDtypeStruct((height, width), BF16)] * splits
     return pl.pallas_call(
-        weight_grad_kernel,
+        functools.partial(weight_grad_kernel, splits, halves, len(pairs)),
         grid_spec=pltpu.PrefetchScalarGridSpec(
-            num_scalar_prefetch=1,
-            grid=(height // step,),
-            in_specs=specs,
-            out_specs=pl.BlockSpec((step, columns), lambda i, o: (o[i], 0)),
+            num_scalar_prefetch=2, grid=(steps,), in_specs=specs, out_specs=outs
         ),
-        out_shape=jax.ShapeDtypeStruct((height, columns), BF16),
+        out_shape=shapes,
         compiler_params=pltpu.CompilerParams(vmem_limit_bytes=56 * 1024 * 1024),
         cost_estimate=LIGHT,
         name="weight_grad",
-    )(order, *[v for pair in pairs for v in pair[:2]])
+    )(
+        plain if source is None else source,
+        plain if target is None else target,
+        *[v for pair in pairs for v in pair[:2]],
+    )
 
 
 def project_kernel(pieces, which_ref, *refs):
@@ -315,10 +342,10 @@
     )
     depth, block = first.shape[0], first.shape[1] // pieces
     for n in range(pieces):
-        first[:, n * block : (n + 1) * block] = weights[2 * n][:depth, :]
-        last[:, n * block : (n + 1) * block] = weights[2 * n + 1][:depth, :]
+        first[:, n * block : (n + 1) * block] = weights[2 * n][:depth, :block]
+        last[:, n * block : (n + 1) * block] = weights[2 * n + 1][:depth, :block]
     bias = jnp.concatenate(
-        [weights[2 * n][depth : depth + 1, :].astype(F32) for n in range(pieces)], axis=1
+        [weights[2 * n][depth : depth + 1, :block].astype(F32) for n in range(pieces)], axis=1
     )
     lane = lax.broadcasted_iota(jnp.int32, bias.shape, 1)
     scale = jnp.where(lane % block < PAIR, HD**-0.5, 1.0)
@@ -336,7 +363,7 @@
 
 def project(which, weights, rows):
     pieces = len(weights)
-    depth, block = rows[0].shape[1] // 2, weights[0][0].shape[1]
+    depth, block = rows[0].shape[1] // 2, 3 * PAIR
     height = sum(v.shape[0] for v in rows)
     return pl.pallas_call(
         functools.partial(project_kernel, pieces),
@@ -354,18 +381,20 @@
     )(which, *[v for pair in weights for v in pair], *rows)
 
 
-def matmul_kernel(transposed, left_ref, right_ref, *rest):
-    out_ref = rest[-1]
-    chunk = min(256, left_ref.shape[0])
+def matmul_kernel(transposed, parts, left_ref, right_ref, *rest):
+    outs = rest[-parts:]
+    rows = left_ref.shape[0] // parts
+    chunk = min(256, rows)
     for start in range(0, left_ref.shape[0], chunk):
-        rows = slice(start, start + chunk)
-        value = (dot_nt if transposed else dot)(left_ref[rows, :], right_ref[...])
-        if len(rest) == 2:
-            value = value * rest[0][rows, :].astype(F32)
-        out_ref[rows, :] = value.astype(BF16)
-
-
-def matmul(left, right, transposed, scale=None, place=0, rows=None, step=512):
+        here = slice(start, start + chunk)
+        value = (dot_nt if transposed else dot)(left_ref[here, :], right_ref[...])
+        if len(rest) > parts:
+            value = value * rest[0][here, :].astype(F32)
+        at = start % rows
+        outs[start // rows][at : at + chunk, :] = value.astype(BF16)
+
+
+def matmul(left, right, transposed, scale=None, place=0, rows=None, step=512, parts=1):
     rows = rows or left.shape[0]
     depth = left.shape[1]
     columns = right.shape[0] if transposed else right.shape[1]
@@ -374,19 +403,19 @@
         if transposed
         else pl.BlockSpec((depth, step), lambda i: (0, i))
     )
-    out_spec = pl.BlockSpec((rows, step), lambda i: (0, i))
     more = () if scale is None else (scale,)
-    return pl.pallas_call(
-        functools.partial(matmul_kernel, transposed),
+    out = pl.pallas_call(
+        functools.partial(matmul_kernel, transposed, parts),
         grid=(columns // step,),
         in_specs=[pl.BlockSpec((rows, depth), lambda i: (place, 0)), right_spec]
-        + [out_spec] * len(more),
-        out_specs=out_spec,
-        out_shape=jax.ShapeDtypeStruct((rows, columns), BF16),
+        + [pl.BlockSpec((rows, step), lambda i: (0, i))] * len(more),
+        out_specs=[pl.BlockSpec((rows // parts, step), lambda i: (0, i))] * parts,
+        out_shape=[jax.ShapeDtypeStruct((rows // parts, columns), BF16)] * parts,
         compiler_params=pltpu.CompilerParams(vmem_limit_bytes=56 * 1024 * 1024),
         cost_estimate=LIGHT,
         name="matmul",
     )(left, right, *more)
+    return out if parts > 1 else out[0]
 
 
 def body(
@@ -477,6 +506,9 @@
     block = 3 * PAIR
     pad = 16
 
+    def across_swap(v):
+        return lax.ppermute(v, "mp", [(i, i ^ 3) for i in range(n_mp)])
+
     def with_bias(weight, bias):
         return jnp.concatenate(
             [weight, jnp.broadcast_to(bias[None], (pad, bias.shape[0]))], axis=0
@@ -486,12 +518,7 @@
         size = terms.shape[0] // 2
         return add(terms[:size], core_swap(terms[size:]))
 
-    def shard_halves(v):
-        return [
-            [v[:, (2 * r + k) * wide : (2 * r + k + 1) * wide] for k in range(2)]
-            for r in range(teams)
-        ]
-
+    along = [[t * TEAM + i for t in range(teams)] for i in range(TEAM)]
     part = SEG // 2
     pairs_along = [
         [(first + d) * n_mp + t * TEAM + i for t in range(teams) for d in range(2)]
@@ -507,8 +534,10 @@
     def cat(*parts, axis=0):
         return jnp.concatenate(parts, axis=axis)
 
-    qkv_local = cat(query_weight, key_weight, value_weight, axis=1)
-    qkv_bias_local = cat(query_bias, jnp.zeros_like(query_bias), value_bias)
+    qkv_local = cat(query_weight, key_weight, value_weight, output_weight.T, axis=1)
+    qkv_bias_local = cat(
+        query_bias, jnp.zeros_like(query_bias), value_bias, jnp.zeros_like(query_bias)
+    )
     packed = with_bias(half(qkv_local, 0, second), qkv_bias_local)
     q0_o = half(qkv_local, 0, 1 - second)
     hidden_in = inputs.astype(F32)
@@ -517,98 +546,102 @@
     q1 = ring_up(packed)
     normed_xa = chip_swap(normed[:part])
     normed_c = core_swap(normed)
-    early = line_up(normed[SEG - TAIL :])
-    earlier = line_up(normed[SEG - TAIL :], 2)
-    q1, normed_xa, normed_c, early, earlier, normed = sync(
-        q1, normed_xa, normed_c, early, earlier, normed
+    normed_tail, normed_b = normed[SEG - TAIL :], normed[part:]
+    q1, normed_xa, normed_c, normed_tail, normed_b = sync(
+        q1, normed_xa, normed_c, normed_tail, normed_b
     )
     q2 = ring_up(q1)
+    normed_xb = chip_swap(normed_b)
     q1_o = group_swap(q1)
-    normed_xb = chip_swap(normed[part:])
-    rest = cat(early, earlier)
-    rest_x = chip_swap(rest)
-    rest_c = core_swap(rest)
-    q2, q1_o, normed_xb, rest_x, rest_c, cot = sync(q2, q1_o, normed_xb, rest_x, rest_c, cotangent)
+    early = line_up(normed_tail)
+    earlier = line_up(normed_tail, 2)
+    q2, q1_o, normed_x, rest = sync(q2, q1_o, cat(normed_xa, normed_xb), cat(early, earlier))
     q3 = ring_up(q2)
     q2_o = group_swap(q2)
-    normed_x = cat(normed_xa, normed_xb)
     normed_xc = core_swap(normed_x)
-    rest_xc = core_swap(rest_x)
-    cot_xa = chip_swap(cot[:part])
+    rest_x = chip_swap(rest)
+    rest_xc = across_swap(rest)
+    rest_c = core_swap(rest)
     tops = width // 2
-    out_half = half(output_weight, 0, second)
-    q3, q2_o, normed_xc, rest_xc, cot_xa, cot_late, out_half, expand_weight, expand_bias = sync(
-        q3, q2_o, normed_xc, rest_xc, cot_xa, cot, out_half, expand_weight, expand_bias
+    expand_own, expand_rest = half(expand_weight, 1, second), half(expand_weight, 1, 1 - second)
+    expand_bias_own = half(expand_bias, 0, second)
+    expand_bias_rest = half(expand_bias, 0, 1 - second)
+    q3, q2_o, normed_xc, rest_x, rest_xc, rest_c, cot_a, cot_b, e0 = sync(
+        q3,
+        q2_o,
+        normed_xc,
+        rest_x,
+        rest_xc,
+        rest_c,
+        cotangent[:part],
+        cotangent[part:],
+        with_bias(expand_own, expand_bias_own),
     )
     q3_o = group_swap(q3)
-    out_h = [ring_up(out_half, r) for r in range(1, teams)]
-    cot_xb = chip_swap(cot_late[part:])
+    e1 = ring_up(e0)
+    cot_xa = chip_swap(cot_a)
     row_blocks = [normed, normed_c, normed_x, normed_xc, rest, rest_c, rest_x, rest_xc]
     which = jnp.reshape(second, (1,)).astype(jnp.int32)
     qkv_a = project(which, [(packed, q0_o), (q1, q1_o), (q2, q2_o)], row_blocks)
-    expand_own, expand_rest = half(expand_weight, 1, second), half(expand_weight, 1, 1 - second)
-    expand_bias_own = half(expand_bias, 0, second)
-    expand_bias_rest = half(expand_bias, 0, 1 - second)
-    q3_o, cot_xb, qkv_a, e0, cot_late, *out_h = sync(
-        q3_o, cot_xb, qkv_a, with_bias(expand_own, expand_bias_own), cot_late, *out_h
-    )
-    e1 = ring_up(e0)
-    out_o = group_swap(cat(*out_h))
-    cot_c = core_swap(cot_late)
-    mix_far_a, log_far_a = attend(info, qkv_a, 2, 2)
-    e1, out_o, cot_c, mix_far_a, cot_x = sync(e1, out_o, cot_c, mix_far_a, cat(cot_xa, cot_xb))
+    q3_o, cot_xa, qkv_a, e1, cot_b, cot = sync(q3_o, cot_xa, qkv_a, e1, cot_b, cotangent)
     e2 = ring_up(e1)
     e1_o = group_swap(e1)
-    cot_xc = core_swap(cot_x)
+    cot_xb = chip_swap(cot_b)
+    cot_c = core_swap(cot)
+    mix_far_a, log_far_a = attend(info, qkv_a, 2, 2)
     qkv_b = project(which, [(q3, q3_o)], row_blocks)
     mix_far_b, log_far_b = attend(info, qkv_b, 2, 2)
-    quarter = cols // 2
-    out_all = cat(
-        output_weight,
-        *[ordered(v, out_o[r * quarter : (r + 1) * quarter], 0) for r, v in enumerate(out_h)],
-    )
+    held_pieces = ((packed, q0_o), (q1, q1_o[:tops]), (q2, q2_o[:tops]), (q3, q3_o[:tops]))
+    out_all = cat(*[ordered(v[:tops, block:], o[:, block:], 0) for v, o in held_pieces], axis=1)
     mix_far = cat(mix_far_a, mix_far_b, axis=1)
-    far = matmul(mix_far, out_all, False)
-    e2, e1_o, cot_xc, qkv_b, far, out_all, contract_weight = sync(
-        e2, e1_o, cot_xc, qkv_b, far, out_all, contract_weight
-    )
-    far_c = core_swap(far[SEG:])
-    far, far_c, qkv_a = sync(far, far_c, qkv_a)
-    branch_in = add(far[:SEG], far_c)
-    branch_xa = chip_swap(branch_in[:part])
+    far, far_sent = matmul(mix_far, out_all, True, parts=2)
+    cot_x = cat(cot_xa, cot_xb)
+    e2, e1_o, cot_x, cot_c, qkv_a, qkv_b, far, far_sent, out_all, contract_weight = sync(
+        e2, e1_o, cot_x, cot_c, qkv_a, qkv_b, far, far_sent, out_all, contract_weight
+    )
+    cot_xc = core_swap(cot_x)
+    far_c = core_swap(far_sent)
+    contract_own = half(contract_weight, 0, second)
+    contract_rest = half(contract_weight, 0, 1 - second)
+    far, far_c, qkv_a, cot_xc = sync(far, far_c, qkv_a, cot_xc)
+    branch_in = add(far[part:], far_c[part:])
+    branch_xa = chip_swap(add(far[:part], far_c[:part]))
     e3 = ring_up(e2)
     e2_o = group_swap(e2)
     mix_near_a, log_near_a = attend(info, qkv_a, 0, 2)
-    contract_own = half(contract_weight, 0, second)
-    contract_rest = half(contract_weight, 0, 1 - second)
     branch_xa, e3, e2_o, mix_near_a, branch_in, contract_own, qkv_b = sync(
         branch_xa, e3, e2_o, mix_near_a, branch_in, contract_own, qkv_b
     )
-    branch_xb = chip_swap(branch_in[part:])
+    branch_xb = chip_swap(branch_in)
     k1 = ring_up(contract_own)
     e3_o = group_swap(e3)
     mix_near_b, log_near_b = attend(info, qkv_b, 0, 2)
     mix_near = cat(mix_near_a, mix_near_b, axis=1)
-    near = matmul(mix_near, out_all, False)
-    branch_xb, k1, e3_o, near, mix_near = sync(branch_xb, k1, e3_o, near, mix_near)
-    near_c = core_swap(near[SEG:])
+    near, near_sent = matmul(mix_near, out_all, True, parts=2)
+    branch_xb, k1, e3_o, near, near_sent, mix_near = sync(
+        branch_xb, k1, e3_o, near, near_sent, mix_near
+    )
+    near_c = core_swap(near_sent)
     near, near_c, k1 = sync(near, near_c, k1)
     branch_x = cat(branch_xa, branch_xb)
-    branch = near[:SEG].astype(F32) + near_c.astype(F32) + branch_x.astype(F32)
+    branch = near.astype(F32) + near_c.astype(F32) + branch_x.astype(F32)
     middle = hidden_in + branch + output_bias.astype(F32)
     normed_two = normalize(middle, gain_second, shift_second).astype(BF16)
-    normed_two, k1, e3_o = sync(normed_two, k1, e3_o)
+    normed_two, k1, e3_o, *held = sync(normed_two, k1, e3_o, *[v for p in held_pieces for v in p])
     two_xa = chip_swap(normed_two[:part])
     two_c = core_swap(normed_two)
     k2 = ring_up(k1)
     k1_o = group_swap(k1)
     expand_pairs = (e1, e1_o, e2, e2_o, e3, e3_o)
     expand_all = cat(expand_own, expand_rest, *[v[:width] for v in expand_pairs], axis=1)
+    qkv_all = cat(
+        *[ordered(v[:tops, :block], o[:, :block], 0) for v, o in zip(held[0::2], held[1::2])], axis=1
+    )
     expand_bias_all = cat(
         expand_bias_own, expand_bias_rest, *[v[width] for v in expand_pairs]
     ).astype(F32)
-    two_xa, two_c, k2, k1_o, expand_all, expand_bias_all, normed_two = sync(
-        two_xa, two_c, k2, k1_o, expand_all, expand_bias_all, normed_two
+    two_xa, two_c, k2, k1_o, expand_all, expand_bias_all, normed_two, qkv_all = sync(
+        two_xa, two_c, k2, k1_o, expand_all, expand_bias_all, normed_two, qkv_all
     )
     two_xb = chip_swap(normed_two[part:])
     k3 = ring_up(k2)
@@ -618,51 +651,48 @@
         value, slope = gelu_and_slope(dot(rows, expand_all) + expand_bias_all)
         return value.astype(BF16), slope.astype(BF16)
 
+    two_xac = core_swap(two_xa)
     two_near = cat(normed_two, two_c)
     active_near, slope_near = front(two_near)
-    two_xb, k3, k2_o, active_near, slope_near, two_near = sync(
-        two_xb, k3, k2_o, active_near, slope_near, two_near
-    )
-    two_x = cat(two_xa, two_xb)
-    two_xc = core_swap(two_x)
-    two_xc, k3, qkv_a, qkv_b, cot_c = sync(two_xc, k3, qkv_a, qkv_b, cot_c)
+    two_xb, k3, k2_o, active_near, slope_near, two_near, two_xac = sync(
+        two_xb, k3, k2_o, active_near, slope_near, two_near, two_xac
+    )
+    two_xbc = core_swap(two_xb)
+    two_xbc, k3, qkv_a, qkv_b, cot_c = sync(two_xbc, k3, qkv_a, qkv_b, cot_c)
     k3_o = group_swap(k3)
-    two_far = cat(two_x, two_xc)
+    two_far = cat(two_xa, two_xb, two_xac, two_xbc)
     active_far, slope_far = front(two_far)
     qkv = cat(qkv_a, qkv_b, axis=1)
-    k3_o, active_far, slope_far, two_far, cot_x, q0_o = sync(
-        k3_o, active_far, slope_far, two_far, cot_x, q0_o
-    )
+    k3_o, active_far, slope_far, two_far, cot_x = sync(k3_o, active_far, slope_far, two_far, cot_x)
     contract_all = cat(contract_own, contract_rest, k1, k1_o, k2, k2_o, k3, k3_o)
     cot_far = cat(cot_x, cot_xc)
     before_far = matmul(cot_far, contract_all, True, slope_far)
-    far = matmul(before_far, expand_all, True)
-    far, before_far, contract_all = sync(far, before_far, contract_all)
-    far_c = core_swap(far[SEG:])
+    far, far_sent = matmul(before_far, expand_all, True, parts=2)
+    far, far_sent, before_far, contract_all = sync(far, far_sent, before_far, contract_all)
+    far_c = core_swap(far_sent)
     cot_near = cat(cot, cot_c)
     far, far_c, cot_near, slope_near = sync(far, far_c, cot_near, slope_near)
-    two_grad_in = add(far[:SEG], far_c)
-    two_grad_xa = chip_swap(two_grad_in[:part])
+    two_grad_in = add(far[part:], far_c[part:])
+    two_grad_xa = chip_swap(add(far[:part], far_c[:part]))
     before_near = matmul(cot_near, contract_all, True, slope_near)
-    near = matmul(before_near, expand_all, True)
-    two_grad_xa, two_grad_in, before_near, near, active_near = sync(
-        two_grad_xa, two_grad_in, before_near, near, active_near
-    )
-    two_grad_xb = chip_swap(two_grad_in[part:])
+    near, near_sent = matmul(before_near, expand_all, True, parts=2)
+    two_grad_xa, two_grad_in, before_near, near, near_sent, active_near = sync(
+        two_grad_xa, two_grad_in, before_near, near, near_sent, active_near
+    )
+    two_grad_xb = chip_swap(two_grad_in)
+    near_c = core_swap(near_sent)
     hidden_order = []
     for r in range(teams):
         owner = (team + teams - r) % teams
         hidden_order += [owner * 2 + second, owner * 2 + 1 - second]
     hidden_order = jnp.stack(hidden_order).astype(jnp.int32)
-    contract_grad = weight_grad(
-        [(active_near, cot_near, 0), (active_far, cot_far, 0)], step=wide, order=hidden_order
-    )
-    two_grad_xb, contract_grad, near = sync(two_grad_xb, contract_grad, near)
+    (contract_grad,) = weight_grad(
+        [(active_near, cot_near, 0), (active_far, cot_far, 0)], step=wide, target=hidden_order
+    )
+    two_grad_xb, contract_grad, near, near_c = sync(two_grad_xb, contract_grad, near, near_c)
     contract_mine = scatter_sum(contract_grad)
-    near_c = core_swap(near[SEG:])
-    near, near_c, two_grad_xb = sync(near, near_c, two_grad_xb)
     normed_two_grad = (
-        near[:SEG].astype(F32)
+        near.astype(F32)
         + near_c.astype(F32)
         + cat(two_grad_xa, two_grad_xb).astype(F32)
     )
@@ -673,111 +703,157 @@
     middle_low, before_near, active_far = sync(middle_grad.astype(BF16), before_near, active_far)
     middle_xa = chip_swap(middle_low[:part])
     middle_c = core_swap(middle_low)
-    expand_grad = weight_grad([(two_near, before_near, 0), (two_far, before_far, 0)])
-    middle_xa, middle_c, expand_grad, middle_low = sync(
-        middle_xa, middle_c, expand_grad, middle_low
-    )
-    middle_xb = chip_swap(middle_low[part:])
-    halves = shard_halves(expand_grad)
-    s3_o = group_swap(halves[3][1])
-    s2_o = group_swap(halves[2][1])
+    expand_parts = weight_grad(
+        [(two_near, before_near, 0), (two_far, before_far, 0)], splits=2 * teams
+    )
+    kept, sent = expand_parts[0::2], expand_parts[1::2]
+    middle_low_b = middle_low[part:]
+    middle_xa, middle_c, middle_low, middle_low_b, *sent = sync(
+        middle_xa, middle_c, middle_low, middle_low_b, *sent
+    )
+    middle_xb = chip_swap(middle_low_b)
+    middle_xac = core_swap(middle_xa)
+    s3_o = group_swap(sent[3])
     middle_near = cat(middle_low, middle_c)
-    mix_grad_near = matmul(middle_near, out_all, True)
+    mix_grad_near = matmul(middle_near, out_all, False)
     log_near = cat(log_near_a, log_near_b)
     part_grad = attend_back(info, qkv, mix_near, mix_grad_near, log_near, 0, 2)
-    two_far_branch = matmul(active_far, contract_all, False)
-    middle_xb, s3_o, s2_o, part_grad, expand_grad, middle_near, two_far_branch, q0_late = sync(
-        middle_xb, s3_o, s2_o, part_grad, expand_grad, middle_near, two_far_branch, q0_o
-    )
-    middle_x = cat(middle_xa, middle_xb)
-    middle_xc = core_swap(middle_x)
-    out_c = core_swap(two_far_branch[SEG:])
-    middle_xc, out_c, expand_grad = sync(middle_xc, out_c, expand_grad)
-    halves = shard_halves(expand_grad)
-    two_branch_x = chip_swap(add(two_far_branch[:SEG], out_c))
-    s1_o = group_swap(halves[1][1])
-    s0_o = group_swap(halves[0][1])
-    a3 = ring_down(add(halves[3][0], s3_o))
-    middle_far = cat(middle_x, middle_xc)
-    mix_grad_far = matmul(middle_far, out_all, True)
+    middle_xb, s3_o, part_grad, middle_near, active_far, middle_xac, *sent = sync(
+        middle_xb, s3_o, part_grad, middle_near, active_far, middle_xac, *sent
+    )
+    middle_xbc = core_swap(middle_xb)
+    s3 = add(kept[3], s3_o)
+    middle_xbc, s3, *sent = sync(middle_xbc, s3, *sent)
+    s2_o = group_swap(sent[2])
+    s1_o = group_swap(sent[1])
+    a3 = ring_down(s3)
+    middle_far = cat(middle_xa, middle_xb, middle_xac, middle_xbc)
+    mix_grad_far = matmul(middle_far, out_all, False)
     log_far = cat(log_far_a, log_far_b)
     qkv_grad = attend_back(info, qkv, mix_far, mix_grad_far, log_far, 2, 2, part_grad)
-    qkv_all = cat(
-        *[
-            ordered(v[:tops], o, 0)
-            for v, o in ((packed, q0_late), (q1, q1_o[:tops]), (q2, q2_o[:tops]), (q3, q3_o[:tops]))
-        ],
-        axis=1,
-    )
-    far = matmul(qkv_grad, qkv_all, True, place=1, rows=near_rows)
-    s1_o, s0_o, a3, far, qkv_grad, expand_grad, middle_far, contract_mine, two_branch_x = sync(
-        s1_o, s0_o, a3, far, qkv_grad, expand_grad, middle_far, contract_mine, two_branch_x
-    )
-    far_c = core_swap(far[SEG:])
-    far, far_c, qkv_grad = sync(far, far_c, qkv_grad)
-
-    def turn(v, by):
-        shift = (by % teams) * block
-        return cat(v[:, shift:], v[:, :shift], axis=1) if shift else v
-
-    normed_in = add(far[:SEG], far_c)
-    normed_ga = chip_swap(normed_in[:part])
-    far_rows = qkv_grad[team_rows:].reshape(TEAM, 2, TAIL, -1)
-    one = line_down(far_rows[:, 0].reshape(span, -1))
-    two = line_down(far_rows[:, 1].reshape(span, -1), 2)
+    far, far_sent = matmul(qkv_grad, qkv_all, True, place=1, rows=near_rows, parts=2)
+    far_rows = qkv_grad[team_rows:].reshape(TEAM, 2, TAIL, teams, 3, PAIR)[:, :, :, :, 1:]
+    one = far_rows[:, 0].reshape(span, -1)
+    two = far_rows[:, 1].reshape(span, -1)
+    s2_o, s1_o, a3, far, far_sent, qkv_grad, middle_far, contract_mine, one, two, sent0 = sync(
+        s2_o, s1_o, a3, far, far_sent, qkv_grad, middle_far, contract_mine, one, two, sent[0]
+    )
+    far_c = core_swap(far_sent)
+    far, far_c, qkv_grad, mix_near = sync(far, far_c, qkv_grad, mix_near)
+    normed_in = add(far[part:], far_c[part:])
+    normed_ga = chip_swap(add(far[:part], far_c[:part]))
+    one = line_down(one)
+    two = line_down(two, 2)
+    s0_o = group_swap(sent0)
     contract_sum = other_groups(contract_mine)
     contract_other = group_swap(contract_sum)
+    row_halves = jnp.arange(8, dtype=jnp.int32)
+    row_halves = jnp.where(second == 0, row_halves, (row_halves + 4) % 8)
     grad_pairs = [
         (v, qkv_grad, n)
         for n, v in enumerate([normed, normed_c, normed_x, normed_xc, cat(rest, rest_c, rest_x, rest_xc)])
     ]
-    last_grad = weight_grad(grad_pairs, 1, 2 * block)
-    near = matmul(qkv_grad, qkv_all, True, place=0, rows=near_rows)
+    kept2, sent2, kept3, sent3 = weight_grad(
+        grad_pairs, 1, 2 * block, splits=2, source=row_halves, halves=True, step=width // 8
+    )
+    near, near_sent = matmul(qkv_grad, qkv_all, True, place=0, rows=near_rows, parts=2)
+    a3_s2 = add(a3, add(kept[2], s2_o))
     place_order = jnp.stack([(team + teams - r) % teams for r in range(teams)]).astype(jnp.int32)
-    out_grad = weight_grad(
-        [(mix_near, middle_near, 0), (mix_far, middle_far, 0)], step=cols, order=place_order
-    )
-    normed_ga, normed_in, one, two, last_grad, near, qkv_grad, contract_other, out_grad = sync(
-        normed_ga, normed_in, one, two, last_grad, near, qkv_grad, contract_other, out_grad
-    )
-
-    def qkv_halves(v, k):
-        piece = v[:, k * block : (k + 1) * block]
-        return half(piece, 0, second), half(piece, 0, 1 - second)
-
+    (out_grad,) = weight_grad(
+        [(mix_near, middle_near, 0), (mix_far, middle_far, 0)], step=cols, target=place_order
+    )
+    (
+        normed_ga,
+        normed_in,
+        one,
+        two,
+        s0_o,
+        sent2,
+        sent3,
+        near,
+        near_sent,
+        qkv_grad,
+        a3_s2,
+        active_far,
+        out_grad,
+        contract_other,
+    ) = sync(
+        normed_ga,
+        normed_in,
+        one,
+        two,
+        s0_o,
+        sent2,
+        sent3,
+        near,
+        near_sent,
+        qkv_grad,
+        a3_s2,
+        active_far,
+        out_grad,
+        contract_other,
+    )
     out_mine = scatter_sum(out_grad)
-    normed_gb = chip_swap(normed_in[part:])
-    kept3, sent3 = qkv_halves(last_grad, 1)
-    kept2, sent2 = qkv_halves(last_grad, 0)
+    normed_gb = chip_swap(normed_in)
     q3_in = group_swap(sent3)
     q2_in = group_swap(sent2)
-    near_c = core_swap(near[SEG:])
-    late = add(turn(one, 1), turn(two, 2))
+    a2 = ring_down(a3_s2)
+    near_c = core_swap(near_sent)
+
+    def turn(v, by):
+        shift = (by % teams) * 2 * PAIR
+        return cat(v[:, shift:], v[:, :shift], axis=1) if shift else v
+
+    late = add(turn(one, 1), turn(two, 2)).reshape(span, teams, 2, PAIR)
+    late = jnp.pad(late, ((0, 0), (0, 0), (1, 0), (0, 0))).reshape(span, teams * block)
     late_terms = matmul(late, qkv_all, True)
     grad_pairs = [(v, qkv_grad, n) for v, _, n in grad_pairs]
-    first_grad = weight_grad(grad_pairs, 0, 2 * block)
-    normed_gb, q3_in, q2_in, near_c, late_terms, first_grad, expand_grad = sync(
-        normed_gb, q3_in, q2_in, near_c, late_terms, first_grad, expand_grad
-    )
-    late_c, late_cn = core_swap(late_terms[3 * TAIL :]), core_swap(late_terms[TAIL : 2 * TAIL])
-    late_c, late_cn, late_terms, first_grad, expand_grad = sync(
-        late_c, late_cn, late_terms, first_grad, expand_grad
-    )
-    late_x = chip_swap(add(late_terms[2 * TAIL : 3 * TAIL], late_c))
-    kept1, sent1 = qkv_halves(first_grad, 1)
-    kept0, sent0 = qkv_halves(first_grad, 0)
+    kept0, sent0, kept1, sent1 = weight_grad(
+        grad_pairs, 0, 2 * block, splits=2, source=row_halves, halves=True, step=width // 8
+    )
+    two_far_branch, two_far_sent = matmul(active_far, contract_all, False, parts=2)
+    (
+        normed_gb,
+        q3_in,
+        q2_in,
+        a2,
+        near_c,
+        late_terms,
+        sent0,
+        sent1,
+        two_far_branch,
+        two_far_sent,
+        active_near,
+    ) = sync(
+        normed_gb,
+        q3_in,
+        q2_in,
+        a2,
+        near_c,
+        late_terms,
+        sent0,
+        sent1,
+        two_far_branch,
+        two_far_sent,
+        active_near,
+    )
+    out_c = core_swap(two_far_sent)
+    late_n = core_swap(late_terms[TAIL : 2 * TAIL])
+    late_x = chip_swap(late_terms[2 * TAIL : 3 * TAIL])
+    late_xc = across_swap(late_terms[3 * TAIL :])
+    q3_sum = add(kept3, q3_in)
+    a2_s1 = add(a2, add(kept[1], s1_o))
+    late_n, late_x, late_xc, q3_sum, a2_s1, sent0, sent1, out_c, active_near, q2_in = sync(
+        late_n, late_x, late_xc, q3_sum, a2_s1, sent0, sent1, out_c, active_near, q2_in
+    )
+    branch_two_xa = chip_swap(add(two_far_branch[:part], out_c[:part]))
+    branch_two_in = add(two_far_branch[part:], out_c[part:])
     q1_in = group_swap(sent1)
-    qa3 = ring_down(add(kept3, q3_in))
-    halves = shard_halves(expand_grad)
-    late_x, q1_in, qa3, sent0, expand_grad, active_near = sync(
-        late_x, q1_in, qa3, sent0, expand_grad, active_near
-    )
-    q0_in = group_swap(sent0)
-    qa2 = ring_down(add(qa3, add(kept2, q2_in)))
-    halves = shard_halves(expand_grad)
-    a2 = ring_down(add(a3, add(halves[2][0], s2_o)))
-    normed_grad = near[:SEG].astype(F32) + near_c.astype(F32) + cat(normed_ga, normed_gb).astype(F32)
-    tail = add(late_terms[:TAIL], late_cn).astype(F32) + late_x.astype(F32)
+    qa3 = ring_down(q3_sum)
+    normed_grad = near.astype(F32) + near_c.astype(F32) + cat(normed_ga, normed_gb).astype(F32)
+    tail = functools.reduce(
+        jnp.add, [v.astype(F32) for v in (late_terms[:TAIL], late_n, late_x, late_xc)]
+    )
     normed_grad = normed_grad + cat(jnp.zeros((SEG - TAIL, width), F32), tail)
     _, pull_first = jax.vjp(normalize, hidden_in, gain_first, shift_first)
     input_part, first_gain_grad, first_shift_grad = pull_first(normed_grad)
@@ -786,19 +862,6 @@
     expand_bias_sums = jnp.sum(before_near.astype(F32), axis=0) + jnp.sum(
         before_far.astype(F32), axis=0
     )
-    q0_in, qa2, a2, first_gain_grad, first_shift_grad, expand_grad, active_near = sync(
-        q0_in, qa2, a2, first_gain_grad, first_shift_grad, expand_grad, active_near
-    )
-    halves = shard_halves(expand_grad)
-    qa1 = ring_down(add(qa2, add(kept1, q1_in)))
-    a1 = ring_down(add(a2, add(halves[1][0], s1_o)))
-    two_near_branch = matmul(active_near, contract_all, False)
-    expand_mine = other_groups(add(a1, add(halves[0][0], s0_o)))
-    expand_other = group_swap(expand_mine)
-    qkv_mine = other_groups(add(qa1, add(kept0, q0_in)))
-    qkv_other = group_swap(qkv_mine)
-    out_sum = other_groups(out_mine)
-    out_other = group_swap(out_sum)
     small = jnp.concatenate(
         [
             first_gain_grad,
@@ -823,22 +886,52 @@
         )
         owners = lax.dynamic_update_slice(owners, piece, ((owner * TEAM + mine) * place,))
 
-    def total(v, axes):
-        for axis, size in axes:
-            bit = 1
-            while bit < size:
-                v = v + lax.ppermute(v, axis, [(i, i ^ bit) for i in range(size)])
-                bit *= 2
-        return v
-
-    vector = total(jnp.concatenate([small, owners]), (("mp", n_mp), ("dp", n_dp)))
+    vector, q1_in, qa3, branch_two_xa, branch_two_in, sent0, a2_s1 = sync(
+        cat(small, owners), q1_in, qa3, branch_two_xa, branch_two_in, sent0, a2_s1
+    )
+
+    def add_shifts(shifts, here):
+        shifts = jnp.stack(shifts)
+        return functools.reduce(jnp.add, [shifts[here(i)] for i in range(shifts.shape[0])])
+
+    shifts = [vector, core_swap(vector), chip_swap(vector), across_swap(vector)]
+    q0_in = group_swap(sent0)
+    a1 = ring_down(a2_s1)
+    qa3_sum = add(qa3, add(kept2, q2_in))
+    q0_in, a1, qa3_sum, active_near, out_mine, *shifts = sync(
+        q0_in, a1, qa3_sum, active_near, out_mine, *shifts
+    )
+    vector = add_shifts(shifts, lambda i: mine ^ i)
+    shifts = [vector] + [ring_up(vector, r) for r in range(1, teams)]
+    qa2 = ring_down(qa3_sum)
+    expand_mine = other_groups(add(a1, add(kept[0], s0_o)))
+    expand_other = group_swap(expand_mine)
+    two_near_branch, two_near_sent = matmul(active_near, contract_all, False, parts=2)
+    qa2, expand_other, two_near_branch, two_near_sent, branch_two_in, *shifts = sync(
+        qa2, expand_other, two_near_branch, two_near_sent, branch_two_in, *shifts
+    )
+    vector = add_shifts(shifts, lambda i: (team + teams - i) % teams)
+    bit = 1
+    while bit < n_dp:
+        vector = vector + group_swap(vector, bit)
+        bit *= 2
+    qa1 = ring_down(add(qa2, add(kept1, q1_in)))
+    branch_two_xb = chip_swap(branch_two_in)
+    two_near_c = core_swap(two_near_sent)
+    out_sum = other_groups(out_mine)
+    out_other = group_swap(out_sum)
+    vector, qa1, branch_two_xb, two_near_c, out_other = sync(
+        vector, qa1, branch_two_xb, two_near_c, out_other
+    )
+    qkv_mine = other_groups(add(qa1, add(kept0, q0_in)))
+    qkv_other = group_swap(qkv_mine)
     mine_spot = lax.dynamic_slice(vector, (6 * width + me * place,), (place,))
     six = [vector[k * width : (k + 1) * width] for k in range(6)]
 
     branch_two = (
-        two_near_branch[:SEG].astype(F32)
-        + core_swap(two_near_branch[SEG:]).astype(F32)
-        + two_branch_x.astype(F32)
+        two_near_branch.astype(F32)
+        + two_near_c.astype(F32)
+        + cat(branch_two_xa, branch_two_xb).astype(F32)
     )
     layer_out = (middle + branch_two + contract_bias.astype(F32)).astype(BF16)
     qkv_final = ordered(qkv_mine, qkv_other, 0).astype(F32)

time: 1030 us -> 935 us (0.908)
  waiting for transfers between devices: 293 us -> 202 us
  other arithmetic: 94.3 us -> 109 us
    ppermute x22, waiting for transfers between devices: 103 us -> 54.5 us  [group_swap(): return lax.ppermute(v, 'dp', [(i, i ^ bit) for i in range(n_dp)])]
    ppermute x12, waiting for transfers between devices: 22.6 us -> 2.09 us  [ring_up(): lax.ppermute(v, 'mp', [(i, (i + by * TEAM) % n_mp) for i in range(n_mp)])]
    ppermute x6, waiting for transfers between devices: 42 us -> 22.1 us  [ring_down(): return lax.ppermute(v, 'mp', [(i, (i - TEAM) % n_mp) for i in range(n_mp)])]
    reduce_scatter x2, waiting for transfers between devices: 0.04 us -> 18.4 us  [scatter_sum(): lax.psum_scatter(v, ('dp', 'mp'), scatter_dimension=0, axis_index_groups=...]
    ppermute x2, waiting for transfers between devices: 14.5 us -> 0.01 us  [line_down(): lax.ppermute(v, 'mp', [(i + by * TEAM, i) for i in range(n_mp - by * TEAM)])]
    ppermute x5 -> x3, waiting for transfers between devices: 22.9 us -> 10.1 us  [across_swap(): return lax.ppermute(v, 'mp', [(i, i ^ 3) for i in range(n_mp)])]
    slice x34 -> x27, local copies, waits for them, and re-layouts: 35.8 us -> 24.1 us  [the longest x4 5.44 us: body(): v[:tops, :block]]
    convert_element_type x14 -> x13, other arithmetic: 20 us -> 28.2 us  [add(): functools.reduce(jnp.add, [t.astype(F32) for t in terms]).astype(BF16)]
  transfers between devices with their start and end apart: 88 -> 89, of which waited for: 37 -> 28; matrix products, arithmetic and copies ran while one was open for 20% -> 24% of each run, Pallas kernels for 33% -> 36%
where the time goes in v2:
time: 935 us; the launch traced here: 929 us
  Pallas kernels  358 us (38%)
  waiting for transfers between devices  202 us (22%)
  local copies, waits for them, and re-layouts  121 us (13%)
  other arithmetic  109 us (12%)
  starting transfers between devices  89.9 us (10%)
  matrix products  31.7 us (3%)
  between operations  16.3 us (2%)
    pallas_call x13, Pallas kernels, matmul(): pl.pallas_call(functools.partial(matmul_kernel, transposed, parts), grid=...  132 us
    pallas_call x5, Pallas kernels, weight_grad(): pl.pallas_call(functools.partial(weight_grad_kernel, splits, halves, len(...  91.9 us
    ppermute x19, waiting for transfers between devices, chip_swap(): return lax.ppermute(v, 'mp', [(i, i ^ 2) for i in range(n_mp)])  63.7 us
    unnamed x247, local copies, waits for them, and re-layouts  59.4 us
    ppermute x22, waiting for transfers between devices, group_swap(): return lax.ppermute(v, 'dp', [(i, i ^ bit) for i in range(n_dp)])  54.5 us
    pallas_call x2, Pallas kernels, attend_back(): pl.pallas_call(functools.partial(attend_back_kernel, first, count), grid_...  52.4 us
    pallas_call x4, Pallas kernels, attend(): pl.pallas_call(functools.partial(attend_kernel, first, count), grid_spec=...  47.9 us
    pallas_call x2, Pallas kernels, project(): pl.pallas_call(functools.partial(project_kernel, pieces), grid_spec=pltpu...  34.1 us
  transfers between devices with their start and end apart: 89, of which 28 were waited for; matrix products, arithmetic and copies ran while one was open for 24% of the time, Pallas kernels for 36%

profile of v2, /device:TPU:0, one launch (start us, length us, event | category | flops | bytes accessed | tf_op | source)
XLA Modules:
  0.0 928.8 jit_solution(11317838298832045544)
XLA Ops:
  21.5 23.7 %collective-permute-done.1 = bf16[256,2048]{1,0:T(8,128)(2,1)S(1)} collective-permute-done((bf16[256,2048]{1,0:T(8,128)(2,1)S(1)}, bf16[256,2048]{1,0:T(8,128)(2,1)S(1)}, u32[]{:S(2)}, u32[]{:S(2)}) %collective-permute-start.1) | collective-permute-done | bytes 1048608 | tf_op jit(solution)/shard_map/ppermute | solution.py:451
  58.4 22.3 %collective-permute-done.7 = bf16[64,2048]{1,0:T(8,128)(2,1)S(1)} collective-permute-done((bf16[64,2048]{1,0:T(8,128)(2,1)S(1)}, bf16[64,2048]{1,0:T(8,128)(2,1)S(1)}, u32[]{:S(2)}, u32[]{:S(2)}) %collective-permute-start.7) | collective-permute-done | bytes 262176 | tf_op jit(solution)/shard_map/ppermute | solution.py:460
  112.2 11.9 %collective-permute-done.11.refs_12_.refs_8_ = bf16[128,2048]{1,0:T(8,128)(2,1)S(1)} collective-permute-done((bf16[128,2048]{1,0:T(8,128)(2,1)S(1)}, bf16[128,2048]{1,0:T(8,128)(2,1)S(1)}, u32[]{:S(2)}, u32[]{:S(2)}) %collective-permute-start.11) | collective-permute-done | bytes 524320 | tf_op jit(solution)/shard_map/ppermute | solution.py:451
  128.9 22.5 %project.2.qkv_ref = bf16[2560,1152]{1,0:T(8,128)(2,1)} custom-call(s32[1]{0:T(128)} %bitcast.1.which_ref, bf16[1040,512]{1,0:T(8,128)(2,1)} %copy-done.18, bf16[1024,512]{1,0:T(8,128)(2,1)} %get-tuple-element.337.refs_1_, bf16[1040,512]{1,0:T(8,128)(2,1)} %copy-done.34, bf16[1040,512]{1,0:T(8,128)(2,1)} %collective-permute-done.4.refs_3_, ...), custom_call_target="tpu_custom_call" | custom-call | flops 1024 | bytes 1024 | tf_op jit(solution)/shard_map/project/pallas_call | solution.py:368
  162.8 11.6 %project.3.qkv_ref = bf16[2560,384]{1,0:T(8,128)(2,1)} custom-call(s32[1]{0:T(128)} %bitcast.1.which_ref, bf16[1040,512]{1,0:T(8,128)(2,1)} %collective-permute-done.8.refs_0_, bf16[1040,512]{1,0:T(8,128)(2,1)} %collective-permute-done.14.refs_1_, bf16[512,2048]{1,0:T(8,128)(2,1)} %copy-done.5, bf16[512,2048]{1,0:T(8,128)(2,1)} %copy-done.10, ...), custom_call_target="tpu_custom_call" | custom-call | flops 1024 | bytes 1024 | tf_op jit(solution)/shard_map/project/pallas_call | solution.py:368
  182.8 16.5 %attend.4 = (bf16[1024,384]{1,0:T(8,128)(2,1)}, f32[3,2,2,512]{3,2,1,0:T(2,128)}) custom-call(s32[18]{0:T(128)} %compare_select_fusion.3.info_ref, bf16[2560,1152]{1,0:T(8,128)(2,1)} %project.2.qkv_ref), custom_call_target="tpu_custom_call" | custom-call | flops 1024 | bytes 1024 | tf_op jit(solution)/shard_map/attend/pallas_call | solution.py:147
  231.8 16.5 %attend.6 = (bf16[1024,384]{1,0:T(8,128)(2,1)}, f32[3,2,2,512]{3,2,1,0:T(2,128)}) custom-call(s32[18]{0:T(128)} %compare_select_fusion.3.info_ref, bf16[2560,1152]{1,0:T(8,128)(2,1)} %project.2.qkv_ref), custom_call_target="tpu_custom_call" | custom-call | flops 1024 | bytes 1024 | tf_op jit(solution)/shard_map/attend/pallas_call | solution.py:147
  338.5 15.8 %fusion.6 = (bf16[1024,2048]{1,0:T(8,128)(2,1)}, bf16[1024,2048]{1,0:T(8,128)(2,1)}) fusion(f32[2048]{0:T(1024)S(1)} %convert_element_type.360, bf16[1024,2048]{1,0:T(8,128)(2,1)S(1)} %constant_dynamic-update-slice_fusion.5.refs_0_, bf16[2048,2048]{1,0:T(8,128)(2,1)S(1)} %slice_dynamic-update-slice_fusion.right_ref), kind=kOutput, calls=%fused_computation.11 | convolution fusion | flops 8633974784 | bytes 20979712 | tf_op jit(solution)/shard_map/dot_general | solution.py:48
  366.3 15.9 %fusion.13 = (bf16[1024,2048]{1,0:T(8,128)(2,1)}, bf16[1024,2048]{1,0:T(8,128)(2,1)}) fusion(f32[2048]{0:T(1024)S(1)} %convert_element_type.360, bf16[1024,2048]{1,0:T(8,128)(2,1)S(1)} %constant_dynamic-update-slice_fusion.7.refs_2_, bf16[2048,2048]{1,0:T(8,128)(2,1)S(1)} %slice_dynamic-update-slice_fusion.right_ref), kind=kOutput, calls=%fused_computation.18 | convolution fusion | flops 8633974784 | bytes 20979712 | tf_op jit(solution)/shard_map/dot_general | solution.py:48
  396.3 14.3 %matmul.15.left_ref.refs_3_ = bf16[1024,2048]{1,0:T(8,128)(2,1)} custom-call(bf16[1024,2048]{1,0:T(8,128)(2,1)} %copy-done.12, bf16[2048,2048]{1,0:T(8,128)(2,1)} %constant_dynamic-update-slice_fusion.13.right_ref, bf16[1024,2048]{1,0:T(8,128)(2,1)} %get-tuple-element.361.rest_0_), custom_call_target="tpu_custom_call" | custom-call | flops 1024 | bytes 1024 | tf_op jit(solution)/shard_map/matmul/pallas_call | solution.py:407
  410.6 13.4 %matmul.16 = (bf16[512,2048]{1,0:T(8,128)(2,1)}, bf16[512,2048]{1,0:T(8,128)(2,1)}) custom-call(bf16[1024,2048]{1,0:T(8,128)(2,1)} %matmul.15.left_ref.refs_3_, bf16[2048,2048]{1,0:T(8,128)(2,1)} %copy-done.7), custom_call_target="tpu_custom_call" | custom-call | flops 1024 | bytes 1024 | tf_op jit(solution)/shard_map/matmul/pallas_call | solution.py:407
  432.2 14.3 %matmul.17.left_ref.refs_1_ = bf16[1024,2048]{1,0:T(8,128)(2,1)} custom-call(bf16[1024,2048]{1,0:T(8,128)(2,1)} %pad_maximum_fusion.1.left_ref.refs_1_, bf16[2048,2048]{1,0:T(8,128)(2,1)} %constant_dynamic-update-slice_fusion.13.right_ref, bf16[1024,2048]{1,0:T(8,128)(2,1)} %get-tuple-element.372.rest_0_), custom_call_target="tpu_custom_call" | custom-call | flops 1024 | bytes 1024 | tf_op jit(solution)/shard_map/matmul/pallas_call | solution.py:407
  446.5 13.2 %matmul.18 = (bf16[512,2048]{1,0:T(8,128)(2,1)}, bf16[512,2048]{1,0:T(8,128)(2,1)}) custom-call(bf16[1024,2048]{1,0:T(8,128)(2,1)} %matmul.17.left_ref.refs_1_, bf16[2048,2048]{1,0:T(8,128)(2,1)} %copy-done.7), custom_call_target="tpu_custom_call" | custom-call | flops 1024 | bytes 1024 | tf_op jit(solution)/shard_map/matmul/pallas_call | solution.py:407
  461.6 24.7 %weight_grad.5 = bf16[2048,2048]{1,0:T(8,128)(2,1)} custom-call(s32[8]{0:T(128)} %iota.33.source_ref, s32[8]{0:T(128)} %stack.80.target_ref, bf16[1024,2048]{1,0:T(8,128)(2,1)} %get-tuple-element.498.refs_0_.left_ref, bf16[1024,2048]{1,0:T(8,128)(2,1)} %pad_maximum_fusion.1.left_ref.refs_1_, bf16[1024,2048]{1,0:T(8,128)(2,1)} %get-tuple-element.460.refs_2_.left_ref, ...), custom_call_target="tpu_custom_call" | custom-call | flops 1024 | bytes 1024 | tf_op jit(solution)/shard_map/weight_grad/pallas_call | solution.py:319
  505.2 25.3 %weight_grad.6 = (bf16[2048,256]{1,0:T(8,128)(2,1)}, bf16[2048,256]{1,0:T(8,128)(2,1)}, bf16[2048,256]{1,0:T(8,128)(2,1)}, bf16[2048,256]{1,0:T(8,128)(2,1)}, bf...) custom-call(s32[8]{0:T(128)} %iota.34.source_ref.target_ref, ...), custom_call_target="tpu_custom_call" | custom-call | flops 1024 | bytes 1024 | tf_op jit(solution)/shard_map/weight_grad/pallas_call | solution.py:319
  545.9 25.9 %attend_back.2.rest_0_ = bf16[2560,1536]{1,0:T(8,128)(2,1)} custom-call(s32[18]{0:T(128)} %compare_select_fusion.3.info_ref, bf16[2560,1536]{1,0:T(8,128)(2,1)} %constant_dynamic-update-slice_fusion.20.qkv_ref, bf16[1024,512]{1,0:T(8,128)(2,1)} %copy-done.16, bf16[1024,512]{1,0:T(8,128)(2,1)} %matmul.19.grad_ref, f32[4,2,2,512]{3,2,1,0:T(2,128)} %pad_maximum_fusion.11.log_ref), custom_call_target="tpu_custom_call" | custom-call | flops 1024 | bytes 1024 | tf_op jit(solution)/shard_map/attend_back/pallas_call | solution.py:250
  590.0 26.5 %attend_back.3.left_ref.refs_1_.refs_3_.refs_5_.refs_7_.refs_9_ = bf16[2560,1536]{1,0:T(8,128)(2,1)} custom-call(s32[18]{0:T(128)} %compare_select_fusion.3.info_ref, bf16[2560,1536]{1,0:T(8,128)(2,1)} %constant_dynamic-update-slice_fusion.20.qkv_ref, bf16[1024,512]{1,0:T(8,128)(2,1)} %copy-done.15, bf16[1024,512]{1,0:T(8,128)(2,1)} %matmul.20.grad_ref, ...), custom_call_target="tpu_custom_call" | custom-call | flops 1024 | bytes 1024 | tf_op jit(solution)/shard_map/attend_back/pallas_call | solution.py:250
  674.0 15.4 %weight_grad.7 = (bf16[1024,384]{1,0:T(8,128)(2,1)}, bf16[1024,384]{1,0:T(8,128)(2,1)}, bf16[1024,384]{1,0:T(8,128)(2,1)}, bf16[1024,384]{1,0:T(8,128)(2,1)}) custom-call(s32[8]{0:T(128)} %broadcast_select_fusion.source_ref, s32[8]{0:T(128)} %iota.37.target_ref, bf16[512,2048]{1,0:T(8,128)(2,1)} %copy-done.5, ...), custom_call_target="tpu_custom_call" | custom-call | flops 1024 | bytes 1024 | tf_op jit(solution)/shard_map/weight_grad/pallas_call | solution.py:319
  721.8 13.0 %matmul.24 = (bf16[512,2048]{1,0:T(8,128)(2,1)}, bf16[512,2048]{1,0:T(8,128)(2,1)}) custom-call(bf16[1024,2048]{1,0:T(8,128)(2,1)} %get-tuple-element.460.refs_2_.left_ref, bf16[2048,2048]{1,0:T(8,128)(2,1)} %constant_dynamic-update-slice_fusion.13.right_ref), custom_call_target="tpu_custom_call" | custom-call | flops 1024 | bytes 1024 | tf_op jit(solution)/shard_map/matmul/pallas_call | solution.py:407
  735.4 16.1 %weight_grad.9 = (bf16[1024,384]{1,0:T(8,128)(2,1)}, bf16[1024,384]{1,0:T(8,128)(2,1)}, bf16[1024,384]{1,0:T(8,128)(2,1)}, bf16[1024,384]{1,0:T(8,128)(2,1)}) custom-call(s32[8]{0:T(128)} %broadcast_select_fusion.source_ref, s32[8]{0:T(128)} %iota.39.target_ref, bf16[512,2048]{1,0:T(8,128)(2,1)} %copy-done.5, ...), custom_call_target="tpu_custom_call" | custom-call | flops 1024 | bytes 1024 | tf_op jit(solution)/shard_map/weight_grad/pallas_call | solution.py:319
  786.2 20.8 %collective-permute-done.68 = bf16[1024,384]{1,0:T(8,128)(2,1)S(1)} collective-permute-done((bf16[1024,384]{1,0:T(8,128)(2,1)S(1)}, bf16[1024,384]{1,0:T(8,128)(2,1)S(1)}, u32[]{:S(2)}, u32[]{:S(2)}) %collective-permute-start.68) | collective-permute-done | bytes 786464 | tf_op jit(solution)/shard_map/ppermute | solution.py:466
  814.3 11.4 %reduce-scatter.5.cloned.1.call-done = bf16[64,2048]{1,0:T(8,128)(2,1)} async-done(((bf16[512,2048]{1,0:T(8,128)(2,1)}), bf16[64,2048]{1,0:T(8,128)(2,1)}) %reduce-scatter.5.cloned.1.call-update) | async-done | bytes 262160 | tf_op jit(solution)/shard_map/reduce_scatter | solution.py:530
  852.3 13.2 %matmul.25 = (bf16[512,2048]{1,0:T(8,128)(2,1)}, bf16[512,2048]{1,0:T(8,128)(2,1)}) custom-call(bf16[1024,2048]{1,0:T(8,128)(2,1)} %get-tuple-element.498.refs_0_.left_ref, bf16[2048,2048]{1,0:T(8,128)(2,1)} %constant_dynamic-update-slice_fusion.13.right_ref), custom_call_target="tpu_custom_call" | custom-call | flops 1024 | bytes 1024 | tf_op jit(solution)/shard_map/matmul/pallas_call | solution.py:407
  905.4 14.2 %collective-permute-done.86 = bf16[1024,384]{1,0:T(8,128)(2,1)S(1)} collective-permute-done((bf16[1024,384]{1,0:T(8,128)(2,1)S(1)}, bf16[1024,384]{1,0:T(8,128)(2,1)S(1)}, u32[]{:S(2)}, u32[]{:S(2)}) %collective-permute-start.86) | collective-permute-done | bytes 786464 | tf_op jit(solution)/shard_map/ppermute | solution.py:466
  (599 shorter events, 494.0 us)
Async XLA Ops:
  7.3 640.1 %reduce-scatter.3.cloned.1.call-start = ((), (), s32[]{:S(2)}) async-start(), calls=%async_computation.2 | async-start | bytes 9437184 | tf_op jit(solution)/shard_map/reduce_scatter | solution.py:530
  86.7 37.4 %collective-permute-start.10 = (bf16[512,2048]{1,0:T(8,128)(2,1)}, bf16[512,2048]{1,0:T(8,128)(2,1)}, u32[]{:S(2)}, u32[]{:S(2)}) collective-permute-start(bf16[512,2048]{1,0:T(8,128)(2,1)} %pad_maximum_fusion.3.refs_8_.refs_4_), channel_id=1, source_target_pairs={{0,1},{1,0},{2,3},{3,2},{4,5},{5,4},{6,7},{7,6},{8,9},{9,8},{10,11... | collective-permute-start | bytes 6291464 | tf_op jit(solution)/shard_map/ppermute | solution.py:448
  86.7 37.3 %collective-permute-start.9 = (bf16[1040,512]{1,0:T(8,128)(2,1)}, bf16[1040,512]{1,0:T(8,128)(2,1)}, u32[]{:S(2)}, u32[]{:S(2)}) collective-permute-start(bf16[1040,512]{1,0:T(8,128)(2,1)} %copy-done.35), channel_id=1, source_target_pairs={{0,16},{16,0},{1,17},{17,1},{2,18},{18,2},{3,19},{19,3},{4,20},{20... | collective-permute-start | bytes 3194888 | tf_op jit(solution)/shard_map/ppermute | solution.py:466
  153.2 58.7 %collective-permute-start.20 = (bf16[512,2048]{1,0:T(8,128)(2,1)}, bf16[512,2048]{1,0:T(8,128)(2,1)}, u32[]{:S(2)}, u32[]{:S(2)}) collective-permute-start(bf16[512,2048]{1,0:T(8,128)(2,1)} %param.35), channel_id=1, source_target_pairs={{0,1},{1,0},{2,3},{3,2},{4,5},{5,4},{6,7},{7,6},{8,9},{9,8},{10,11... | collective-permute-start | bytes 6291464 | tf_op jit(solution)/shard_map/ppermute | solution.py:448
  158.9 51.3 %collective-permute-start.19 = (bf16[256,2048]{1,0:T(8,128)(2,1)}, bf16[256,2048]{1,0:T(8,128)(2,1)}, u32[]{:S(2)}, u32[]{:S(2)}) collective-permute-start(bf16[256,2048]{1,0:T(8,128)(2,1)} %get-tuple-element.294), channel_id=1, source_target_pairs={{0,2},{1,3},{2,0},{3,1},{4,6},{5,7},{6,4},{7,5},{8,10},{9,11},{10,... | collective-permute-start | bytes 3145736 | tf_op jit(solution)/shard_map/ppermute | solution.py:451
  161.7 50.2 %collective-permute-start.18 = (bf16[2064,256]{1,0:T(8,128)(2,1)}, bf16[2064,256]{1,0:T(8,128)(2,1)}, u32[]{:S(2)}, u32[]{:S(2)}) collective-permute-start(bf16[2064,256]{1,0:T(8,128)(2,1)} %collective-permute-done.16), channel_id=1, source_target_pairs={{0,16},{16,0},{1,17},{17,1},{2,18},{18,2},{3,19},{19,3},{4,20},{20... | collective-permute-start | bytes 3170312 | tf_op jit(solution)/shard_map/ppermute | solution.py:466
  162.3 49.6 %collective-permute-start.17 = (bf16[2064,256]{1,0:T(8,128)(2,1)}, bf16[2064,256]{1,0:T(8,128)(2,1)}, u32[]{:S(2)}, u32[]{:S(2)}) collective-permute-start(bf16[2064,256]{1,0:T(8,128)(2,1)} %collective-permute-done.16), channel_id=1, source_target_pairs={{0,4},{1,5},{2,6},{3,7},{4,8},{5,9},{6,10},{7,11},{8,12},{9,13},{1... | collective-permute-start | bytes 3170312 | tf_op jit(solution)/shard_map/ppermute | solution.py:454
  486.3 339.4 %reduce-scatter.5.cloned.1.call-start = ((), (), s32[]{:S(2)}) async-start(), calls=%async_computation.3 | async-start | bytes 2359296 | tf_op jit(solution)/shard_map/reduce_scatter | solution.py:530
  530.5 41.3 %collective-permute-start.46 = (bf16[256,2048]{1,0:T(8,128)(2,1)}, bf16[256,2048]{1,0:T(8,128)(2,1)}, u32[]{:S(2)}, u32[]{:S(2)}) collective-permute-start(bf16[256,2048]{1,0:T(8,128)(2,1)} %get-tuple-element.395), channel_id=1, source_target_pairs={{0,2},{1,3},{2,0},{3,1},{4,6},{5,7},{6,4},{7,5},{8,10},{9,11},{10,... | collective-permute-start | bytes 3145736 | tf_op jit(solution)/shard_map/ppermute | solution.py:451
  531.2 40.6 %collective-permute-start.47 = (bf16[2048,256]{1,0:T(8,128)(2,1)}, bf16[2048,256]{1,0:T(8,128)(2,1)}, u32[]{:S(2)}, u32[]{:S(2)}) collective-permute-start(bf16[2048,256]{1,0:T(8,128)(2,1)} %get-tuple-element.396), channel_id=1, source_target_pairs={{0,16},{16,0},{1,17},{17,1},{2,18},{18,2},{3,19},{19,3},{4,20},{20... | collective-permute-start | bytes 3145736 | tf_op jit(solution)/shard_map/ppermute | solution.py:466
  531.8 40.0 %collective-permute-start.48 = (bf16[256,2048]{1,0:T(8,128)(2,1)}, bf16[256,2048]{1,0:T(8,128)(2,1)}, u32[]{:S(2)}, u32[]{:S(2)}) collective-permute-start(bf16[256,2048]{1,0:T(8,128)(2,1)} %collective-permute-done.44), channel_id=1, source_target_pairs={{0,1},{1,0},{2,3},{3,2},{4,5},{5,4},{6,7},{7,6},{8,9},{9,8},{10,11... | collective-permute-start | bytes 3145736 | tf_op jit(solution)/shard_map/ppermute | solution.py:448
  575.3 60.6 %collective-permute-start.50 = (bf16[2048,256]{1,0:T(8,128)(2,1)}, bf16[2048,256]{1,0:T(8,128)(2,1)}, u32[]{:S(2)}, u32[]{:S(2)}) collective-permute-start(bf16[2048,256]{1,0:T(8,128)(2,1)} %get-tuple-element.415), channel_id=1, source_target_pairs={{0,16},{16,0},{1,17},{17,1},{2,18},{18,2},{3,19},{19,3},{4,20},{20... | collective-permute-start | bytes 3145736 | tf_op jit(solution)/shard_map/ppermute | solution.py:466
  576.8 63.5 %collective-permute-start.51 = (bf16[2048,256]{1,0:T(8,128)(2,1)}, bf16[2048,256]{1,0:T(8,128)(2,1)}, u32[]{:S(2)}, u32[]{:S(2)}) collective-permute-start(bf16[2048,256]{1,0:T(8,128)(2,1)} %get-tuple-element.416), channel_id=1, source_target_pairs={{0,16},{16,0},{1,17},{17,1},{2,18},{18,2},{3,19},{19,3},{4,20},{20... | collective-permute-start | bytes 3145736 | tf_op jit(solution)/shard_map/ppermute | solution.py:466
  577.4 62.9 %collective-permute-start.52 = (bf16[2048,256]{1,0:T(8,128)(2,1)S(1)}, bf16[2048,256]{1,0:T(8,128)(2,1)}, u32[]{:S(2)}, u32[]{:S(2)}) collective-permute-start(bf16[2048,256]{1,0:T(8,128)(2,1)S(1)} %add_convert_fusion.13), channel_id=1, source_target_pairs={{0,12},{1,13},{2,14},{3,15},{4,0},{5,1},{6,2},{7,3},{8,4},{9,5},{1... | collective-permute-start | bytes 3145736 | tf_op jit(solution)/shard_map/ppermute | solution.py:457
  648.5 51.9 %collective-permute-start.57 = (bf16[2048,256]{1,0:T(8,128)(2,1)}, bf16[2048,256]{1,0:T(8,128)(2,1)S(1)}, u32[]{:S(2)}, u32[]{:S(2)}) collective-permute-start(bf16[2048,256]{1,0:T(8,128)(2,1)} %get-tuple-element.435), channel_id=1, source_target_pairs={{0,16},{16,0},{1,17},{17,1},{2,18},{18,2},{3,19},{19,3},{4,20},{20... | collective-permute-start | bytes 3145736 | tf_op jit(solution)/shard_map/ppermute | solution.py:466
  649.2 51.3 %collective-permute-start.58 = (bf16[256,2048]{1,0:T(8,128)(2,1)}, bf16[256,2048]{1,0:T(8,128)(2,1)S(1)}, u32[]{:S(2)}, u32[]{:S(2)}) collective-permute-start(bf16[256,2048]{1,0:T(8,128)(2,1)} %reduce-scatter.3.cloned.1.call-done), channel_id=1, source_target_pairs={{0,16},{16,0},{1,17},{17,1},{2,18},{18,2},{3,19},{19,3},{4,20},{20... | collective-permute-start | bytes 3145736 | tf_op jit(solution)/shard_map/ppermute | solution.py:466
  655.5 45.0 %collective-permute-start.54 = (bf16[256,2048]{1,0:T(8,128)(2,1)}, bf16[256,2048]{1,0:T(8,128)(2,1)}, u32[]{:S(2)}, u32[]{:S(2)}) collective-permute-start(bf16[256,2048]{1,0:T(8,128)(2,1)} %get-tuple-element.551), channel_id=1, source_target_pairs={{0,2},{1,3},{2,0},{3,1},{4,6},{5,7},{6,4},{7,5},{8,10},{9,11},{10,... | collective-permute-start | bytes 3145736 | tf_op jit(solution)/shard_map/ppermute | solution.py:451
  657.2 43.3 %collective-permute-start.55 = (bf16[256,1024]{1,0:T(8,128)(2,1)}, bf16[256,1024]{1,0:T(8,128)(2,1)S(1)}, u32[]{:S(2)}, u32[]{:S(2)}) collective-permute-start(bf16[256,1024]{1,0:T(8,128)(2,1)} %reshape_squeeze.6), channel_id=1, source_target_pairs={{4,0},{5,1},{6,2},{7,3},{8,4},{9,5},{10,6},{11,7},{12,8},{13,9},{1... | collective-permute-start | bytes 1572872 | tf_op jit(solution)/shard_map/ppermute | solution.py:463
  658.5 42.0 %collective-permute-start.56 = (bf16[256,1024]{1,0:T(8,128)(2,1)}, bf16[256,1024]{1,0:T(8,128)(2,1)S(1)}, u32[]{:S(2)}, u32[]{:S(2)}) collective-permute-start(bf16[256,1024]{1,0:T(8,128)(2,1)} %reshape_squeeze.7), channel_id=1, source_target_pairs={{8,0},{9,1},{10,2},{11,3},{12,4},{13,5},{14,6},{15,7},{24,16},{25,... | collective-permute-start | bytes 1572872 | tf_op jit(solution)/shard_map/ppermute | solution.py:463
  700.5 51.1 %collective-permute-start.63 = (bf16[512,2048]{1,0:T(8,128)(2,1)}, bf16[512,2048]{1,0:T(8,128)(2,1)}, u32[]{:S(2)}, u32[]{:S(2)}) collective-permute-start(bf16[512,2048]{1,0:T(8,128)(2,1)} %get-tuple-element.454), channel_id=1, source_target_pairs={{0,1},{1,0},{2,3},{3,2},{4,5},{5,4},{6,7},{7,6},{8,9},{9,8},{10,11... | collective-permute-start | bytes 6291464 | tf_op jit(solution)/shard_map/ppermute | solution.py:448
  705.5 46.0 %collective-permute-start.59 = (bf16[256,2048]{1,0:T(8,128)(2,1)}, bf16[256,2048]{1,0:T(8,128)(2,1)}, u32[]{:S(2)}, u32[]{:S(2)}) collective-permute-start(bf16[256,2048]{1,0:T(8,128)(2,1)} %get-tuple-element.450), channel_id=1, source_target_pairs={{0,2},{1,3},{2,0},{3,1},{4,6},{5,7},{6,4},{7,5},{8,10},{9,11},{10,... | collective-permute-start | bytes 3145736 | tf_op jit(solution)/shard_map/ppermute | solution.py:451
  706.1 45.5 %collective-permute-start.62 = (bf16[2048,256]{1,0:T(8,128)(2,1)}, bf16[2048,256]{1,0:T(8,128)(2,1)}, u32[]{:S(2)}, u32[]{:S(2)}) collective-permute-start(bf16[2048,256]{1,0:T(8,128)(2,1)} %add_convert_fusion.9), channel_id=1, source_target_pairs={{0,12},{1,13},{2,14},{3,15},{4,0},{5,1},{6,2},{7,3},{8,4},{9,5},{1... | collective-permute-start | bytes 3145736 | tf_op jit(solution)/shard_map/ppermute | solution.py:457
  711.8 39.7 %collective-permute-start.60 = (bf16[1024,384]{1,0:T(8,128)(2,1)}, bf16[1024,384]{1,0:T(8,128)(2,1)}, u32[]{:S(2)}, u32[]{:S(2)}) collective-permute-start(bf16[1024,384]{1,0:T(8,128)(2,1)} %get-tuple-element.451), channel_id=1, source_target_pairs={{0,16},{16,0},{1,17},{17,1},{2,18},{18,2},{3,19},{19,3},{4,20},{20... | collective-permute-start | bytes 2359304 | tf_op jit(solution)/shard_map/ppermute | solution.py:466
  712.5 39.1 %collective-permute-start.61 = (bf16[1024,384]{1,0:T(8,128)(2,1)}, bf16[1024,384]{1,0:T(8,128)(2,1)}, u32[]{:S(2)}, u32[]{:S(2)}) collective-permute-start(bf16[1024,384]{1,0:T(8,128)(2,1)} %get-tuple-element.452), channel_id=1, source_target_pairs={{0,16},{16,0},{1,17},{17,1},{2,18},{18,2},{3,19},{19,3},{4,20},{20... | collective-permute-start | bytes 2359304 | tf_op jit(solution)/shard_map/ppermute | solution.py:466
  (171 other events, 2720.1 us)
Sparse Core Ops, SparseCore 0:
  486.4 160.9 reduce-scatter.2
  753.0 72.7 reduce-scatter.4

commit v3 on v2

--- a/solution.py
+++ b/solution.py
@@ -166,13 +166,14 @@
 
 
 def attend_back_kernel(first, count, info_ref, qkv_ref, mix_ref, grad_ref, log_ref, *rest):
-    out_ref, key_acc, value_acc = rest[-3:]
-    if len(rest) == 4:
-        before_ref = rest[0]
+    key_acc, value_acc = rest[-2:]
+    if len(rest) == 6:
+        before_ref, out_ref = rest[:2]
         key_acc[...] = before_ref[:, PAIR : 2 * PAIR].astype(F32)
         value_acc[...] = before_ref[:, 2 * PAIR : 3 * PAIR].astype(F32)
         out_ref[:, 0:PAIR] = before_ref[:, 0:PAIR]
     else:
+        out_ref = rest[0]
         key_acc[...] = jnp.zeros_like(key_acc)
         value_acc[...] = jnp.zeros_like(value_acc)
         out_ref[:, 0:PAIR] = jnp.zeros((out_ref.shape[0], PAIR), BF16)
@@ -239,6 +240,13 @@
     lax.fori_loop(first, first + count, segment, 0)
     out_ref[:, PAIR : 2 * PAIR] = key_acc[...].astype(BF16)
     out_ref[:, 2 * PAIR : 3 * PAIR] = value_acc[...].astype(BF16)
+    if len(rest) == 6:
+        for f in range(TEAM):
+            for k, far_ref in enumerate(rest[2:4]):
+                at = TEAM * SEG + (2 * f + k) * TAIL
+                here = slice(f * TAIL, (f + 1) * TAIL)
+                far_ref[here, :PAIR] = key_acc[at : at + TAIL, :].astype(BF16)
+                far_ref[here, PAIR:] = value_acc[at : at + TAIL, :].astype(BF16)
 
 
 def attend_back(info, qkv, mixture, grad, logs, first, count, before=None):
@@ -259,13 +267,14 @@
                 pl.BlockSpec((1, count, 2, SEG), lambda r, t: (r, 0, 0, 0)),
             ]
             + [wide] * len(more),
-            out_specs=wide,
+            out_specs=[wide] + [pl.BlockSpec((TEAM * TAIL, 2 * PAIR), lambda r, t: (0, r))] * (2 * len(more)),
             scratch_shapes=[
                 pltpu.VMEM((qkv.shape[0], PAIR), F32),
                 pltpu.VMEM((qkv.shape[0], PAIR), F32),
             ],
         ),
-        out_shape=jax.ShapeDtypeStruct(qkv.shape, BF16),
+        out_shape=[jax.ShapeDtypeStruct(qkv.shape, BF16)]
+        + [jax.ShapeDtypeStruct((TEAM * TAIL, pieces * 2 * PAIR), BF16)] * (2 * len(more)),
         compiler_params=pltpu.CompilerParams(vmem_limit_bytes=56 * 1024 * 1024),
         cost_estimate=LIGHT,
         name="attend_back",
@@ -332,6 +341,60 @@
     )
 
 
+def pack_kernel(plan, which_ref, *refs):
+    sources, out_ref, sems = refs[:-2], refs[-2], refs[-1]
+    copies = []
+    for n, (ref, (row, rows, column, columns, at_row, at_column)) in enumerate(zip(sources, plan)):
+        if at_row == "held":
+            at_row = pl.multiple_of(which_ref[0] * rows, rows)
+        elif at_row == "other":
+            at_row = pl.multiple_of((1 - which_ref[0]) * rows, rows)
+        copies.append(
+            pltpu.make_async_copy(
+                ref.at[pl.ds(row, rows), pl.ds(column, columns)],
+                out_ref.at[pl.ds(at_row, rows), pl.ds(at_column, columns)],
+                sems.at[n],
+            )
+        )
+    for copy in copies:
+        copy.start()
+    for copy in copies:
+        copy.wait()
+
+
+def pack(which, shape, parts):
+    return pl.pallas_call(
+        functools.partial(pack_kernel, [plan for _, plan in parts]),
+        grid_spec=pltpu.PrefetchScalarGridSpec(
+            num_scalar_prefetch=1,
+            grid=(),
+            in_specs=[pl.BlockSpec(memory_space=pl.ANY)] * len(parts),
+            out_specs=pl.BlockSpec(memory_space=pltpu.VMEM),
+            scratch_shapes=[pltpu.SemaphoreType.DMA((len(parts),))],
+        ),
+        out_shape=jax.ShapeDtypeStruct(shape, BF16),
+        compiler_params=pltpu.CompilerParams(vmem_limit_bytes=32 * 1024 * 1024),
+        cost_estimate=LIGHT,
+        name="pack",
+    )(which, *[v for v, _ in parts])
+
+
+def pack_rows(which, parts):
+    columns, row, plan = parts[0].shape[1], 0, []
+    for v in parts:
+        plan.append((v, (0, v.shape[0], 0, columns, row, 0)))
+        row += v.shape[0]
+    return pack(which, (row, columns), plan)
+
+
+def pack_columns(which, parts, rows):
+    column, plan = 0, []
+    for v in parts:
+        plan.append((v, (0, rows, 0, v.shape[1], 0, column)))
+        column += v.shape[1]
+    return pack(which, (rows, column), plan)
+
+
 def project_kernel(pieces, which_ref, *refs):
     weights, rows, out_ref, first, last = (
         refs[: 2 * pieces],
@@ -534,6 +597,8 @@
     def cat(*parts, axis=0):
         return jnp.concatenate(parts, axis=axis)
 
+    which = jnp.reshape(second, (1,)).astype(jnp.int32)
+
     qkv_local = cat(query_weight, key_weight, value_weight, output_weight.T, axis=1)
     qkv_bias_local = cat(
         query_bias, jnp.zeros_like(query_bias), value_bias, jnp.zeros_like(query_bias)
@@ -542,19 +607,17 @@
     q0_o = half(qkv_local, 0, 1 - second)
     hidden_in = inputs.astype(F32)
     normed = normalize(hidden_in, gain_first, shift_first).astype(BF16)
-    packed, normed = sync(packed, normed)
+    packed, normed, normed_tail = sync(packed, normed, normed[SEG - TAIL :])
     q1 = ring_up(packed)
     normed_xa = chip_swap(normed[:part])
     normed_c = core_swap(normed)
-    normed_tail, normed_b = normed[SEG - TAIL :], normed[part:]
-    q1, normed_xa, normed_c, normed_tail, normed_b = sync(
-        q1, normed_xa, normed_c, normed_tail, normed_b
-    )
+    early = line_up(normed_tail)
+    normed_b = normed[part:]
+    q1, normed_xa, normed_c, early, normed_b = sync(q1, normed_xa, normed_c, early, normed_b)
     q2 = ring_up(q1)
     normed_xb = chip_swap(normed_b)
     q1_o = group_swap(q1)
-    early = line_up(normed_tail)
-    earlier = line_up(normed_tail, 2)
+    earlier = line_up(early)
     q2, q1_o, normed_x, rest = sync(q2, q1_o, cat(normed_xa, normed_xb), cat(early, earlier))
     q3 = ring_up(q2)
     q2_o = group_swap(q2)
@@ -581,7 +644,6 @@
     e1 = ring_up(e0)
     cot_xa = chip_swap(cot_a)
     row_blocks = [normed, normed_c, normed_x, normed_xc, rest, rest_c, rest_x, rest_xc]
-    which = jnp.reshape(second, (1,)).astype(jnp.int32)
     qkv_a = project(which, [(packed, q0_o), (q1, q1_o), (q2, q2_o)], row_blocks)
     q3_o, cot_xa, qkv_a, e1, cot_b, cot = sync(q3_o, cot_xa, qkv_a, e1, cot_b, cotangent)
     e2 = ring_up(e1)
@@ -591,19 +653,26 @@
     mix_far_a, log_far_a = attend(info, qkv_a, 2, 2)
     qkv_b = project(which, [(q3, q3_o)], row_blocks)
     mix_far_b, log_far_b = attend(info, qkv_b, 2, 2)
-    held_pieces = ((packed, q0_o), (q1, q1_o[:tops]), (q2, q2_o[:tops]), (q3, q3_o[:tops]))
-    out_all = cat(*[ordered(v[:tops, block:], o[:, block:], 0) for v, o in held_pieces], axis=1)
-    mix_far = cat(mix_far_a, mix_far_b, axis=1)
+    held_pieces = ((packed, q0_o), (q1, q1_o), (q2, q2_o), (q3, q3_o))
+
+    def whole(pieces, column, columns):
+        plan = []
+        for n, (v, o) in enumerate(pieces):
+            plan.append((v, (0, tops, column, columns, "held", n * columns)))
+            plan.append((o, (0, tops, column, columns, "other", n * columns)))
+        return pack(which, (width, len(pieces) * columns), plan)
+
+    out_all = whole(held_pieces, block, cols)
+    mix_far = pack_columns(which, [mix_far_a, mix_far_b], near_rows)
     far, far_sent = matmul(mix_far, out_all, True, parts=2)
-    cot_x = cat(cot_xa, cot_xb)
+    cot_x = pack_rows(which, [cot_xa, cot_xb])
     e2, e1_o, cot_x, cot_c, qkv_a, qkv_b, far, far_sent, out_all, contract_weight = sync(
         e2, e1_o, cot_x, cot_c, qkv_a, qkv_b, far, far_sent, out_all, contract_weight
     )
-    cot_xc = core_swap(cot_x)
     far_c = core_swap(far_sent)
     contract_own = half(contract_weight, 0, second)
     contract_rest = half(contract_weight, 0, 1 - second)
-    far, far_c, qkv_a, cot_xc = sync(far, far_c, qkv_a, cot_xc)
+    far, far_c, qkv_a = sync(far, far_c, qkv_a)
     branch_in = add(far[part:], far_c[part:])
     branch_xa = chip_swap(add(far[:part], far_c[:part]))
     e3 = ring_up(e2)
@@ -613,13 +682,14 @@
         branch_xa, e3, e2_o, mix_near_a, branch_in, contract_own, qkv_b
     )
     branch_xb = chip_swap(branch_in)
+    cot_xc = core_swap(cot_x)
     k1 = ring_up(contract_own)
     e3_o = group_swap(e3)
     mix_near_b, log_near_b = attend(info, qkv_b, 0, 2)
-    mix_near = cat(mix_near_a, mix_near_b, axis=1)
+    mix_near = pack_columns(which, [mix_near_a, mix_near_b], near_rows)
     near, near_sent = matmul(mix_near, out_all, True, parts=2)
-    branch_xb, k1, e3_o, near, near_sent, mix_near = sync(
-        branch_xb, k1, e3_o, near, near_sent, mix_near
+    branch_xb, k1, e3_o, near, near_sent, mix_near, cot_xc = sync(
+        branch_xb, k1, e3_o, near, near_sent, mix_near, cot_xc
     )
     near_c = core_swap(near_sent)
     near, near_c, k1 = sync(near, near_c, k1)
@@ -633,15 +703,15 @@
     k2 = ring_up(k1)
     k1_o = group_swap(k1)
     expand_pairs = (e1, e1_o, e2, e2_o, e3, e3_o)
-    expand_all = cat(expand_own, expand_rest, *[v[:width] for v in expand_pairs], axis=1)
-    qkv_all = cat(
-        *[ordered(v[:tops, :block], o[:, :block], 0) for v, o in zip(held[0::2], held[1::2])], axis=1
-    )
+    expand_all = pack_columns(which, [expand_own, expand_rest, *expand_pairs], width)
+    held = tuple(zip(held[0::2], held[1::2]))
+    qkv_all = whole(held, 0, block)
+    key_value_all = whole(held, PAIR, 2 * PAIR)
     expand_bias_all = cat(
         expand_bias_own, expand_bias_rest, *[v[width] for v in expand_pairs]
     ).astype(F32)
-    two_xa, two_c, k2, k1_o, expand_all, expand_bias_all, normed_two, qkv_all = sync(
-        two_xa, two_c, k2, k1_o, expand_all, expand_bias_all, normed_two, qkv_all
+    two_xa, two_c, k2, k1_o, expand_all, expand_bias_all, normed_two, qkv_all, key_value_all = sync(
+        two_xa, two_c, k2, k1_o, expand_all, expand_bias_all, normed_two, qkv_all, key_value_all
     )
     two_xb = chip_swap(normed_two[part:])
     k3 = ring_up(k2)
@@ -652,7 +722,7 @@
         return value.astype(BF16), slope.astype(BF16)
 
     two_xac = core_swap(two_xa)
-    two_near = cat(normed_two, two_c)
+    two_near = pack_rows(which, [normed_two, two_c])
     active_near, slope_near = front(two_near)
     two_xb, k3, k2_o, active_near, slope_near, two_near, two_xac = sync(
         two_xb, k3, k2_o, active_near, slope_near, two_near, two_xac
@@ -660,17 +730,17 @@
     two_xbc = core_swap(two_xb)
     two_xbc, k3, qkv_a, qkv_b, cot_c = sync(two_xbc, k3, qkv_a, qkv_b, cot_c)
     k3_o = group_swap(k3)
-    two_far = cat(two_xa, two_xb, two_xac, two_xbc)
+    two_far = pack_rows(which, [two_xa, two_xb, two_xac, two_xbc])
     active_far, slope_far = front(two_far)
-    qkv = cat(qkv_a, qkv_b, axis=1)
+    qkv = pack_columns(which, [qkv_a, qkv_b], qkv_a.shape[0])
     k3_o, active_far, slope_far, two_far, cot_x = sync(k3_o, active_far, slope_far, two_far, cot_x)
-    contract_all = cat(contract_own, contract_rest, k1, k1_o, k2, k2_o, k3, k3_o)
-    cot_far = cat(cot_x, cot_xc)
+    contract_all = pack_rows(which, [contract_own, contract_rest, k1, k1_o, k2, k2_o, k3, k3_o])
+    cot_far = pack_rows(which, [cot_x, cot_xc])
     before_far = matmul(cot_far, contract_all, True, slope_far)
     far, far_sent = matmul(before_far, expand_all, True, parts=2)
     far, far_sent, before_far, contract_all = sync(far, far_sent, before_far, contract_all)
     far_c = core_swap(far_sent)
-    cot_near = cat(cot, cot_c)
+    cot_near = pack_rows(which, [cot, cot_c])
     far, far_c, cot_near, slope_near = sync(far, far_c, cot_near, slope_near)
     two_grad_in = add(far[part:], far_c[part:])
     two_grad_xa = chip_swap(add(far[:part], far_c[:part]))
@@ -714,10 +784,10 @@
     middle_xb = chip_swap(middle_low_b)
     middle_xac = core_swap(middle_xa)
     s3_o = group_swap(sent[3])
-    middle_near = cat(middle_low, middle_c)
+    middle_near = pack_rows(which, [middle_low, middle_c])
     mix_grad_near = matmul(middle_near, out_all, False)
     log_near = cat(log_near_a, log_near_b)
-    part_grad = attend_back(info, qkv, mix_near, mix_grad_near, log_near, 0, 2)
+    (part_grad,) = attend_back(info, qkv, mix_near, mix_grad_near, log_near, 0, 2)
     middle_xb, s3_o, part_grad, middle_near, active_far, middle_xac, *sent = sync(
         middle_xb, s3_o, part_grad, middle_near, active_far, middle_xac, *sent
     )
@@ -727,19 +797,23 @@
     s2_o = group_swap(sent[2])
     s1_o = group_swap(sent[1])
     a3 = ring_down(s3)
-    middle_far = cat(middle_xa, middle_xb, middle_xac, middle_xbc)
+    middle_far = pack_rows(which, [middle_xa, middle_xb, middle_xac, middle_xbc])
     mix_grad_far = matmul(middle_far, out_all, False)
     log_far = cat(log_far_a, log_far_b)
-    qkv_grad = attend_back(info, qkv, mix_far, mix_grad_far, log_far, 2, 2, part_grad)
+    qkv_grad, one, two = attend_back(
+        info, qkv, mix_far, mix_grad_far, log_far, 2, 2, part_grad
+    )
     far, far_sent = matmul(qkv_grad, qkv_all, True, place=1, rows=near_rows, parts=2)
-    far_rows = qkv_grad[team_rows:].reshape(TEAM, 2, TAIL, teams, 3, PAIR)[:, :, :, :, 1:]
-    one = far_rows[:, 0].reshape(span, -1)
-    two = far_rows[:, 1].reshape(span, -1)
-    s2_o, s1_o, a3, far, far_sent, qkv_grad, middle_far, contract_mine, one, two, sent0 = sync(
-        s2_o, s1_o, a3, far, far_sent, qkv_grad, middle_far, contract_mine, one, two, sent[0]
+    place_order = jnp.stack([(team + teams - r) % teams for r in range(teams)]).astype(jnp.int32)
+    (out_grad,) = weight_grad(
+        [(sync(mix_near, far)[0], middle_near, 0), (mix_far, middle_far, 0)], step=cols, target=place_order
+    )
+    s2_o, s1_o, a3, far, far_sent, qkv_grad, contract_mine, one, two, sent0, out_grad = sync(
+        s2_o, s1_o, a3, far, far_sent, qkv_grad, contract_mine, one, two, sent[0], out_grad
     )
     far_c = core_swap(far_sent)
-    far, far_c, qkv_grad, mix_near = sync(far, far_c, qkv_grad, mix_near)
+    far, far_c, qkv_grad, out_grad = sync(far, far_c, qkv_grad, out_grad)
+    out_mine = scatter_sum(out_grad)
     normed_in = add(far[part:], far_c[part:])
     normed_ga = chip_swap(add(far[:part], far_c[:part]))
     one = line_down(one)
@@ -751,17 +825,13 @@
     row_halves = jnp.where(second == 0, row_halves, (row_halves + 4) % 8)
     grad_pairs = [
         (v, qkv_grad, n)
-        for n, v in enumerate([normed, normed_c, normed_x, normed_xc, cat(rest, rest_c, rest_x, rest_xc)])
+        for n, v in enumerate([normed, normed_c, normed_x, normed_xc, pack_rows(which, [rest, rest_c, rest_x, rest_xc])])
     ]
     kept2, sent2, kept3, sent3 = weight_grad(
         grad_pairs, 1, 2 * block, splits=2, source=row_halves, halves=True, step=width // 8
     )
     near, near_sent = matmul(qkv_grad, qkv_all, True, place=0, rows=near_rows, parts=2)
     a3_s2 = add(a3, add(kept[2], s2_o))
-    place_order = jnp.stack([(team + teams - r) % teams for r in range(teams)]).astype(jnp.int32)
-    (out_grad,) = weight_grad(
-        [(mix_near, middle_near, 0), (mix_far, middle_far, 0)], step=cols, target=place_order
-    )
     (
         normed_ga,
         normed_in,
@@ -775,7 +845,6 @@
         qkv_grad,
         a3_s2,
         active_far,
-        out_grad,
         contract_other,
     ) = sync(
         normed_ga,
@@ -790,10 +859,8 @@
         qkv_grad,
         a3_s2,
         active_far,
-        out_grad,
         contract_other,
     )
-    out_mine = scatter_sum(out_grad)
     normed_gb = chip_swap(normed_in)
     q3_in = group_swap(sent3)
     q2_in = group_swap(sent2)
@@ -801,12 +868,21 @@
     near_c = core_swap(near_sent)
 
     def turn(v, by):
+        rows, columns = v.shape
         shift = (by % teams) * 2 * PAIR
-        return cat(v[:, shift:], v[:, :shift], axis=1) if shift else v
-
-    late = add(turn(one, 1), turn(two, 2)).reshape(span, teams, 2, PAIR)
-    late = jnp.pad(late, ((0, 0), (0, 0), (1, 0), (0, 0))).reshape(span, teams * block)
-    late_terms = matmul(late, qkv_all, True)
+        if not shift:
+            return v
+        return pack(
+            which,
+            v.shape,
+            [
+                (v, (0, rows, shift, columns - shift, 0, 0)),
+                (v, (0, rows, 0, shift, 0, columns - shift)),
+            ],
+        )
+
+    late = add(turn(one, 1), turn(two, 2))
+    late_terms = matmul(late, key_value_all, True)
     grad_pairs = [(v, qkv_grad, n) for v, _, n in grad_pairs]
     kept0, sent0, kept1, sent1 = weight_grad(
         grad_pairs, 0, 2 * block, splits=2, source=row_halves, halves=True, step=width // 8
@@ -824,6 +900,7 @@
         two_far_branch,
         two_far_sent,
         active_near,
+        out_mine,
     ) = sync(
         normed_gb,
         q3_in,
@@ -836,6 +913,7 @@
         two_far_branch,
         two_far_sent,
         active_near,
+        out_mine,
     )
     out_c = core_swap(two_far_sent)
     late_n = core_swap(late_terms[TAIL : 2 * TAIL])
@@ -898,17 +976,15 @@
     q0_in = group_swap(sent0)
     a1 = ring_down(a2_s1)
     qa3_sum = add(qa3, add(kept2, q2_in))
-    q0_in, a1, qa3_sum, active_near, out_mine, *shifts = sync(
-        q0_in, a1, qa3_sum, active_near, out_mine, *shifts
-    )
+    q0_in, a1, qa3_sum, active_near, *shifts = sync(q0_in, a1, qa3_sum, active_near, *shifts)
     vector = add_shifts(shifts, lambda i: mine ^ i)
     shifts = [vector] + [ring_up(vector, r) for r in range(1, teams)]
     qa2 = ring_down(qa3_sum)
     expand_mine = other_groups(add(a1, add(kept[0], s0_o)))
     expand_other = group_swap(expand_mine)
     two_near_branch, two_near_sent = matmul(active_near, contract_all, False, parts=2)
-    qa2, expand_other, two_near_branch, two_near_sent, branch_two_in, *shifts = sync(
-        qa2, expand_other, two_near_branch, two_near_sent, branch_two_in, *shifts
+    qa2, expand_other, two_near_branch, two_near_sent, branch_two_in, out_mine, *shifts = sync(
+        qa2, expand_other, two_near_branch, two_near_sent, branch_two_in, out_mine, *shifts
     )
     vector = add_shifts(shifts, lambda i: (team + teams - i) % teams)
     bit = 1

time: 935 us -> 903 us (0.966)
  local copies, waits for them, and re-layouts: 121 us -> 81.7 us
  other arithmetic: 109 us -> 86.9 us
  Pallas kernels: 358 us -> 379 us
  waiting for transfers between devices: 202 us -> 212 us
    slice x32 -> x2, local copies, waits for them, and re-layouts: 25.7 us -> 0.19 us  [the longest x1 0.18 us: body(): normed_b = normed[part:]]
    ppermute x2, waiting for transfers between devices: 25.7 us -> 48.1 us  [line_up(): lax.ppermute(v, 'mp', [(i, i + by * TEAM) for i in range(n_mp - by * TEAM)])]
    pallas_call x0 -> x18, Pallas kernels: none -> 21.7 us  [pack(): pl.pallas_call(functools.partial(pack_kernel, [plan for _, plan in parts]...]
    ppermute x19, waiting for transfers between devices: 63.7 us -> 42 us  [chip_swap(): return lax.ppermute(v, 'mp', [(i, i ^ 2) for i in range(n_mp)])]
    ppermute x2, waiting for transfers between devices: 0.01 us -> 18 us  [line_down(): lax.ppermute(v, 'mp', [(i + by * TEAM, i) for i in range(n_mp - by * TEAM)])]
    ppermute x6, waiting for transfers between devices: 22.1 us -> 7.35 us  [ring_down(): return lax.ppermute(v, 'mp', [(i, (i - TEAM) % n_mp) for i in range(n_mp)])]
    reduce_scatter x2, waiting for transfers between devices: 18.4 us -> 6.77 us  [scatter_sum(): lax.psum_scatter(v, ('dp', 'mp'), scatter_dimension=0, axis_index_groups=...]
    concatenate x13 -> x2, local copies, waits for them, and re-layouts: 11.2 us -> 0.23 us  [cat(): return jnp.concatenate(parts, axis=axis)]
  transfers between devices with their start and end apart: 89 -> 89, of which waited for: 28 -> 38; matrix products, arithmetic and copies ran while one was open for 24% -> 13% of each run, Pallas kernels for 36% -> 39%
where the time goes in v3:
time: 903 us; the launch traced here: 896 us
  Pallas kernels  379 us (42%)
  waiting for transfers between devices  212 us (23%)
  starting transfers between devices  88.2 us (10%)
  other arithmetic  86.9 us (10%)
  local copies, waits for them, and re-layouts  81.7 us (9%)
  matrix products  31.7 us (4%)
  between operations  16.2 us (2%)
    pallas_call x13, Pallas kernels, matmul(): pl.pallas_call(functools.partial(matmul_kernel, transposed, parts), grid=...  131 us
    pallas_call x5, Pallas kernels, weight_grad(): pl.pallas_call(functools.partial(weight_grad_kernel, splits, halves, len(...  91.6 us
    unnamed x276, local copies, waits for them, and re-layouts  57.9 us
    ppermute x22, waiting for transfers between devices, group_swap(): return lax.ppermute(v, 'dp', [(i, i ^ bit) for i in range(n_dp)])  54.3 us
    pallas_call x2, Pallas kernels, attend_back(): pl.pallas_call(functools.partial(attend_back_kernel, first, count), grid_...  52.5 us
    ppermute x2, waiting for transfers between devices, line_up(): lax.ppermute(v, 'mp', [(i, i + by * TEAM) for i in range(n_mp - by * TEAM)])  48.1 us
    pallas_call x4, Pallas kernels, attend(): pl.pallas_call(functools.partial(attend_kernel, first, count), grid_spec=...  48 us
    ppermute x19, waiting for transfers between devices, chip_swap(): return lax.ppermute(v, 'mp', [(i, i ^ 2) for i in range(n_mp)])  42 us
  transfers between devices with their start and end apart: 89, of which 38 were waited for; matrix products, arithmetic and copies ran while one was open for 13% of the time, Pallas kernels for 39%

profile of v3, /device:TPU:0, one launch (start us, length us, event | category | flops | bytes accessed | tf_op | source)
XLA Modules:
  0.0 896.1 jit_solution(13544961212429894612)
XLA Ops:
  26.9 23.8 %collective-permute-done.3 = bf16[64,2048]{1,0:T(8,128)(2,1)S(1)} collective-permute-done((bf16[64,2048]{1,0:T(8,128)(2,1)S(1)}, bf16[64,2048]{1,0:T(8,128)(2,1)S(1)}, u32[]{:S(2)}, u32[]{:S(2)}) %collective-permute-start.3) | collective-permute-done | bytes 262176 | tf_op jit(solution)/shard_map/ppermute | solution.py:523
  59.8 24.3 %collective-permute-done.7 = bf16[64,2048]{1,0:T(8,128)(2,1)S(1)} collective-permute-done((bf16[64,2048]{1,0:T(8,128)(2,1)S(1)}, bf16[64,2048]{1,0:T(8,128)(2,1)S(1)}, u32[]{:S(2)}, u32[]{:S(2)}) %collective-permute-start.7) | collective-permute-done | bytes 262176 | tf_op jit(solution)/shard_map/ppermute | solution.py:523
  108.5 11.6 %collective-permute-done.11.refs_12_.refs_8_.refs_2_ = bf16[128,2048]{1,0:T(8,128)(2,1)S(1)} collective-permute-done((bf16[128,2048]{1,0:T(8,128)(2,1)S(1)}, bf16[128,2048]{1,0:T(8,128)(2,1)S(1)}, u32[]{:S(2)}, u32[]{:S(2)}) %collective-permute-start.11) | collective-permute-done | bytes 524320 | tf_op jit(solution)/shard_map/ppermute | solution.py:514
  125.6 22.5 %project.2.qkv_ref.refs_0_ = bf16[2560,1152]{1,0:T(8,128)(2,1)} custom-call(s32[1]{0:T(128)} %bitcast.1.which_ref, bf16[1040,512]{1,0:T(8,128)(2,1)} %copy-done.12, bf16[1024,512]{1,0:T(8,128)(2,1)} %get-tuple-element.344.refs_1_, bf16[1040,512]{1,0:T(8,128)(2,1)} %copy-done.17, bf16[1040,512]{1,0:T(8,128)(2,1)} %copy-done.20, bf16[1040,512]{1,0:T(8,128)(2,1)} %copy-done.23, ...), custom_call_target="tpu_custom_call" | custom-call | flops 1024 | bytes 1024 | tf_op jit(solution)/shard_map/project/pallas_call | solution.py:431
  153.8 11.7 %project.3.qkv_ref.refs_1_ = bf16[2560,384]{1,0:T(8,128)(2,1)} custom-call(s32[1]{0:T(128)} %bitcast.1.which_ref, bf16[1040,512]{1,0:T(8,128)(2,1)} %copy-done.31, bf16[1040,512]{1,0:T(8,128)(2,1)} %copy-done.35, bf16[512,2048]{1,0:T(8,128)(2,1)} %copy-done.70, bf16[512,2048]{1,0:T(8,128)(2,1)} %copy-done.75, ...), custom_call_target="tpu_custom_call" | custom-call | flops 1024 | bytes 1024 | tf_op jit(solution)/shard_map/project/pallas_call | solution.py:431
  178.5 16.7 %attend.4 = (bf16[1024,384]{1,0:T(8,128)(2,1)}, f32[3,2,2,512]{3,2,1,0:T(2,128)}) custom-call(s32[18]{0:T(128)} %compare_select_fusion.3.info_ref, bf16[2560,1152]{1,0:T(8,128)(2,1)} %project.2.qkv_ref.refs_0_), custom_call_target="tpu_custom_call" | custom-call | flops 1024 | bytes 1024 | tf_op jit(solution)/shard_map/attend/pallas_call | solution.py:147
  213.4 16.5 %attend.6 = (bf16[1024,384]{1,0:T(8,128)(2,1)}, f32[3,2,2,512]{3,2,1,0:T(2,128)}) custom-call(s32[18]{0:T(128)} %compare_select_fusion.3.info_ref, bf16[2560,1152]{1,0:T(8,128)(2,1)} %project.2.qkv_ref.refs_0_), custom_call_target="tpu_custom_call" | custom-call | flops 1024 | bytes 1024 | tf_op jit(solution)/shard_map/attend/pallas_call | solution.py:147
  316.9 15.8 %fusion.6 = (bf16[1024,2048]{1,0:T(8,128)(2,1)}, bf16[1024,2048]{1,0:T(8,128)(2,1)}) fusion(f32[2048]{0:T(1024)S(1)} %convert_element_type.352, bf16[1024,2048]{1,0:T(8,128)(2,1)S(1)} %pack.25.refs_0_, bf16[2048,2048]{1,0:T(8,128)(2,1)S(1)} %copy-done.2), kind=kOutput, calls=%fused_computation.11 | convolution fusion | flops 8633974784 | bytes 20979712 | tf_op jit(solution)/shard_map/dot_general | solution.py:48
  341.5 15.9 %fusion.13 = (bf16[1024,2048]{1,0:T(8,128)(2,1)}, bf16[1024,2048]{1,0:T(8,128)(2,1)}) fusion(f32[2048]{0:T(1024)S(1)} %convert_element_type.352, bf16[1024,2048]{1,0:T(8,128)(2,1)S(1)} %pack.26.refs_2_, bf16[2048,2048]{1,0:T(8,128)(2,1)S(1)} %copy-done.2), kind=kOutput, calls=%fused_computation.18 | convolution fusion | flops 8633974784 | bytes 20979712 | tf_op jit(solution)/shard_map/dot_general | solution.py:48
  374.3 14.4 %matmul.15.left_ref.refs_3_ = bf16[1024,2048]{1,0:T(8,128)(2,1)} custom-call(bf16[1024,2048]{1,0:T(8,128)(2,1)} %copy-done.6, bf16[2048,2048]{1,0:T(8,128)(2,1)} %copy-done, bf16[1024,2048]{1,0:T(8,128)(2,1)} %get-tuple-element.368.rest_0_), custom_call_target="tpu_custom_call" | custom-call | flops 1024 | bytes 1024 | tf_op jit(solution)/shard_map/matmul/pallas_call | solution.py:470
  388.6 13.3 %matmul.16 = (bf16[512,2048]{1,0:T(8,128)(2,1)}, bf16[512,2048]{1,0:T(8,128)(2,1)}) custom-call(bf16[1024,2048]{1,0:T(8,128)(2,1)} %matmul.15.left_ref.refs_3_, bf16[2048,2048]{1,0:T(8,128)(2,1)} %copy-done.1), custom_call_target="tpu_custom_call" | custom-call | flops 1024 | bytes 1024 | tf_op jit(solution)/shard_map/matmul/pallas_call | solution.py:470
  408.7 14.3 %matmul.17.left_ref.refs_1_ = bf16[1024,2048]{1,0:T(8,128)(2,1)} custom-call(bf16[1024,2048]{1,0:T(8,128)(2,1)} %copy-done.7, bf16[2048,2048]{1,0:T(8,128)(2,1)} %copy-done, bf16[1024,2048]{1,0:T(8,128)(2,1)} %get-tuple-element.379.rest_0_), custom_call_target="tpu_custom_call" | custom-call | flops 1024 | bytes 1024 | tf_op jit(solution)/shard_map/matmul/pallas_call | solution.py:470
  423.0 13.1 %matmul.18 = (bf16[512,2048]{1,0:T(8,128)(2,1)}, bf16[512,2048]{1,0:T(8,128)(2,1)}) custom-call(bf16[1024,2048]{1,0:T(8,128)(2,1)} %matmul.17.left_ref.refs_1_, bf16[2048,2048]{1,0:T(8,128)(2,1)} %copy-done.1), custom_call_target="tpu_custom_call" | custom-call | flops 1024 | bytes 1024 | tf_op jit(solution)/shard_map/matmul/pallas_call | solution.py:470
  438.9 24.7 %weight_grad.5 = bf16[2048,2048]{1,0:T(8,128)(2,1)} custom-call(s32[8]{0:T(128)} %iota.33.source_ref, s32[8]{0:T(128)} %stack.80.target_ref, bf16[1024,2048]{1,0:T(8,128)(2,1)} %get-tuple-element.509.refs_0_.left_ref, bf16[1024,2048]{1,0:T(8,128)(2,1)} %copy-done.7, bf16[1024,2048]{1,0:T(8,128)(2,1)} %get-tuple-element.471.refs_2_.left_ref, ...), custom_call_target="tpu_custom_call" | custom-call | flops 1024 | bytes 1024 | tf_op jit(solution)/shard_map/weight_grad/pallas_call | solution.py:328
  481.1 25.3 %weight_grad.6 = (bf16[2048,256]{1,0:T(8,128)(2,1)}, bf16[2048,256]{1,0:T(8,128)(2,1)}, bf16[2048,256]{1,0:T(8,128)(2,1)}, bf16[2048,256]{1,0:T(8,128)(2,1)}, bf...) custom-call(s32[8]{0:T(128)} %iota.34.source_ref.target_ref, ...), custom_call_target="tpu_custom_call" | custom-call | flops 1024 | bytes 1024 | tf_op jit(solution)/shard_map/weight_grad/pallas_call | solution.py:328
  523.5 25.9 %attend_back.2.rest_0_ = bf16[2560,1536]{1,0:T(8,128)(2,1)} custom-call(s32[18]{0:T(128)} %compare_select_fusion.3.info_ref, bf16[2560,1536]{1,0:T(8,128)(2,1)} %copy-done.3, bf16[1024,512]{1,0:T(8,128)(2,1)} %copy-done.39, bf16[1024,512]{1,0:T(8,128)(2,1)} %matmul.19.grad_ref, f32[4,2,2,512]{3,2,1,0:T(2,128)} %pad_maximum_fusion.7.log_ref), custom_call_target="tpu_custom_call" | custom-call | flops 1024 | bytes 1024 | tf_op jit(solution)/shard_map/attend_back/pallas_call | solution.py:258
  569.4 26.6 %attend_back.3 = (bf16[2560,1536]{1,0:T(8,128)(2,1)}, bf16[256,1024]{1,0:T(8,128)(2,1)}, bf16[256,1024]{1,0:T(8,128)(2,1)}) custom-call(s32[18]{0:T(128)} %compare_select_fusion.3.info_ref, bf16[2560,1536]{1,0:T(8,128)(2,1)} %copy-done.3, bf16[1024,512]{1,0:T(8,128)(2,1)} %copy-done.38, bf16[1024,512]{1,0:T(8,128)(2,1)} %matmul.20.grad_ref, ...), custom_call_target="tpu_custom_call" | custom-call | flops 1024 | bytes 1024 | tf_op jit(solution)/shard_map/attend_back/pallas_call | solution.py:258
  658.7 15.4 %weight_grad.8 = (bf16[1024,384]{1,0:T(8,128)(2,1)}, bf16[1024,384]{1,0:T(8,128)(2,1)}, bf16[1024,384]{1,0:T(8,128)(2,1)}, bf16[1024,384]{1,0:T(8,128)(2,1)}) custom-call(s32[8]{0:T(128)} %broadcast_select_fusion.source_ref, s32[8]{0:T(128)} %iota.38.target_ref, bf16[512,2048]{1,0:T(8,128)(2,1)} %copy-done.70, ...), custom_call_target="tpu_custom_call" | custom-call | flops 1024 | bytes 1024 | tf_op jit(solution)/shard_map/weight_grad/pallas_call | solution.py:328
  674.1 18.0 %collective-permute-done.56.refs_0_.refs_1_ = bf16[256,1024]{1,0:T(8,128)(2,1)S(1)} collective-permute-done((bf16[256,1024]{1,0:T(8,128)(2,1)S(1)}, bf16[256,1024]{1,0:T(8,128)(2,1)S(1)}, u32[]{:S(2)}, u32[]{:S(2)}) %collective-permute-start.56) | collective-permute-done | bytes 524320 | tf_op jit(solution)/shard_map/ppermute | solution.py:526
  699.6 13.1 %matmul.24 = (bf16[512,2048]{1,0:T(8,128)(2,1)}, bf16[512,2048]{1,0:T(8,128)(2,1)}) custom-call(bf16[1024,2048]{1,0:T(8,128)(2,1)} %get-tuple-element.471.refs_2_.left_ref, bf16[2048,2048]{1,0:T(8,128)(2,1)} %copy-done), custom_call_target="tpu_custom_call" | custom-call | flops 1024 | bytes 1024 | tf_op jit(solution)/shard_map/matmul/pallas_call | solution.py:470
  713.2 15.6 %weight_grad.9 = (bf16[1024,384]{1,0:T(8,128)(2,1)}, bf16[1024,384]{1,0:T(8,128)(2,1)}, bf16[1024,384]{1,0:T(8,128)(2,1)}, bf16[1024,384]{1,0:T(8,128)(2,1)}) custom-call(s32[8]{0:T(128)} %broadcast_select_fusion.source_ref, s32[8]{0:T(128)} %iota.39.target_ref, bf16[512,2048]{1,0:T(8,128)(2,1)} %copy-done.70, ...), custom_call_target="tpu_custom_call" | custom-call | flops 1024 | bytes 1024 | tf_op jit(solution)/shard_map/weight_grad/pallas_call | solution.py:328
  768.9 16.3 %collective-permute-done.68 = bf16[1024,384]{1,0:T(8,128)(2,1)S(1)} collective-permute-done((bf16[1024,384]{1,0:T(8,128)(2,1)S(1)}, bf16[1024,384]{1,0:T(8,128)(2,1)S(1)}, u32[]{:S(2)}, u32[]{:S(2)}) %collective-permute-start.68) | collective-permute-done | bytes 786464 | tf_op jit(solution)/shard_map/ppermute | solution.py:529
  826.2 13.2 %matmul.25 = (bf16[512,2048]{1,0:T(8,128)(2,1)}, bf16[512,2048]{1,0:T(8,128)(2,1)}) custom-call(bf16[1024,2048]{1,0:T(8,128)(2,1)} %get-tuple-element.509.refs_0_.left_ref, bf16[2048,2048]{1,0:T(8,128)(2,1)} %copy-done), custom_call_target="tpu_custom_call" | custom-call | flops 1024 | bytes 1024 | tf_op jit(solution)/shard_map/matmul/pallas_call | solution.py:470
  874.3 12.5 %collective-permute-done.86 = bf16[1024,384]{1,0:T(8,128)(2,1)S(1)} collective-permute-done((bf16[1024,384]{1,0:T(8,128)(2,1)S(1)}, bf16[1024,384]{1,0:T(8,128)(2,1)S(1)}, u32[]{:S(2)}, u32[]{:S(2)}) %collective-permute-start.86) | collective-permute-done | bytes 786464 | tf_op jit(solution)/shard_map/ppermute | solution.py:529
  (587 shorter events, 459.4 us)
Async XLA Ops:
  7.2 618.2 %reduce-scatter.3.cloned.1.call-start = ((), (), s32[]{:S(2)}) async-start(), calls=%async_computation.2 | async-start | bytes 9437184 | tf_op jit(solution)/shard_map/reduce_scatter | solution.py:593
  50.7 34.3 %collective-permute-start.6 = (bf16[256,2048]{1,0:T(8,128)(2,1)S(1)}, bf16[256,2048]{1,0:T(8,128)(2,1)S(1)}, u32[]{:S(2)}, u32[]{:S(2)}) collective-permute-start(bf16[256,2048]{1,0:T(8,128)(2,1)S(1)} %get-tuple-element.283), channel_id=1, source_target_pairs={{0,2},{1,3},{2,0},{3,1},{4,6},{5,7},{6,4},{7,5},{8,10},{9,11},{10,... | collective-permute-start | bytes 3145736 | tf_op jit(solution)/shard_map/ppermute | solution.py:514
  52.3 34.4 %collective-permute-start.5 = (bf16[1040,512]{1,0:T(8,128)(2,1)S(1)}, bf16[1040,512]{1,0:T(8,128)(2,1)S(1)}, u32[]{:S(2)}, u32[]{:S(2)}) collective-permute-start(bf16[1040,512]{1,0:T(8,128)(2,1)S(1)} %collective-permute-done.refs_2_), channel_id=1, source_target_pairs={{0,16},{16,0},{1,17},{17,1},{2,18},{18,2},{3,19},{19,3},{4,20},{20... | collective-permute-start | bytes 3194888 | tf_op jit(solution)/shard_map/ppermute | solution.py:529
  150.1 54.8 %collective-permute-start.20 = (bf16[512,2048]{1,0:T(8,128)(2,1)S(1)}, bf16[512,2048]{1,0:T(8,128)(2,1)}, u32[]{:S(2)}, u32[]{:S(2)}) collective-permute-start(bf16[512,2048]{1,0:T(8,128)(2,1)S(1)} %copy-done.10), channel_id=1, source_target_pairs={{0,1},{1,0},{2,3},{3,2},{4,5},{5,4},{6,7},{7,6},{8,9},{9,8},{10,11... | collective-permute-start | bytes 6291464 | tf_op jit(solution)/shard_map/ppermute | solution.py:511
  150.1 54.8 %collective-permute-start.18 = (bf16[2064,256]{1,0:T(8,128)(2,1)}, bf16[2064,256]{1,0:T(8,128)(2,1)}, u32[]{:S(2)}, u32[]{:S(2)}) collective-permute-start(bf16[2064,256]{1,0:T(8,128)(2,1)} %collective-permute-done.16.refs_2_), channel_id=1, source_target_pairs={{0,16},{16,0},{1,17},{17,1},{2,18},{18,2},{3,19},{19,3},{4,20},{20... | collective-permute-start | bytes 3170312 | tf_op jit(solution)/shard_map/ppermute | solution.py:529
  150.6 54.3 %collective-permute-start.17 = (bf16[2064,256]{1,0:T(8,128)(2,1)}, bf16[2064,256]{1,0:T(8,128)(2,1)}, u32[]{:S(2)}, u32[]{:S(2)}) collective-permute-start(bf16[2064,256]{1,0:T(8,128)(2,1)} %collective-permute-done.16.refs_2_), channel_id=1, source_target_pairs={{0,4},{1,5},{2,6},{3,7},{4,8},{5,9},{6,10},{7,11},{8,12},{9,13},{1... | collective-permute-start | bytes 3170312 | tf_op jit(solution)/shard_map/ppermute | solution.py:517
  151.5 51.6 %collective-permute-start.19 = (bf16[256,2048]{1,0:T(8,128)(2,1)}, bf16[256,2048]{1,0:T(8,128)(2,1)}, u32[]{:S(2)}, u32[]{:S(2)}) collective-permute-start(bf16[256,2048]{1,0:T(8,128)(2,1)} %get-tuple-element.301), channel_id=1, source_target_pairs={{0,2},{1,3},{2,0},{3,1},{4,6},{5,7},{6,4},{7,5},{8,10},{9,11},{10,... | collective-permute-start | bytes 3145736 | tf_op jit(solution)/shard_map/ppermute | solution.py:514
  212.2 43.9 %collective-permute-start.28 = (bf16[512,2048]{1,0:T(8,128)(2,1)S(1)}, bf16[512,2048]{1,0:T(8,128)(2,1)}, u32[]{:S(2)}, u32[]{:S(2)}) collective-permute-start(bf16[512,2048]{1,0:T(8,128)(2,1)S(1)} %pack.18.refs_0_), channel_id=1, source_target_pairs={{0,1},{1,0},{2,3},{3,2},{4,5},{5,4},{6,7},{7,6},{8,9},{9,8},{10,11... | collective-permute-start | bytes 6291464 | tf_op jit(solution)/shard_map/ppermute | solution.py:511
  463.6 271.3 %reduce-scatter.5.cloned.1.call-start = ((), (), s32[]{:S(2)}) async-start(), calls=%async_computation.3 | async-start | bytes 2359296 | tf_op jit(solution)/shard_map/reduce_scatter | solution.py:593
  506.4 43.0 %collective-permute-start.46 = (bf16[256,2048]{1,0:T(8,128)(2,1)}, bf16[256,2048]{1,0:T(8,128)(2,1)}, u32[]{:S(2)}, u32[]{:S(2)}) collective-permute-start(bf16[256,2048]{1,0:T(8,128)(2,1)} %get-tuple-element.402), channel_id=1, source_target_pairs={{0,2},{1,3},{2,0},{3,1},{4,6},{5,7},{6,4},{7,5},{8,10},{9,11},{10,... | collective-permute-start | bytes 3145736 | tf_op jit(solution)/shard_map/ppermute | solution.py:514
  508.3 41.1 %collective-permute-start.47 = (bf16[2048,256]{1,0:T(8,128)(2,1)}, bf16[2048,256]{1,0:T(8,128)(2,1)}, u32[]{:S(2)}, u32[]{:S(2)}) collective-permute-start(bf16[2048,256]{1,0:T(8,128)(2,1)} %get-tuple-element.403), channel_id=1, source_target_pairs={{0,16},{16,0},{1,17},{17,1},{2,18},{18,2},{3,19},{19,3},{4,20},{20... | collective-permute-start | bytes 3145736 | tf_op jit(solution)/shard_map/ppermute | solution.py:529
  508.5 41.0 %collective-permute-start.48 = (bf16[256,2048]{1,0:T(8,128)(2,1)}, bf16[256,2048]{1,0:T(8,128)(2,1)}, u32[]{:S(2)}, u32[]{:S(2)}) collective-permute-start(bf16[256,2048]{1,0:T(8,128)(2,1)} %collective-permute-done.44.refs_0_), channel_id=1, source_target_pairs={{0,1},{1,0},{2,3},{3,2},{4,5},{5,4},{6,7},{7,6},{8,9},{9,8},{10,11... | collective-permute-start | bytes 3145736 | tf_op jit(solution)/shard_map/ppermute | solution.py:511
  552.5 65.2 %collective-permute-start.50 = (bf16[2048,256]{1,0:T(8,128)(2,1)}, bf16[2048,256]{1,0:T(8,128)(2,1)}, u32[]{:S(2)}, u32[]{:S(2)}) collective-permute-start(bf16[2048,256]{1,0:T(8,128)(2,1)} %get-tuple-element.422), channel_id=1, source_target_pairs={{0,16},{16,0},{1,17},{17,1},{2,18},{18,2},{3,19},{19,3},{4,20},{20... | collective-permute-start | bytes 3145736 | tf_op jit(solution)/shard_map/ppermute | solution.py:529
  554.5 64.2 %collective-permute-start.51 = (bf16[2048,256]{1,0:T(8,128)(2,1)}, bf16[2048,256]{1,0:T(8,128)(2,1)}, u32[]{:S(2)}, u32[]{:S(2)}) collective-permute-start(bf16[2048,256]{1,0:T(8,128)(2,1)} %get-tuple-element.423), channel_id=1, source_target_pairs={{0,16},{16,0},{1,17},{17,1},{2,18},{18,2},{3,19},{19,3},{4,20},{20... | collective-permute-start | bytes 3145736 | tf_op jit(solution)/shard_map/ppermute | solution.py:529
  554.6 64.1 %collective-permute-start.52 = (bf16[2048,256]{1,0:T(8,128)(2,1)S(1)}, bf16[2048,256]{1,0:T(8,128)(2,1)}, u32[]{:S(2)}, u32[]{:S(2)}) collective-permute-start(bf16[2048,256]{1,0:T(8,128)(2,1)S(1)} %add_convert_fusion.13), channel_id=1, source_target_pairs={{0,12},{1,13},{2,14},{3,15},{4,0},{5,1},{6,2},{7,3},{8,4},{9,5},{1... | collective-permute-start | bytes 3145736 | tf_op jit(solution)/shard_map/ppermute | solution.py:520
  630.0 62.2 %collective-permute-start.57 = (bf16[2048,256]{1,0:T(8,128)(2,1)}, bf16[2048,256]{1,0:T(8,128)(2,1)}, u32[]{:S(2)}, u32[]{:S(2)}) collective-permute-start(bf16[2048,256]{1,0:T(8,128)(2,1)} %get-tuple-element.448), channel_id=1, source_target_pairs={{0,16},{16,0},{1,17},{17,1},{2,18},{18,2},{3,19},{19,3},{4,20},{20... | collective-permute-start | bytes 3145736 | tf_op jit(solution)/shard_map/ppermute | solution.py:529
  630.6 61.6 %collective-permute-start.58 = (bf16[256,2048]{1,0:T(8,128)(2,1)}, bf16[256,2048]{1,0:T(8,128)(2,1)}, u32[]{:S(2)}, u32[]{:S(2)}) collective-permute-start(bf16[256,2048]{1,0:T(8,128)(2,1)} %reduce-scatter.3.cloned.1.call-done), channel_id=1, source_target_pairs={{0,16},{16,0},{1,17},{17,1},{2,18},{18,2},{3,19},{19,3},{4,20},{20... | collective-permute-start | bytes 3145736 | tf_op jit(solution)/shard_map/ppermute | solution.py:529
  636.5 55.7 %collective-permute-start.54 = (bf16[256,2048]{1,0:T(8,128)(2,1)}, bf16[256,2048]{1,0:T(8,128)(2,1)}, u32[]{:S(2)}, u32[]{:S(2)}) collective-permute-start(bf16[256,2048]{1,0:T(8,128)(2,1)} %get-tuple-element.561), channel_id=1, source_target_pairs={{0,2},{1,3},{2,0},{3,1},{4,6},{5,7},{6,4},{7,5},{8,10},{9,11},{10,... | collective-permute-start | bytes 3145736 | tf_op jit(solution)/shard_map/ppermute | solution.py:514
  643.4 48.8 %collective-permute-start.56 = (bf16[256,1024]{1,0:T(8,128)(2,1)S(1)}, bf16[256,1024]{1,0:T(8,128)(2,1)S(1)}, u32[]{:S(2)}, u32[]{:S(2)}) collective-permute-start(bf16[256,1024]{1,0:T(8,128)(2,1)S(1)} %copy-done.126), channel_id=1, source_target_pairs={{8,0},{9,1},{10,2},{11,3},{12,4},{13,5},{14,6},{15,7},{24,16},{25,... | collective-permute-start | bytes 1572872 | tf_op jit(solution)/shard_map/ppermute | solution.py:526
  692.2 42.7 %collective-permute-start.63 = (bf16[512,2048]{1,0:T(8,128)(2,1)}, bf16[512,2048]{1,0:T(8,128)(2,1)}, u32[]{:S(2)}, u32[]{:S(2)}) collective-permute-start(bf16[512,2048]{1,0:T(8,128)(2,1)} %get-tuple-element.464), channel_id=1, source_target_pairs={{0,1},{1,0},{2,3},{3,2},{4,5},{5,4},{6,7},{7,6},{8,9},{9,8},{10,11... | collective-permute-start | bytes 6291464 | tf_op jit(solution)/shard_map/ppermute | solution.py:511
  692.3 42.6 %collective-permute-start.59 = (bf16[256,2048]{1,0:T(8,128)(2,1)}, bf16[256,2048]{1,0:T(8,128)(2,1)}, u32[]{:S(2)}, u32[]{:S(2)}) collective-permute-start(bf16[256,2048]{1,0:T(8,128)(2,1)} %get-tuple-element.460), channel_id=1, source_target_pairs={{0,2},{1,3},{2,0},{3,1},{4,6},{5,7},{6,4},{7,5},{8,10},{9,11},{10,... | collective-permute-start | bytes 3145736 | tf_op jit(solution)/shard_map/ppermute | solution.py:514
  693.5 41.4 %collective-permute-start.62 = (bf16[2048,256]{1,0:T(8,128)(2,1)}, bf16[2048,256]{1,0:T(8,128)(2,1)}, u32[]{:S(2)}, u32[]{:S(2)}) collective-permute-start(bf16[2048,256]{1,0:T(8,128)(2,1)} %add_convert_fusion.9), channel_id=1, source_target_pairs={{0,12},{1,13},{2,14},{3,15},{4,0},{5,1},{6,2},{7,3},{8,4},{9,5},{1... | collective-permute-start | bytes 3145736 | tf_op jit(solution)/shard_map/ppermute | solution.py:520
  696.7 38.2 %collective-permute-start.60 = (bf16[1024,384]{1,0:T(8,128)(2,1)}, bf16[1024,384]{1,0:T(8,128)(2,1)}, u32[]{:S(2)}, u32[]{:S(2)}) collective-permute-start(bf16[1024,384]{1,0:T(8,128)(2,1)} %get-tuple-element.461), channel_id=1, source_target_pairs={{0,16},{16,0},{1,17},{17,1},{2,18},{18,2},{3,19},{19,3},{4,20},{20... | collective-permute-start | bytes 2359304 | tf_op jit(solution)/shard_map/ppermute | solution.py:529
  697.2 37.7 %collective-permute-start.61 = (bf16[1024,384]{1,0:T(8,128)(2,1)}, bf16[1024,384]{1,0:T(8,128)(2,1)}, u32[]{:S(2)}, u32[]{:S(2)}) collective-permute-start(bf16[1024,384]{1,0:T(8,128)(2,1)} %get-tuple-element.462), channel_id=1, source_target_pairs={{0,16},{16,0},{1,17},{17,1},{2,18},{18,2},{3,19},{19,3},{4,20},{20... | collective-permute-start | bytes 2359304 | tf_op jit(solution)/shard_map/ppermute | solution.py:529
  (196 other events, 2768.5 us)
Sparse Core Ops, SparseCore 0:
  463.7 161.6 reduce-scatter.2
  630.1 83.4 reduce-scatter.4

commit v4 on v3

--- a/solution.py
+++ b/solution.py
@@ -915,18 +915,17 @@
         active_near,
         out_mine,
     )
-    out_c = core_swap(two_far_sent)
     late_n = core_swap(late_terms[TAIL : 2 * TAIL])
     late_x = chip_swap(late_terms[2 * TAIL : 3 * TAIL])
     late_xc = across_swap(late_terms[3 * TAIL :])
+    q1_in = group_swap(sent1)
+    a1 = ring_down(add(a2, add(kept[1], s1_o)))
     q3_sum = add(kept3, q3_in)
-    a2_s1 = add(a2, add(kept[1], s1_o))
-    late_n, late_x, late_xc, q3_sum, a2_s1, sent0, sent1, out_c, active_near, q2_in = sync(
-        late_n, late_x, late_xc, q3_sum, a2_s1, sent0, sent1, out_c, active_near, q2_in
-    )
-    branch_two_xa = chip_swap(add(two_far_branch[:part], out_c[:part]))
-    branch_two_in = add(two_far_branch[part:], out_c[part:])
-    q1_in = group_swap(sent1)
+    late_n, late_x, late_xc, q1_in, a1, q3_sum, sent0, active_near, q2_in, two_far_sent = sync(
+        late_n, late_x, late_xc, q1_in, a1, q3_sum, sent0, active_near, q2_in, two_far_sent
+    )
+    out_c = core_swap(two_far_sent)
+    q0_in = group_swap(sent0)
     qa3 = ring_down(q3_sum)
     normed_grad = near.astype(F32) + near_c.astype(F32) + cat(normed_ga, normed_gb).astype(F32)
     tail = functools.reduce(
@@ -964,43 +963,39 @@
         )
         owners = lax.dynamic_update_slice(owners, piece, ((owner * TEAM + mine) * place,))
 
-    vector, q1_in, qa3, branch_two_xa, branch_two_in, sent0, a2_s1 = sync(
-        cat(small, owners), q1_in, qa3, branch_two_xa, branch_two_in, sent0, a2_s1
-    )
+    vector, q0_in, qa3, out_c, a1 = sync(cat(small, owners), q0_in, qa3, out_c, a1)
 
     def add_shifts(shifts, here):
         shifts = jnp.stack(shifts)
         return functools.reduce(jnp.add, [shifts[here(i)] for i in range(shifts.shape[0])])
 
     shifts = [vector, core_swap(vector), chip_swap(vector), across_swap(vector)]
-    q0_in = group_swap(sent0)
-    a1 = ring_down(a2_s1)
-    qa3_sum = add(qa3, add(kept2, q2_in))
-    q0_in, a1, qa3_sum, active_near, *shifts = sync(q0_in, a1, qa3_sum, active_near, *shifts)
+    branch_two_xa = chip_swap(add(two_far_branch[:part], out_c[:part]))
+    branch_two_in = add(two_far_branch[part:], out_c[part:])
+    qa2 = ring_down(add(qa3, add(kept2, q2_in)))
+    branch_two_xa, branch_two_in, qa2, active_near, a1, *shifts = sync(
+        branch_two_xa, branch_two_in, qa2, active_near, a1, *shifts
+    )
     vector = add_shifts(shifts, lambda i: mine ^ i)
     shifts = [vector] + [ring_up(vector, r) for r in range(1, teams)]
-    qa2 = ring_down(qa3_sum)
+    qa1 = ring_down(add(qa2, add(kept1, q1_in)))
     expand_mine = other_groups(add(a1, add(kept[0], s0_o)))
     expand_other = group_swap(expand_mine)
     two_near_branch, two_near_sent = matmul(active_near, contract_all, False, parts=2)
-    qa2, expand_other, two_near_branch, two_near_sent, branch_two_in, out_mine, *shifts = sync(
-        qa2, expand_other, two_near_branch, two_near_sent, branch_two_in, out_mine, *shifts
+    qa1, expand_other, two_near_branch, two_near_sent, branch_two_in, out_mine, *shifts = sync(
+        qa1, expand_other, two_near_branch, two_near_sent, branch_two_in, out_mine, *shifts
     )
     vector = add_shifts(shifts, lambda i: (team + teams - i) % teams)
     bit = 1
     while bit < n_dp:
         vector = vector + group_swap(vector, bit)
         bit *= 2
-    qa1 = ring_down(add(qa2, add(kept1, q1_in)))
+    qkv_mine = other_groups(add(qa1, add(kept0, q0_in)))
+    qkv_other = group_swap(qkv_mine)
     branch_two_xb = chip_swap(branch_two_in)
     two_near_c = core_swap(two_near_sent)
     out_sum = other_groups(out_mine)
     out_other = group_swap(out_sum)
-    vector, qa1, branch_two_xb, two_near_c, out_other = sync(
-        vector, qa1, branch_two_xb, two_near_c, out_other
-    )
-    qkv_mine = other_groups(add(qa1, add(kept0, q0_in)))
-    qkv_other = group_swap(qkv_mine)
     mine_spot = lax.dynamic_slice(vector, (6 * width + me * place,), (place,))
     six = [vector[k * width : (k + 1) * width] for k in range(6)]
 

time: 903 us -> 897 us (level)
    ppermute x22, waiting for transfers between devices: 54.3 us -> 36.5 us  [group_swap(): return lax.ppermute(v, 'dp', [(i, i ^ bit) for i in range(n_dp)])]
    ppermute x3, waiting for transfers between devices: 13.2 us -> 30.7 us  [across_swap(): return lax.ppermute(v, 'mp', [(i, i ^ 3) for i in range(n_mp)])]
    unnamed x276 -> x280, local copies, waits for them, and re-layouts: 57.9 us -> 59 us
  transfers between devices with their start and end apart: 89 -> 89, of which waited for: 38 -> 35; matrix products, arithmetic and copies ran while one was open for 13% -> 13% of each run, Pallas kernels for 39% -> 39%
where the time goes in v4:
time: 897 us; the launch traced here: 890 us
  Pallas kernels  380 us (42%)
  waiting for transfers between devices  203 us (23%)
  other arithmetic  88.2 us (10%)
  starting transfers between devices  87.8 us (10%)
  local copies, waits for them, and re-layouts  82.7 us (9%)
  matrix products  31.7 us (4%)
  between operations  16.1 us (2%)
    pallas_call x13, Pallas kernels, matmul(): pl.pallas_call(functools.partial(matmul_kernel, transposed, parts), grid=...  132 us
    pallas_call x5, Pallas kernels, weight_grad(): pl.pallas_call(functools.partial(weight_grad_kernel, splits, halves, len(...  91.9 us
    unnamed x280, local copies, waits for them, and re-layouts  59 us
    pallas_call x2, Pallas kernels, attend_back(): pl.pallas_call(functools.partial(attend_back_kernel, first, count), grid_...  52.7 us
    ppermute x2, waiting for transfers between devices, line_up(): lax.ppermute(v, 'mp', [(i, i + by * TEAM) for i in range(n_mp - by * TEAM)])  48.1 us
    pallas_call x4, Pallas kernels, attend(): pl.pallas_call(functools.partial(attend_kernel, first, count), grid_spec=...  48 us
    ppermute x22, waiting for transfers between devices, group_swap(): return lax.ppermute(v, 'dp', [(i, i ^ bit) for i in range(n_dp)])  36.5 us
    ppermute x19, waiting for transfers between devices, chip_swap(): return lax.ppermute(v, 'mp', [(i, i ^ 2) for i in range(n_mp)])  36.3 us
  transfers between devices with their start and end apart: 89, of which 35 were waited for; matrix products, arithmetic and copies ran while one was open for 13% of the time, Pallas kernels for 39%

profile of v4, /device:TPU:0, one launch (start us, length us, event | category | flops | bytes accessed | tf_op | source)
XLA Modules:
  0.0 890.1 jit_solution(2609319458965402153)
XLA Ops:
  26.9 23.8 %collective-permute-done.3 = bf16[64,2048]{1,0:T(8,128)(2,1)S(1)} collective-permute-done((bf16[64,2048]{1,0:T(8,128)(2,1)S(1)}, bf16[64,2048]{1,0:T(8,128)(2,1)S(1)}, u32[]{:S(2)}, u32[]{:S(2)}) %collective-permute-start.3) | collective-permute-done | bytes 262176 | tf_op jit(solution)/shard_map/ppermute | solution.py:523
  59.8 24.3 %collective-permute-done.7 = bf16[64,2048]{1,0:T(8,128)(2,1)S(1)} collective-permute-done((bf16[64,2048]{1,0:T(8,128)(2,1)S(1)}, bf16[64,2048]{1,0:T(8,128)(2,1)S(1)}, u32[]{:S(2)}, u32[]{:S(2)}) %collective-permute-start.7) | collective-permute-done | bytes 262176 | tf_op jit(solution)/shard_map/ppermute | solution.py:523
  108.5 11.6 %collective-permute-done.11.refs_12_.refs_8_.refs_2_ = bf16[128,2048]{1,0:T(8,128)(2,1)S(1)} collective-permute-done((bf16[128,2048]{1,0:T(8,128)(2,1)S(1)}, bf16[128,2048]{1,0:T(8,128)(2,1)S(1)}, u32[]{:S(2)}, u32[]{:S(2)}) %collective-permute-start.11) | collective-permute-done | bytes 524320 | tf_op jit(solution)/shard_map/ppermute | solution.py:514
  125.6 22.5 %project.2.qkv_ref.refs_0_ = bf16[2560,1152]{1,0:T(8,128)(2,1)} custom-call(s32[1]{0:T(128)} %bitcast.1.which_ref, bf16[1040,512]{1,0:T(8,128)(2,1)} %copy-done.12, bf16[1024,512]{1,0:T(8,128)(2,1)} %get-tuple-element.338.refs_1_, bf16[1040,512]{1,0:T(8,128)(2,1)} %copy-done.17, bf16[1040,512]{1,0:T(8,128)(2,1)} %copy-done.20, bf16[1040,512]{1,0:T(8,128)(2,1)} %copy-done.23, ...), custom_call_target="tpu_custom_call" | custom-call | flops 1024 | bytes 1024 | tf_op jit(solution)/shard_map/project/pallas_call | solution.py:431
  153.8 11.7 %project.3.qkv_ref.refs_1_ = bf16[2560,384]{1,0:T(8,128)(2,1)} custom-call(s32[1]{0:T(128)} %bitcast.1.which_ref, bf16[1040,512]{1,0:T(8,128)(2,1)} %copy-done.31, bf16[1040,512]{1,0:T(8,128)(2,1)} %copy-done.35, bf16[512,2048]{1,0:T(8,128)(2,1)} %copy-done.70, bf16[512,2048]{1,0:T(8,128)(2,1)} %copy-done.76, ...), custom_call_target="tpu_custom_call" | custom-call | flops 1024 | bytes 1024 | tf_op jit(solution)/shard_map/project/pallas_call | solution.py:431
  178.4 16.7 %attend.4 = (bf16[1024,384]{1,0:T(8,128)(2,1)}, f32[3,2,2,512]{3,2,1,0:T(2,128)}) custom-call(s32[18]{0:T(128)} %compare_select_fusion.3.info_ref, bf16[2560,1152]{1,0:T(8,128)(2,1)} %project.2.qkv_ref.refs_0_), custom_call_target="tpu_custom_call" | custom-call | flops 1024 | bytes 1024 | tf_op jit(solution)/shard_map/attend/pallas_call | solution.py:147
  213.4 16.5 %attend.6 = (bf16[1024,384]{1,0:T(8,128)(2,1)}, f32[3,2,2,512]{3,2,1,0:T(2,128)}) custom-call(s32[18]{0:T(128)} %compare_select_fusion.3.info_ref, bf16[2560,1152]{1,0:T(8,128)(2,1)} %project.2.qkv_ref.refs_0_), custom_call_target="tpu_custom_call" | custom-call | flops 1024 | bytes 1024 | tf_op jit(solution)/shard_map/attend/pallas_call | solution.py:147
  316.9 15.8 %fusion.6 = (bf16[1024,2048]{1,0:T(8,128)(2,1)}, bf16[1024,2048]{1,0:T(8,128)(2,1)}) fusion(f32[2048]{0:T(1024)S(1)} %convert_element_type.352, bf16[1024,2048]{1,0:T(8,128)(2,1)S(1)} %pack.25.refs_0_, bf16[2048,2048]{1,0:T(8,128)(2,1)S(1)} %copy-done.2), kind=kOutput, calls=%fused_computation.11 | convolution fusion | flops 8633974784 | bytes 20979712 | tf_op jit(solution)/shard_map/dot_general | solution.py:48
  341.4 15.9 %fusion.13 = (bf16[1024,2048]{1,0:T(8,128)(2,1)}, bf16[1024,2048]{1,0:T(8,128)(2,1)}) fusion(f32[2048]{0:T(1024)S(1)} %convert_element_type.352, bf16[1024,2048]{1,0:T(8,128)(2,1)S(1)} %pack.26.refs_2_, bf16[2048,2048]{1,0:T(8,128)(2,1)S(1)} %copy-done.2), kind=kOutput, calls=%fused_computation.18 | convolution fusion | flops 8633974784 | bytes 20979712 | tf_op jit(solution)/shard_map/dot_general | solution.py:48
  374.3 14.4 %matmul.15.left_ref.refs_3_ = bf16[1024,2048]{1,0:T(8,128)(2,1)} custom-call(bf16[1024,2048]{1,0:T(8,128)(2,1)} %copy-done.6, bf16[2048,2048]{1,0:T(8,128)(2,1)} %copy-done, bf16[1024,2048]{1,0:T(8,128)(2,1)} %get-tuple-element.362.rest_0_), custom_call_target="tpu_custom_call" | custom-call | flops 1024 | bytes 1024 | tf_op jit(solution)/shard_map/matmul/pallas_call | solution.py:470
  388.6 13.3 %matmul.16 = (bf16[512,2048]{1,0:T(8,128)(2,1)}, bf16[512,2048]{1,0:T(8,128)(2,1)}) custom-call(bf16[1024,2048]{1,0:T(8,128)(2,1)} %matmul.15.left_ref.refs_3_, bf16[2048,2048]{1,0:T(8,128)(2,1)} %copy-done.1), custom_call_target="tpu_custom_call" | custom-call | flops 1024 | bytes 1024 | tf_op jit(solution)/shard_map/matmul/pallas_call | solution.py:470
  408.7 14.3 %matmul.17.left_ref.refs_1_ = bf16[1024,2048]{1,0:T(8,128)(2,1)} custom-call(bf16[1024,2048]{1,0:T(8,128)(2,1)} %copy-done.7, bf16[2048,2048]{1,0:T(8,128)(2,1)} %copy-done, bf16[1024,2048]{1,0:T(8,128)(2,1)} %get-tuple-element.373.rest_0_), custom_call_target="tpu_custom_call" | custom-call | flops 1024 | bytes 1024 | tf_op jit(solution)/shard_map/matmul/pallas_call | solution.py:470
  423.0 13.1 %matmul.18 = (bf16[512,2048]{1,0:T(8,128)(2,1)}, bf16[512,2048]{1,0:T(8,128)(2,1)}) custom-call(bf16[1024,2048]{1,0:T(8,128)(2,1)} %matmul.17.left_ref.refs_1_, bf16[2048,2048]{1,0:T(8,128)(2,1)} %copy-done.1), custom_call_target="tpu_custom_call" | custom-call | flops 1024 | bytes 1024 | tf_op jit(solution)/shard_map/matmul/pallas_call | solution.py:470
  438.9 24.7 %weight_grad.5 = bf16[2048,2048]{1,0:T(8,128)(2,1)} custom-call(s32[8]{0:T(128)} %iota.33.source_ref, s32[8]{0:T(128)} %stack.80.target_ref, bf16[1024,2048]{1,0:T(8,128)(2,1)} %get-tuple-element.504.refs_0_.left_ref, bf16[1024,2048]{1,0:T(8,128)(2,1)} %copy-done.7, bf16[1024,2048]{1,0:T(8,128)(2,1)} %get-tuple-element.464.refs_2_.left_ref, ...), custom_call_target="tpu_custom_call" | custom-call | flops 1024 | bytes 1024 | tf_op jit(solution)/shard_map/weight_grad/pallas_call | solution.py:328
  481.1 25.3 %weight_grad.6 = (bf16[2048,256]{1,0:T(8,128)(2,1)}, bf16[2048,256]{1,0:T(8,128)(2,1)}, bf16[2048,256]{1,0:T(8,128)(2,1)}, bf16[2048,256]{1,0:T(8,128)(2,1)}, bf...) custom-call(s32[8]{0:T(128)} %iota.34.source_ref.target_ref, ...), custom_call_target="tpu_custom_call" | custom-call | flops 1024 | bytes 1024 | tf_op jit(solution)/shard_map/weight_grad/pallas_call | solution.py:328
  523.5 26.0 %attend_back.2.rest_0_ = bf16[2560,1536]{1,0:T(8,128)(2,1)} custom-call(s32[18]{0:T(128)} %compare_select_fusion.3.info_ref, bf16[2560,1536]{1,0:T(8,128)(2,1)} %copy-done.3, bf16[1024,512]{1,0:T(8,128)(2,1)} %copy-done.39, bf16[1024,512]{1,0:T(8,128)(2,1)} %matmul.19.grad_ref, f32[4,2,2,512]{3,2,1,0:T(2,128)} %pad_maximum_fusion.7.log_ref), custom_call_target="tpu_custom_call" | custom-call | flops 1024 | bytes 1024 | tf_op jit(solution)/shard_map/attend_back/pallas_call | solution.py:258
  569.4 26.7 %attend_back.3 = (bf16[2560,1536]{1,0:T(8,128)(2,1)}, bf16[256,1024]{1,0:T(8,128)(2,1)}, bf16[256,1024]{1,0:T(8,128)(2,1)}) custom-call(s32[18]{0:T(128)} %compare_select_fusion.3.info_ref, bf16[2560,1536]{1,0:T(8,128)(2,1)} %copy-done.3, bf16[1024,512]{1,0:T(8,128)(2,1)} %copy-done.38, bf16[1024,512]{1,0:T(8,128)(2,1)} %matmul.20.grad_ref, ...), custom_call_target="tpu_custom_call" | custom-call | flops 1024 | bytes 1024 | tf_op jit(solution)/shard_map/attend_back/pallas_call | solution.py:258
  659.0 16.0 %weight_grad.8 = (bf16[1024,384]{1,0:T(8,128)(2,1)}, bf16[1024,384]{1,0:T(8,128)(2,1)}, bf16[1024,384]{1,0:T(8,128)(2,1)}, bf16[1024,384]{1,0:T(8,128)(2,1)}) custom-call(s32[8]{0:T(128)} %broadcast_select_fusion.source_ref, s32[8]{0:T(128)} %iota.38.target_ref, bf16[512,2048]{1,0:T(8,128)(2,1)} %copy-done.70, ...), custom_call_target="tpu_custom_call" | custom-call | flops 1024 | bytes 1024 | tf_op jit(solution)/shard_map/weight_grad/pallas_call | solution.py:328
  675.0 17.5 %collective-permute-done.56.refs_0_.refs_1_ = bf16[256,1024]{1,0:T(8,128)(2,1)S(1)} collective-permute-done((bf16[256,1024]{1,0:T(8,128)(2,1)S(1)}, bf16[256,1024]{1,0:T(8,128)(2,1)S(1)}, u32[]{:S(2)}, u32[]{:S(2)}) %collective-permute-start.56) | collective-permute-done | bytes 524320 | tf_op jit(solution)/shard_map/ppermute | solution.py:526
  697.1 13.1 %matmul.24 = (bf16[512,2048]{1,0:T(8,128)(2,1)}, bf16[512,2048]{1,0:T(8,128)(2,1)}) custom-call(bf16[1024,2048]{1,0:T(8,128)(2,1)} %get-tuple-element.464.refs_2_.left_ref, bf16[2048,2048]{1,0:T(8,128)(2,1)} %copy-done), custom_call_target="tpu_custom_call" | custom-call | flops 1024 | bytes 1024 | tf_op jit(solution)/shard_map/matmul/pallas_call | solution.py:470
  710.6 15.4 %weight_grad.9 = (bf16[1024,384]{1,0:T(8,128)(2,1)}, bf16[1024,384]{1,0:T(8,128)(2,1)}, bf16[1024,384]{1,0:T(8,128)(2,1)}, bf16[1024,384]{1,0:T(8,128)(2,1)}) custom-call(s32[8]{0:T(128)} %broadcast_select_fusion.source_ref, s32[8]{0:T(128)} %iota.39.target_ref, bf16[512,2048]{1,0:T(8,128)(2,1)} %copy-done.70, ...), custom_call_target="tpu_custom_call" | custom-call | flops 1024 | bytes 1024 | tf_op jit(solution)/shard_map/weight_grad/pallas_call | solution.py:328
  799.5 15.2 %collective-permute-done.76 = f32[26624]{0:T(1024)S(1)} collective-permute-done((f32[26624]{0:T(1024)S(1)}, f32[26624]{0:T(1024)S(1)}, u32[]{:S(2)}, u32[]{:S(2)}) %collective-permute-start.76) | collective-permute-done | bytes 106528 | tf_op jit(solution)/shard_map/ppermute | solution.py:573
  835.0 13.2 %matmul.25 = (bf16[512,2048]{1,0:T(8,128)(2,1)}, bf16[512,2048]{1,0:T(8,128)(2,1)}) custom-call(bf16[1024,2048]{1,0:T(8,128)(2,1)} %get-tuple-element.504.refs_0_.left_ref, bf16[2048,2048]{1,0:T(8,128)(2,1)} %copy-done), custom_call_target="tpu_custom_call" | custom-call | flops 1024 | bytes 1024 | tf_op jit(solution)/shard_map/matmul/pallas_call | solution.py:470
  861.0 12.3 %collective-permute-done.85 = bf16[1024,384]{1,0:T(8,128)(2,1)S(1)} collective-permute-done((bf16[1024,384]{1,0:T(8,128)(2,1)S(1)}, bf16[1024,384]{1,0:T(8,128)(2,1)S(1)}, u32[]{:S(2)}, u32[]{:S(2)}) %collective-permute-start.85) | collective-permute-done | bytes 786464 | tf_op jit(solution)/shard_map/ppermute | solution.py:529
  (591 shorter events, 454.7 us)
Async XLA Ops:
  7.2 618.2 %reduce-scatter.3.cloned.1.call-start = ((), (), s32[]{:S(2)}) async-start(), calls=%async_computation.2 | async-start | bytes 9437184 | tf_op jit(solution)/shard_map/reduce_scatter | solution.py:593
  50.7 34.3 %collective-permute-start.6 = (bf16[256,2048]{1,0:T(8,128)(2,1)S(1)}, bf16[256,2048]{1,0:T(8,128)(2,1)S(1)}, u32[]{:S(2)}, u32[]{:S(2)}) collective-permute-start(bf16[256,2048]{1,0:T(8,128)(2,1)S(1)} %get-tuple-element.277), channel_id=1, source_target_pairs={{0,2},{1,3},{2,0},{3,1},{4,6},{5,7},{6,4},{7,5},{8,10},{9,11},{10,... | collective-permute-start | bytes 3145736 | tf_op jit(solution)/shard_map/ppermute | solution.py:514
  52.3 34.4 %collective-permute-start.5 = (bf16[1040,512]{1,0:T(8,128)(2,1)S(1)}, bf16[1040,512]{1,0:T(8,128)(2,1)S(1)}, u32[]{:S(2)}, u32[]{:S(2)}) collective-permute-start(bf16[1040,512]{1,0:T(8,128)(2,1)S(1)} %collective-permute-done.refs_2_), channel_id=1, source_target_pairs={{0,16},{16,0},{1,17},{17,1},{2,18},{18,2},{3,19},{19,3},{4,20},{20... | collective-permute-start | bytes 3194888 | tf_op jit(solution)/shard_map/ppermute | solution.py:529
  150.0 54.8 %collective-permute-start.20 = (bf16[512,2048]{1,0:T(8,128)(2,1)S(1)}, bf16[512,2048]{1,0:T(8,128)(2,1)}, u32[]{:S(2)}, u32[]{:S(2)}) collective-permute-start(bf16[512,2048]{1,0:T(8,128)(2,1)S(1)} %copy-done.10), channel_id=1, source_target_pairs={{0,1},{1,0},{2,3},{3,2},{4,5},{5,4},{6,7},{7,6},{8,9},{9,8},{10,11... | collective-permute-start | bytes 6291464 | tf_op jit(solution)/shard_map/ppermute | solution.py:511
  150.0 54.8 %collective-permute-start.18 = (bf16[2064,256]{1,0:T(8,128)(2,1)}, bf16[2064,256]{1,0:T(8,128)(2,1)}, u32[]{:S(2)}, u32[]{:S(2)}) collective-permute-start(bf16[2064,256]{1,0:T(8,128)(2,1)} %collective-permute-done.16.refs_2_), channel_id=1, source_target_pairs={{0,16},{16,0},{1,17},{17,1},{2,18},{18,2},{3,19},{19,3},{4,20},{20... | collective-permute-start | bytes 3170312 | tf_op jit(solution)/shard_map/ppermute | solution.py:529
  150.6 54.3 %collective-permute-start.17 = (bf16[2064,256]{1,0:T(8,128)(2,1)}, bf16[2064,256]{1,0:T(8,128)(2,1)}, u32[]{:S(2)}, u32[]{:S(2)}) collective-permute-start(bf16[2064,256]{1,0:T(8,128)(2,1)} %collective-permute-done.16.refs_2_), channel_id=1, source_target_pairs={{0,4},{1,5},{2,6},{3,7},{4,8},{5,9},{6,10},{7,11},{8,12},{9,13},{1... | collective-permute-start | bytes 3170312 | tf_op jit(solution)/shard_map/ppermute | solution.py:517
  151.5 51.6 %collective-permute-start.19 = (bf16[256,2048]{1,0:T(8,128)(2,1)}, bf16[256,2048]{1,0:T(8,128)(2,1)}, u32[]{:S(2)}, u32[]{:S(2)}) collective-permute-start(bf16[256,2048]{1,0:T(8,128)(2,1)} %get-tuple-element.295), channel_id=1, source_target_pairs={{0,2},{1,3},{2,0},{3,1},{4,6},{5,7},{6,4},{7,5},{8,10},{9,11},{10,... | collective-permute-start | bytes 3145736 | tf_op jit(solution)/shard_map/ppermute | solution.py:514
  212.1 43.9 %collective-permute-start.28 = (bf16[512,2048]{1,0:T(8,128)(2,1)S(1)}, bf16[512,2048]{1,0:T(8,128)(2,1)}, u32[]{:S(2)}, u32[]{:S(2)}) collective-permute-start(bf16[512,2048]{1,0:T(8,128)(2,1)S(1)} %pack.18.refs_0_), channel_id=1, source_target_pairs={{0,1},{1,0},{2,3},{3,2},{4,5},{5,4},{6,7},{7,6},{8,9},{9,8},{10,11... | collective-permute-start | bytes 6291464 | tf_op jit(solution)/shard_map/ppermute | solution.py:511
  463.6 274.1 %reduce-scatter.5.cloned.1.call-start = ((), (), s32[]{:S(2)}) async-start(), calls=%async_computation.3 | async-start | bytes 2359296 | tf_op jit(solution)/shard_map/reduce_scatter | solution.py:593
  506.3 43.1 %collective-permute-start.46 = (bf16[256,2048]{1,0:T(8,128)(2,1)}, bf16[256,2048]{1,0:T(8,128)(2,1)}, u32[]{:S(2)}, u32[]{:S(2)}) collective-permute-start(bf16[256,2048]{1,0:T(8,128)(2,1)} %get-tuple-element.396), channel_id=1, source_target_pairs={{0,2},{1,3},{2,0},{3,1},{4,6},{5,7},{6,4},{7,5},{8,10},{9,11},{10,... | collective-permute-start | bytes 3145736 | tf_op jit(solution)/shard_map/ppermute | solution.py:514
  508.3 41.2 %collective-permute-start.47 = (bf16[2048,256]{1,0:T(8,128)(2,1)}, bf16[2048,256]{1,0:T(8,128)(2,1)}, u32[]{:S(2)}, u32[]{:S(2)}) collective-permute-start(bf16[2048,256]{1,0:T(8,128)(2,1)} %get-tuple-element.397), channel_id=1, source_target_pairs={{0,16},{16,0},{1,17},{17,1},{2,18},{18,2},{3,19},{19,3},{4,20},{20... | collective-permute-start | bytes 3145736 | tf_op jit(solution)/shard_map/ppermute | solution.py:529
  508.4 41.0 %collective-permute-start.48 = (bf16[256,2048]{1,0:T(8,128)(2,1)}, bf16[256,2048]{1,0:T(8,128)(2,1)}, u32[]{:S(2)}, u32[]{:S(2)}) collective-permute-start(bf16[256,2048]{1,0:T(8,128)(2,1)} %collective-permute-done.44.refs_0_), channel_id=1, source_target_pairs={{0,1},{1,0},{2,3},{3,2},{4,5},{5,4},{6,7},{7,6},{8,9},{9,8},{10,11... | collective-permute-start | bytes 3145736 | tf_op jit(solution)/shard_map/ppermute | solution.py:511
  552.6 65.2 %collective-permute-start.50 = (bf16[2048,256]{1,0:T(8,128)(2,1)}, bf16[2048,256]{1,0:T(8,128)(2,1)}, u32[]{:S(2)}, u32[]{:S(2)}) collective-permute-start(bf16[2048,256]{1,0:T(8,128)(2,1)} %get-tuple-element.416), channel_id=1, source_target_pairs={{0,16},{16,0},{1,17},{17,1},{2,18},{18,2},{3,19},{19,3},{4,20},{20... | collective-permute-start | bytes 3145736 | tf_op jit(solution)/shard_map/ppermute | solution.py:529
  554.5 64.2 %collective-permute-start.51 = (bf16[2048,256]{1,0:T(8,128)(2,1)}, bf16[2048,256]{1,0:T(8,128)(2,1)}, u32[]{:S(2)}, u32[]{:S(2)}) collective-permute-start(bf16[2048,256]{1,0:T(8,128)(2,1)} %get-tuple-element.417), channel_id=1, source_target_pairs={{0,16},{16,0},{1,17},{17,1},{2,18},{18,2},{3,19},{19,3},{4,20},{20... | collective-permute-start | bytes 3145736 | tf_op jit(solution)/shard_map/ppermute | solution.py:529
  554.6 64.1 %collective-permute-start.52 = (bf16[2048,256]{1,0:T(8,128)(2,1)S(1)}, bf16[2048,256]{1,0:T(8,128)(2,1)}, u32[]{:S(2)}, u32[]{:S(2)}) collective-permute-start(bf16[2048,256]{1,0:T(8,128)(2,1)S(1)} %add_convert_fusion.13), channel_id=1, source_target_pairs={{0,12},{1,13},{2,14},{3,15},{4,0},{5,1},{6,2},{7,3},{8,4},{9,5},{1... | collective-permute-start | bytes 3145736 | tf_op jit(solution)/shard_map/ppermute | solution.py:520
  629.9 62.5 %collective-permute-start.57 = (bf16[2048,256]{1,0:T(8,128)(2,1)}, bf16[2048,256]{1,0:T(8,128)(2,1)}, u32[]{:S(2)}, u32[]{:S(2)}) collective-permute-start(bf16[2048,256]{1,0:T(8,128)(2,1)} %get-tuple-element.442), channel_id=1, source_target_pairs={{0,16},{16,0},{1,17},{17,1},{2,18},{18,2},{3,19},{19,3},{4,20},{20... | collective-permute-start | bytes 3145736 | tf_op jit(solution)/shard_map/ppermute | solution.py:529
  630.6 61.8 %collective-permute-start.58 = (bf16[256,2048]{1,0:T(8,128)(2,1)}, bf16[256,2048]{1,0:T(8,128)(2,1)}, u32[]{:S(2)}, u32[]{:S(2)}) collective-permute-start(bf16[256,2048]{1,0:T(8,128)(2,1)} %reduce-scatter.3.cloned.1.call-done), channel_id=1, source_target_pairs={{0,16},{16,0},{1,17},{17,1},{2,18},{18,2},{3,19},{19,3},{4,20},{20... | collective-permute-start | bytes 3145736 | tf_op jit(solution)/shard_map/ppermute | solution.py:529
  636.4 56.0 %collective-permute-start.54 = (bf16[256,2048]{1,0:T(8,128)(2,1)}, bf16[256,2048]{1,0:T(8,128)(2,1)}, u32[]{:S(2)}, u32[]{:S(2)}) collective-permute-start(bf16[256,2048]{1,0:T(8,128)(2,1)} %get-tuple-element.549), channel_id=1, source_target_pairs={{0,2},{1,3},{2,0},{3,1},{4,6},{5,7},{6,4},{7,5},{8,10},{9,11},{10,... | collective-permute-start | bytes 3145736 | tf_op jit(solution)/shard_map/ppermute | solution.py:514
  643.4 49.0 %collective-permute-start.56 = (bf16[256,1024]{1,0:T(8,128)(2,1)S(1)}, bf16[256,1024]{1,0:T(8,128)(2,1)S(1)}, u32[]{:S(2)}, u32[]{:S(2)}) collective-permute-start(bf16[256,1024]{1,0:T(8,128)(2,1)S(1)} %copy-done.129), channel_id=1, source_target_pairs={{8,0},{9,1},{10,2},{11,3},{12,4},{13,5},{14,6},{15,7},{24,16},{25,... | collective-permute-start | bytes 1572872 | tf_op jit(solution)/shard_map/ppermute | solution.py:526
  692.4 45.2 %collective-permute-start.63 = (bf16[512,2048]{1,0:T(8,128)(2,1)}, bf16[512,2048]{1,0:T(8,128)(2,1)}, u32[]{:S(2)}, u32[]{:S(2)}) collective-permute-start(bf16[512,2048]{1,0:T(8,128)(2,1)} %get-tuple-element.457), channel_id=1, source_target_pairs={{0,1},{1,0},{2,3},{3,2},{4,5},{5,4},{6,7},{7,6},{8,9},{9,8},{10,11... | collective-permute-start | bytes 6291464 | tf_op jit(solution)/shard_map/ppermute | solution.py:511
  694.0 42.6 %collective-permute-start.60 = (bf16[1024,384]{1,0:T(8,128)(2,1)}, bf16[1024,384]{1,0:T(8,128)(2,1)}, u32[]{:S(2)}, u32[]{:S(2)}) collective-permute-start(bf16[1024,384]{1,0:T(8,128)(2,1)} %get-tuple-element.454), channel_id=1, source_target_pairs={{0,16},{16,0},{1,17},{17,1},{2,18},{18,2},{3,19},{19,3},{4,20},{20... | collective-permute-start | bytes 2359304 | tf_op jit(solution)/shard_map/ppermute | solution.py:529
  694.7 42.0 %collective-permute-start.61 = (bf16[1024,384]{1,0:T(8,128)(2,1)}, bf16[1024,384]{1,0:T(8,128)(2,1)}, u32[]{:S(2)}, u32[]{:S(2)}) collective-permute-start(bf16[1024,384]{1,0:T(8,128)(2,1)} %get-tuple-element.455), channel_id=1, source_target_pairs={{0,16},{16,0},{1,17},{17,1},{2,18},{18,2},{3,19},{19,3},{4,20},{20... | collective-permute-start | bytes 2359304 | tf_op jit(solution)/shard_map/ppermute | solution.py:529
  696.1 40.5 %collective-permute-start.59 = (bf16[256,2048]{1,0:T(8,128)(2,1)S(1)}, bf16[256,2048]{1,0:T(8,128)(2,1)}, u32[]{:S(2)}, u32[]{:S(2)}) collective-permute-start(bf16[256,2048]{1,0:T(8,128)(2,1)S(1)} %copy-done.92), channel_id=1, source_target_pairs={{0,2},{1,3},{2,0},{3,1},{4,6},{5,7},{6,4},{7,5},{8,10},{9,11},{10,... | collective-permute-start | bytes 3145736 | tf_op jit(solution)/shard_map/ppermute | solution.py:514
  697.1 39.6 %collective-permute-start.62 = (bf16[2048,256]{1,0:T(8,128)(2,1)S(1)}, bf16[2048,256]{1,0:T(8,128)(2,1)S(1)}, u32[]{:S(2)}, u32[]{:S(2)}) collective-permute-start(bf16[2048,256]{1,0:T(8,128)(2,1)S(1)} %copy-done.93), channel_id=1, source_target_pairs={{0,12},{1,13},{2,14},{3,15},{4,0},{5,1},{6,2},{7,3},{8,4},{9,5},{1... | collective-permute-start | bytes 3145736 | tf_op jit(solution)/shard_map/ppermute | solution.py:520
  (198 other events, 2843.3 us)
Sparse Core Ops, SparseCore 0:
  463.7 161.6 reduce-scatter.2
  630.1 83.1 reduce-scatter.4

commit v5 on v4

--- a/solution.py
+++ b/solution.py
@@ -733,9 +733,11 @@
     two_far = pack_rows(which, [two_xa, two_xb, two_xac, two_xbc])
     active_far, slope_far = front(two_far)
     qkv = pack_columns(which, [qkv_a, qkv_b], qkv_a.shape[0])
-    k3_o, active_far, slope_far, two_far, cot_x = sync(k3_o, active_far, slope_far, two_far, cot_x)
+    cot_far = pack_rows(which, [cot_x, cot_xc])
+    k3_o, active_far, slope_far, two_far, cot_far, qkv = sync(
+        k3_o, active_far, slope_far, two_far, cot_far, qkv
+    )
     contract_all = pack_rows(which, [contract_own, contract_rest, k1, k1_o, k2, k2_o, k3, k3_o])
-    cot_far = pack_rows(which, [cot_x, cot_xc])
     before_far = matmul(cot_far, contract_all, True, slope_far)
     far, far_sent = matmul(before_far, expand_all, True, parts=2)
     far, far_sent, before_far, contract_all = sync(far, far_sent, before_far, contract_all)

time: 897 us -> 899 us (level)
  transfers between devices with their start and end apart: 89 -> 89, of which waited for: 35 -> 34; matrix products, arithmetic and copies ran while one was open for 13% -> 13% of each run, Pallas kernels for 39% -> 39%
where the time goes in v5:
time: 899 us; the launch traced here: 892 us
  Pallas kernels  378 us (42%)
  waiting for transfers between devices  210 us (23%)
  starting transfers between devices  87.6 us (10%)
  other arithmetic  87.6 us (10%)
  local copies, waits for them, and re-layouts  81 us (9%)
  matrix products  31.6 us (4%)
  between operations  16.2 us (2%)
    pallas_call x13, Pallas kernels, matmul(): pl.pallas_call(functools.partial(matmul_kernel, transposed, parts), grid=...  132 us
    pallas_call x5, Pallas kernels, weight_grad(): pl.pallas_call(functools.partial(weight_grad_kernel, splits, halves, len(...  91.7 us
    unnamed x280, local copies, waits for them, and re-layouts  59.2 us
    pallas_call x2, Pallas kernels, attend_back(): pl.pallas_call(functools.partial(attend_back_kernel, first, count), grid_...  52.6 us
    ppermute x2, waiting for transfers between devices, line_up(): lax.ppermute(v, 'mp', [(i, i + by * TEAM) for i in range(n_mp - by * TEAM)])  48.1 us
    pallas_call x4, Pallas kernels, attend(): pl.pallas_call(functools.partial(attend_kernel, first, count), grid_spec=...  48 us
    ppermute x22, waiting for transfers between devices, group_swap(): return lax.ppermute(v, 'dp', [(i, i ^ bit) for i in range(n_dp)])  37.7 us
    ppermute x19, waiting for transfers between devices, chip_swap(): return lax.ppermute(v, 'mp', [(i, i ^ 2) for i in range(n_mp)])  36.1 us
  transfers between devices with their start and end apart: 89, of which 34 were waited for; matrix products, arithmetic and copies ran while one was open for 13% of the time, Pallas kernels for 39%

profile of v5, /device:TPU:0, one launch (start us, length us, event | category | flops | bytes accessed | tf_op | source)
XLA Modules:
  0.0 892.1 jit_solution(3498205416555152959)
XLA Ops:
  26.9 23.8 %collective-permute-done.3 = bf16[64,2048]{1,0:T(8,128)(2,1)S(1)} collective-permute-done((bf16[64,2048]{1,0:T(8,128)(2,1)S(1)}, bf16[64,2048]{1,0:T(8,128)(2,1)S(1)}, u32[]{:S(2)}, u32[]{:S(2)}) %collective-permute-start.3) | collective-permute-done | bytes 262176 | tf_op jit(solution)/shard_map/ppermute | solution.py:523
  59.8 24.3 %collective-permute-done.7 = bf16[64,2048]{1,0:T(8,128)(2,1)S(1)} collective-permute-done((bf16[64,2048]{1,0:T(8,128)(2,1)S(1)}, bf16[64,2048]{1,0:T(8,128)(2,1)S(1)}, u32[]{:S(2)}, u32[]{:S(2)}) %collective-permute-start.7) | collective-permute-done | bytes 262176 | tf_op jit(solution)/shard_map/ppermute | solution.py:523
  125.5 22.6 %project.2.qkv_ref.refs_0_ = bf16[2560,1152]{1,0:T(8,128)(2,1)} custom-call(s32[1]{0:T(128)} %bitcast.1.which_ref, bf16[1040,512]{1,0:T(8,128)(2,1)} %copy-done.12, bf16[1024,512]{1,0:T(8,128)(2,1)} %get-tuple-element.339.refs_1_, bf16[1040,512]{1,0:T(8,128)(2,1)} %copy-done.17, bf16[1040,512]{1,0:T(8,128)(2,1)} %copy-done.20, bf16[1040,512]{1,0:T(8,128)(2,1)} %copy-done.23, ...), custom_call_target="tpu_custom_call" | custom-call | flops 1024 | bytes 1024 | tf_op jit(solution)/shard_map/project/pallas_call | solution.py:431
  153.7 11.7 %project.3.qkv_ref.refs_1_ = bf16[2560,384]{1,0:T(8,128)(2,1)} custom-call(s32[1]{0:T(128)} %bitcast.1.which_ref, bf16[1040,512]{1,0:T(8,128)(2,1)} %copy-done.31, bf16[1040,512]{1,0:T(8,128)(2,1)} %copy-done.35, bf16[512,2048]{1,0:T(8,128)(2,1)} %copy-done.70, bf16[512,2048]{1,0:T(8,128)(2,1)} %copy-done.76, ...), custom_call_target="tpu_custom_call" | custom-call | flops 1024 | bytes 1024 | tf_op jit(solution)/shard_map/project/pallas_call | solution.py:431
  178.4 16.7 %attend.4 = (bf16[1024,384]{1,0:T(8,128)(2,1)}, f32[3,2,2,512]{3,2,1,0:T(2,128)}) custom-call(s32[18]{0:T(128)} %compare_select_fusion.3.info_ref, bf16[2560,1152]{1,0:T(8,128)(2,1)} %project.2.qkv_ref.refs_0_), custom_call_target="tpu_custom_call" | custom-call | flops 1024 | bytes 1024 | tf_op jit(solution)/shard_map/attend/pallas_call | solution.py:147
  213.3 16.5 %attend.6 = (bf16[1024,384]{1,0:T(8,128)(2,1)}, f32[3,2,2,512]{3,2,1,0:T(2,128)}) custom-call(s32[18]{0:T(128)} %compare_select_fusion.3.info_ref, bf16[2560,1152]{1,0:T(8,128)(2,1)} %project.2.qkv_ref.refs_0_), custom_call_target="tpu_custom_call" | custom-call | flops 1024 | bytes 1024 | tf_op jit(solution)/shard_map/attend/pallas_call | solution.py:147
  316.8 15.8 %fusion.6 = (bf16[1024,2048]{1,0:T(8,128)(2,1)}, bf16[1024,2048]{1,0:T(8,128)(2,1)}) fusion(f32[2048]{0:T(1024)S(1)} %convert_element_type.352, bf16[1024,2048]{1,0:T(8,128)(2,1)S(1)} %pack.25.refs_0_, bf16[2048,2048]{1,0:T(8,128)(2,1)S(1)} %copy-done.2), kind=kOutput, calls=%fused_computation.11 | convolution fusion | flops 8633974784 | bytes 20979712 | tf_op jit(solution)/shard_map/dot_general | solution.py:48
  342.7 15.8 %fusion.13 = (bf16[1024,2048]{1,0:T(8,128)(2,1)}, bf16[1024,2048]{1,0:T(8,128)(2,1)}) fusion(f32[2048]{0:T(1024)S(1)} %convert_element_type.352, bf16[1024,2048]{1,0:T(8,128)(2,1)S(1)} %pack.26.refs_2_, bf16[2048,2048]{1,0:T(8,128)(2,1)S(1)} %copy-done.2), kind=kOutput, calls=%fused_computation.18 | convolution fusion | flops 8633974784 | bytes 20979712 | tf_op jit(solution)/shard_map/dot_general | solution.py:48
  371.7 14.4 %matmul.15.left_ref.refs_3_ = bf16[1024,2048]{1,0:T(8,128)(2,1)} custom-call(bf16[1024,2048]{1,0:T(8,128)(2,1)} %copy-done.6, bf16[2048,2048]{1,0:T(8,128)(2,1)} %copy-done, bf16[1024,2048]{1,0:T(8,128)(2,1)} %get-tuple-element.365.rest_0_), custom_call_target="tpu_custom_call" | custom-call | flops 1024 | bytes 1024 | tf_op jit(solution)/shard_map/matmul/pallas_call | solution.py:470
  386.1 13.4 %matmul.16 = (bf16[512,2048]{1,0:T(8,128)(2,1)}, bf16[512,2048]{1,0:T(8,128)(2,1)}) custom-call(bf16[1024,2048]{1,0:T(8,128)(2,1)} %matmul.15.left_ref.refs_3_, bf16[2048,2048]{1,0:T(8,128)(2,1)} %copy-done.1), custom_call_target="tpu_custom_call" | custom-call | flops 1024 | bytes 1024 | tf_op jit(solution)/shard_map/matmul/pallas_call | solution.py:470
  406.2 14.3 %matmul.17.left_ref.refs_1_ = bf16[1024,2048]{1,0:T(8,128)(2,1)} custom-call(bf16[1024,2048]{1,0:T(8,128)(2,1)} %copy-done.7, bf16[2048,2048]{1,0:T(8,128)(2,1)} %copy-done, bf16[1024,2048]{1,0:T(8,128)(2,1)} %get-tuple-element.376.rest_0_), custom_call_target="tpu_custom_call" | custom-call | flops 1024 | bytes 1024 | tf_op jit(solution)/shard_map/matmul/pallas_call | solution.py:470
  420.6 13.2 %matmul.18 = (bf16[512,2048]{1,0:T(8,128)(2,1)}, bf16[512,2048]{1,0:T(8,128)(2,1)}) custom-call(bf16[1024,2048]{1,0:T(8,128)(2,1)} %matmul.17.left_ref.refs_1_, bf16[2048,2048]{1,0:T(8,128)(2,1)} %copy-done.1), custom_call_target="tpu_custom_call" | custom-call | flops 1024 | bytes 1024 | tf_op jit(solution)/shard_map/matmul/pallas_call | solution.py:470
  436.4 24.7 %weight_grad.5 = bf16[2048,2048]{1,0:T(8,128)(2,1)} custom-call(s32[8]{0:T(128)} %iota.33.source_ref, s32[8]{0:T(128)} %stack.80.target_ref, bf16[1024,2048]{1,0:T(8,128)(2,1)} %get-tuple-element.506.refs_0_.left_ref, bf16[1024,2048]{1,0:T(8,128)(2,1)} %copy-done.7, bf16[1024,2048]{1,0:T(8,128)(2,1)} %get-tuple-element.466.refs_2_.left_ref, ...), custom_call_target="tpu_custom_call" | custom-call | flops 1024 | bytes 1024 | tf_op jit(solution)/shard_map/weight_grad/pallas_call | solution.py:328
  475.7 25.1 %weight_grad.6 = (bf16[2048,256]{1,0:T(8,128)(2,1)}, bf16[2048,256]{1,0:T(8,128)(2,1)}, bf16[2048,256]{1,0:T(8,128)(2,1)}, bf16[2048,256]{1,0:T(8,128)(2,1)}, bf...) custom-call(s32[8]{0:T(128)} %iota.34.source_ref.target_ref, ...), custom_call_target="tpu_custom_call" | custom-call | flops 1024 | bytes 1024 | tf_op jit(solution)/shard_map/weight_grad/pallas_call | solution.py:328
  512.2 25.9 %attend_back.2.rest_0_ = bf16[2560,1536]{1,0:T(8,128)(2,1)} custom-call(s32[18]{0:T(128)} %compare_select_fusion.3.info_ref, bf16[2560,1536]{1,0:T(8,128)(2,1)} %copy-done.3, bf16[1024,512]{1,0:T(8,128)(2,1)} %copy-done.39, bf16[1024,512]{1,0:T(8,128)(2,1)} %matmul.19.grad_ref, f32[4,2,2,512]{3,2,1,0:T(2,128)} %pad_maximum_fusion.7.log_ref), custom_call_target="tpu_custom_call" | custom-call | flops 1024 | bytes 1024 | tf_op jit(solution)/shard_map/attend_back/pallas_call | solution.py:258
  557.8 26.6 %attend_back.3 = (bf16[2560,1536]{1,0:T(8,128)(2,1)}, bf16[256,1024]{1,0:T(8,128)(2,1)}, bf16[256,1024]{1,0:T(8,128)(2,1)}) custom-call(s32[18]{0:T(128)} %compare_select_fusion.3.info_ref, bf16[2560,1536]{1,0:T(8,128)(2,1)} %copy-done.3, bf16[1024,512]{1,0:T(8,128)(2,1)} %copy-done.38, bf16[1024,512]{1,0:T(8,128)(2,1)} %matmul.20.grad_ref, ...), custom_call_target="tpu_custom_call" | custom-call | flops 1024 | bytes 1024 | tf_op jit(solution)/shard_map/attend_back/pallas_call | solution.py:258
  612.0 15.6 %reduce-scatter.3.cloned.1.call-done = bf16[256,2048]{1,0:T(8,128)(2,1)} async-done(((bf16[2048,2048]{1,0:T(8,128)(2,1)}), bf16[256,2048]{1,0:T(8,128)(2,1)}) %reduce-scatter.3.cloned.1.call-update) | async-done | bytes 1048592 | tf_op jit(solution)/shard_map/reduce_scatter | solution.py:593
  660.9 16.0 %weight_grad.8 = (bf16[1024,384]{1,0:T(8,128)(2,1)}, bf16[1024,384]{1,0:T(8,128)(2,1)}, bf16[1024,384]{1,0:T(8,128)(2,1)}, bf16[1024,384]{1,0:T(8,128)(2,1)}) custom-call(s32[8]{0:T(128)} %broadcast_select_fusion.source_ref, s32[8]{0:T(128)} %iota.38.target_ref, bf16[512,2048]{1,0:T(8,128)(2,1)} %copy-done.70, ...), custom_call_target="tpu_custom_call" | custom-call | flops 1024 | bytes 1024 | tf_op jit(solution)/shard_map/weight_grad/pallas_call | solution.py:328
  676.9 17.5 %collective-permute-done.56.refs_0_.refs_1_ = bf16[256,1024]{1,0:T(8,128)(2,1)S(1)} collective-permute-done((bf16[256,1024]{1,0:T(8,128)(2,1)S(1)}, bf16[256,1024]{1,0:T(8,128)(2,1)S(1)}, u32[]{:S(2)}, u32[]{:S(2)}) %collective-permute-start.56) | collective-permute-done | bytes 524320 | tf_op jit(solution)/shard_map/ppermute | solution.py:526
  699.1 13.1 %matmul.24 = (bf16[512,2048]{1,0:T(8,128)(2,1)}, bf16[512,2048]{1,0:T(8,128)(2,1)}) custom-call(bf16[1024,2048]{1,0:T(8,128)(2,1)} %get-tuple-element.466.refs_2_.left_ref, bf16[2048,2048]{1,0:T(8,128)(2,1)} %copy-done), custom_call_target="tpu_custom_call" | custom-call | flops 1024 | bytes 1024 | tf_op jit(solution)/shard_map/matmul/pallas_call | solution.py:470
  712.6 15.4 %weight_grad.9 = (bf16[1024,384]{1,0:T(8,128)(2,1)}, bf16[1024,384]{1,0:T(8,128)(2,1)}, bf16[1024,384]{1,0:T(8,128)(2,1)}, bf16[1024,384]{1,0:T(8,128)(2,1)}) custom-call(s32[8]{0:T(128)} %broadcast_select_fusion.source_ref, s32[8]{0:T(128)} %iota.39.target_ref, bf16[512,2048]{1,0:T(8,128)(2,1)} %copy-done.70, ...), custom_call_target="tpu_custom_call" | custom-call | flops 1024 | bytes 1024 | tf_op jit(solution)/shard_map/weight_grad/pallas_call | solution.py:328
  801.6 15.2 %collective-permute-done.76 = f32[26624]{0:T(1024)S(1)} collective-permute-done((f32[26624]{0:T(1024)S(1)}, f32[26624]{0:T(1024)S(1)}, u32[]{:S(2)}, u32[]{:S(2)}) %collective-permute-start.76) | collective-permute-done | bytes 106528 | tf_op jit(solution)/shard_map/ppermute | solution.py:573
  836.9 13.2 %matmul.25 = (bf16[512,2048]{1,0:T(8,128)(2,1)}, bf16[512,2048]{1,0:T(8,128)(2,1)}) custom-call(bf16[1024,2048]{1,0:T(8,128)(2,1)} %get-tuple-element.506.refs_0_.left_ref, bf16[2048,2048]{1,0:T(8,128)(2,1)} %copy-done), custom_call_target="tpu_custom_call" | custom-call | flops 1024 | bytes 1024 | tf_op jit(solution)/shard_map/matmul/pallas_call | solution.py:470
  863.0 12.3 %collective-permute-done.85 = bf16[1024,384]{1,0:T(8,128)(2,1)S(1)} collective-permute-done((bf16[1024,384]{1,0:T(8,128)(2,1)S(1)}, bf16[1024,384]{1,0:T(8,128)(2,1)S(1)}, u32[]{:S(2)}, u32[]{:S(2)}) %collective-permute-start.85) | collective-permute-done | bytes 786464 | tf_op jit(solution)/shard_map/ppermute | solution.py:529
  (591 shorter events, 452.6 us)
Async XLA Ops:
  7.2 620.3 %reduce-scatter.3.cloned.1.call-start = ((), (), s32[]{:S(2)}) async-start(), calls=%async_computation.2 | async-start | bytes 9437184 | tf_op jit(solution)/shard_map/reduce_scatter | solution.py:593
  50.7 34.2 %collective-permute-start.6 = (bf16[256,2048]{1,0:T(8,128)(2,1)S(1)}, bf16[256,2048]{1,0:T(8,128)(2,1)S(1)}, u32[]{:S(2)}, u32[]{:S(2)}) collective-permute-start(bf16[256,2048]{1,0:T(8,128)(2,1)S(1)} %get-tuple-element.278), channel_id=1, source_target_pairs={{0,2},{1,3},{2,0},{3,1},{4,6},{5,7},{6,4},{7,5},{8,10},{9,11},{10,... | collective-permute-start | bytes 3145736 | tf_op jit(solution)/shard_map/ppermute | solution.py:514
  52.3 34.3 %collective-permute-start.5 = (bf16[1040,512]{1,0:T(8,128)(2,1)S(1)}, bf16[1040,512]{1,0:T(8,128)(2,1)S(1)}, u32[]{:S(2)}, u32[]{:S(2)}) collective-permute-start(bf16[1040,512]{1,0:T(8,128)(2,1)S(1)} %collective-permute-done.refs_2_), channel_id=1, source_target_pairs={{0,16},{16,0},{1,17},{17,1},{2,18},{18,2},{3,19},{19,3},{4,20},{20... | collective-permute-start | bytes 3194888 | tf_op jit(solution)/shard_map/ppermute | solution.py:529
  150.0 54.9 %collective-permute-start.20 = (bf16[512,2048]{1,0:T(8,128)(2,1)S(1)}, bf16[512,2048]{1,0:T(8,128)(2,1)}, u32[]{:S(2)}, u32[]{:S(2)}) collective-permute-start(bf16[512,2048]{1,0:T(8,128)(2,1)S(1)} %copy-done.10), channel_id=1, source_target_pairs={{0,1},{1,0},{2,3},{3,2},{4,5},{5,4},{6,7},{7,6},{8,9},{9,8},{10,11... | collective-permute-start | bytes 6291464 | tf_op jit(solution)/shard_map/ppermute | solution.py:511
  150.0 54.8 %collective-permute-start.18 = (bf16[2064,256]{1,0:T(8,128)(2,1)}, bf16[2064,256]{1,0:T(8,128)(2,1)}, u32[]{:S(2)}, u32[]{:S(2)}) collective-permute-start(bf16[2064,256]{1,0:T(8,128)(2,1)} %collective-permute-done.16.refs_2_), channel_id=1, source_target_pairs={{0,16},{16,0},{1,17},{17,1},{2,18},{18,2},{3,19},{19,3},{4,20},{20... | collective-permute-start | bytes 3170312 | tf_op jit(solution)/shard_map/ppermute | solution.py:529
  150.5 54.3 %collective-permute-start.17 = (bf16[2064,256]{1,0:T(8,128)(2,1)}, bf16[2064,256]{1,0:T(8,128)(2,1)}, u32[]{:S(2)}, u32[]{:S(2)}) collective-permute-start(bf16[2064,256]{1,0:T(8,128)(2,1)} %collective-permute-done.16.refs_2_), channel_id=1, source_target_pairs={{0,4},{1,5},{2,6},{3,7},{4,8},{5,9},{6,10},{7,11},{8,12},{9,13},{1... | collective-permute-start | bytes 3170312 | tf_op jit(solution)/shard_map/ppermute | solution.py:517
  151.4 51.7 %collective-permute-start.19 = (bf16[256,2048]{1,0:T(8,128)(2,1)}, bf16[256,2048]{1,0:T(8,128)(2,1)}, u32[]{:S(2)}, u32[]{:S(2)}) collective-permute-start(bf16[256,2048]{1,0:T(8,128)(2,1)} %get-tuple-element.296), channel_id=1, source_target_pairs={{0,2},{1,3},{2,0},{3,1},{4,6},{5,7},{6,4},{7,5},{8,10},{9,11},{10,... | collective-permute-start | bytes 3145736 | tf_op jit(solution)/shard_map/ppermute | solution.py:514
  212.1 43.9 %collective-permute-start.28 = (bf16[512,2048]{1,0:T(8,128)(2,1)S(1)}, bf16[512,2048]{1,0:T(8,128)(2,1)}, u32[]{:S(2)}, u32[]{:S(2)}) collective-permute-start(bf16[512,2048]{1,0:T(8,128)(2,1)S(1)} %pack.18.refs_0_), channel_id=1, source_target_pairs={{0,1},{1,0},{2,3},{3,2},{4,5},{5,4},{6,7},{7,6},{8,9},{9,8},{10,11... | collective-permute-start | bytes 6291464 | tf_op jit(solution)/shard_map/ppermute | solution.py:511
  461.1 278.6 %reduce-scatter.5.cloned.1.call-start = ((), (), s32[]{:S(2)}) async-start(), calls=%async_computation.3 | async-start | bytes 2359296 | tf_op jit(solution)/shard_map/reduce_scatter | solution.py:593
  500.8 37.3 %collective-permute-start.46 = (bf16[256,2048]{1,0:T(8,128)(2,1)}, bf16[256,2048]{1,0:T(8,128)(2,1)}, u32[]{:S(2)}, u32[]{:S(2)}) collective-permute-start(bf16[256,2048]{1,0:T(8,128)(2,1)} %get-tuple-element.399), channel_id=1, source_target_pairs={{0,2},{1,3},{2,0},{3,1},{4,6},{5,7},{6,4},{7,5},{8,10},{9,11},{10,... | collective-permute-start | bytes 3145736 | tf_op jit(solution)/shard_map/ppermute | solution.py:514
  502.7 35.4 %collective-permute-start.47 = (bf16[2048,256]{1,0:T(8,128)(2,1)}, bf16[2048,256]{1,0:T(8,128)(2,1)}, u32[]{:S(2)}, u32[]{:S(2)}) collective-permute-start(bf16[2048,256]{1,0:T(8,128)(2,1)} %get-tuple-element.400), channel_id=1, source_target_pairs={{0,16},{16,0},{1,17},{17,1},{2,18},{18,2},{3,19},{19,3},{4,20},{20... | collective-permute-start | bytes 3145736 | tf_op jit(solution)/shard_map/ppermute | solution.py:529
  502.9 35.2 %collective-permute-start.48 = (bf16[256,2048]{1,0:T(8,128)(2,1)S(1)}, bf16[256,2048]{1,0:T(8,128)(2,1)}, u32[]{:S(2)}, u32[]{:S(2)}) collective-permute-start(bf16[256,2048]{1,0:T(8,128)(2,1)S(1)} %collective-permute-done.44.refs_0_), channel_id=1, source_target_pairs={{0,1},{1,0},{2,3},{3,2},{4,5},{5,4},{6,7},{7,6},{8,9},{9,8},{10,11... | collective-permute-start | bytes 3145736 | tf_op jit(solution)/shard_map/ppermute | solution.py:511
  541.1 65.0 %collective-permute-start.50 = (bf16[2048,256]{1,0:T(8,128)(2,1)}, bf16[2048,256]{1,0:T(8,128)(2,1)}, u32[]{:S(2)}, u32[]{:S(2)}) collective-permute-start(bf16[2048,256]{1,0:T(8,128)(2,1)} %get-tuple-element.418), channel_id=1, source_target_pairs={{0,16},{16,0},{1,17},{17,1},{2,18},{18,2},{3,19},{19,3},{4,20},{20... | collective-permute-start | bytes 3145736 | tf_op jit(solution)/shard_map/ppermute | solution.py:529
  542.9 69.0 %collective-permute-start.51 = (bf16[2048,256]{1,0:T(8,128)(2,1)}, bf16[2048,256]{1,0:T(8,128)(2,1)}, u32[]{:S(2)}, u32[]{:S(2)}) collective-permute-start(bf16[2048,256]{1,0:T(8,128)(2,1)} %get-tuple-element.419), channel_id=1, source_target_pairs={{0,16},{16,0},{1,17},{17,1},{2,18},{18,2},{3,19},{19,3},{4,20},{20... | collective-permute-start | bytes 3145736 | tf_op jit(solution)/shard_map/ppermute | solution.py:529
  543.1 68.9 %collective-permute-start.52 = (bf16[2048,256]{1,0:T(8,128)(2,1)}, bf16[2048,256]{1,0:T(8,128)(2,1)}, u32[]{:S(2)}, u32[]{:S(2)}) collective-permute-start(bf16[2048,256]{1,0:T(8,128)(2,1)} %add_convert_fusion.13), channel_id=1, source_target_pairs={{0,12},{1,13},{2,14},{3,15},{4,0},{5,1},{6,2},{7,3},{8,4},{9,5},{1... | collective-permute-start | bytes 3145736 | tf_op jit(solution)/shard_map/ppermute | solution.py:520
  632.1 62.4 %collective-permute-start.57 = (bf16[2048,256]{1,0:T(8,128)(2,1)}, bf16[2048,256]{1,0:T(8,128)(2,1)}, u32[]{:S(2)}, u32[]{:S(2)}) collective-permute-start(bf16[2048,256]{1,0:T(8,128)(2,1)} %get-tuple-element.444), channel_id=1, source_target_pairs={{0,16},{16,0},{1,17},{17,1},{2,18},{18,2},{3,19},{19,3},{4,20},{20... | collective-permute-start | bytes 3145736 | tf_op jit(solution)/shard_map/ppermute | solution.py:529
  632.6 61.8 %collective-permute-start.58 = (bf16[256,2048]{1,0:T(8,128)(2,1)}, bf16[256,2048]{1,0:T(8,128)(2,1)}, u32[]{:S(2)}, u32[]{:S(2)}) collective-permute-start(bf16[256,2048]{1,0:T(8,128)(2,1)} %reduce-scatter.3.cloned.1.call-done), channel_id=1, source_target_pairs={{0,16},{16,0},{1,17},{17,1},{2,18},{18,2},{3,19},{19,3},{4,20},{20... | collective-permute-start | bytes 3145736 | tf_op jit(solution)/shard_map/ppermute | solution.py:529
  638.6 55.9 %collective-permute-start.54 = (bf16[256,2048]{1,0:T(8,128)(2,1)}, bf16[256,2048]{1,0:T(8,128)(2,1)}, u32[]{:S(2)}, u32[]{:S(2)}) collective-permute-start(bf16[256,2048]{1,0:T(8,128)(2,1)} %get-tuple-element.551), channel_id=1, source_target_pairs={{0,2},{1,3},{2,0},{3,1},{4,6},{5,7},{6,4},{7,5},{8,10},{9,11},{10,... | collective-permute-start | bytes 3145736 | tf_op jit(solution)/shard_map/ppermute | solution.py:514
  645.4 49.1 %collective-permute-start.56 = (bf16[256,1024]{1,0:T(8,128)(2,1)S(1)}, bf16[256,1024]{1,0:T(8,128)(2,1)S(1)}, u32[]{:S(2)}, u32[]{:S(2)}) collective-permute-start(bf16[256,1024]{1,0:T(8,128)(2,1)S(1)} %copy-done.129), channel_id=1, source_target_pairs={{8,0},{9,1},{10,2},{11,3},{12,4},{13,5},{14,6},{15,7},{24,16},{25,... | collective-permute-start | bytes 1572872 | tf_op jit(solution)/shard_map/ppermute | solution.py:526
  694.5 45.2 %collective-permute-start.63 = (bf16[512,2048]{1,0:T(8,128)(2,1)}, bf16[512,2048]{1,0:T(8,128)(2,1)}, u32[]{:S(2)}, u32[]{:S(2)}) collective-permute-start(bf16[512,2048]{1,0:T(8,128)(2,1)} %get-tuple-element.459), channel_id=1, source_target_pairs={{0,1},{1,0},{2,3},{3,2},{4,5},{5,4},{6,7},{7,6},{8,9},{9,8},{10,11... | collective-permute-start | bytes 6291464 | tf_op jit(solution)/shard_map/ppermute | solution.py:511
  696.1 42.6 %collective-permute-start.60 = (bf16[1024,384]{1,0:T(8,128)(2,1)}, bf16[1024,384]{1,0:T(8,128)(2,1)}, u32[]{:S(2)}, u32[]{:S(2)}) collective-permute-start(bf16[1024,384]{1,0:T(8,128)(2,1)} %get-tuple-element.456), channel_id=1, source_target_pairs={{0,16},{16,0},{1,17},{17,1},{2,18},{18,2},{3,19},{19,3},{4,20},{20... | collective-permute-start | bytes 2359304 | tf_op jit(solution)/shard_map/ppermute | solution.py:529
  696.7 42.0 %collective-permute-start.61 = (bf16[1024,384]{1,0:T(8,128)(2,1)}, bf16[1024,384]{1,0:T(8,128)(2,1)}, u32[]{:S(2)}, u32[]{:S(2)}) collective-permute-start(bf16[1024,384]{1,0:T(8,128)(2,1)} %get-tuple-element.457), channel_id=1, source_target_pairs={{0,16},{16,0},{1,17},{17,1},{2,18},{18,2},{3,19},{19,3},{4,20},{20... | collective-permute-start | bytes 2359304 | tf_op jit(solution)/shard_map/ppermute | solution.py:529
  698.2 40.5 %collective-permute-start.59 = (bf16[256,2048]{1,0:T(8,128)(2,1)S(1)}, bf16[256,2048]{1,0:T(8,128)(2,1)}, u32[]{:S(2)}, u32[]{:S(2)}) collective-permute-start(bf16[256,2048]{1,0:T(8,128)(2,1)S(1)} %copy-done.92), channel_id=1, source_target_pairs={{0,2},{1,3},{2,0},{3,1},{4,6},{5,7},{6,4},{7,5},{8,10},{9,11},{10,... | collective-permute-start | bytes 3145736 | tf_op jit(solution)/shard_map/ppermute | solution.py:514
  699.1 39.6 %collective-permute-start.62 = (bf16[2048,256]{1,0:T(8,128)(2,1)S(1)}, bf16[2048,256]{1,0:T(8,128)(2,1)S(1)}, u32[]{:S(2)}, u32[]{:S(2)}) collective-permute-start(bf16[2048,256]{1,0:T(8,128)(2,1)S(1)} %copy-done.93), channel_id=1, source_target_pairs={{0,12},{1,13},{2,14},{3,15},{4,0},{5,1},{6,2},{7,3},{8,4},{9,5},{1... | collective-permute-start | bytes 3145736 | tf_op jit(solution)/shard_map/ppermute | solution.py:520
  (198 other events, 2775.1 us)
Sparse Core Ops, SparseCore 0:
  461.2 166.2 reduce-scatter.2
  632.2 82.9 reduce-scatter.4
